TPU v7x, 32 devices: a whole 2x2x4 slice. The times are simulated.
32 devices in a mesh: ctx: 8 (over z, x), head: 4 (over y, core).
Axes of the slice: x: 2, y: 2, z: 4, core: 2. Of those that a mesh axis runs over, the one named last changes fastest.
Arguments:
- queries: bfloat16 [1024, 32, 576], P('ctx', 'head'), may hold values from -62 to 62
- latents: bfloat16 [1024, 576], P('ctx'), may hold values from -8 to 8
- out_grad: bfloat16 [1024, 32, 512], P('ctx', 'head'), may hold values from -6 to 6
- outputs: bfloat16 [1024, 32, 512], P('ctx', 'head'), may hold values from -4 to 4
- span_map: int32 [16], replicated, may hold values from 0 to 15, each once
Outputs:
- query_grads: bfloat16 [1024, 32, 576], P('ctx', 'head')
- latent_grads: float32 [1024, 576], P(('ctx', 'head'))
Inputs may be any that keep to these rules, and one draw needn't show every extreme that they name: Stored span c holds the 64 tokens whose positions begin at span_map[c] * 64; every value appears once.
All inputs are finite; a program needn't handle non-finite values.
Results may differ from a plain program's by a relative error of at most 0.005.
Values may be sent and summed in bfloat16 or wider, within the bound.
No kernel may reach another device: no remote copies, remote signals or barrier semaphores. Data moves between devices by JAX's collectives and lax.ppermute only.
A program may use at most 64 MiB of HBM per device.

v0:
```python
import jax
import jax.numpy as jnp
from jax import lax
from jax.sharding import PartitionSpec as P

QK_HEAD = 192


LARGE_NEGATIVE = -1e30


def block_scores(queries, key_block, score_scale):
    return (
        jnp.einsum("ihc,jc->hij", queries, key_block, preferred_element_type=jnp.float32)
        * score_scale
    )


def stats_update(carried, queries, key_block, key_pos, query_pos, score_scale):
    running_max, running_sum = carried
    scores = block_scores(queries, key_block, score_scale)
    allowed = (key_pos[None, :] <= query_pos[:, None])[None]
    block_max = jnp.max(jnp.where(allowed, scores, LARGE_NEGATIVE), axis=2)
    new_max = jnp.maximum(running_max, block_max)
    new_mass = jnp.sum(jnp.where(allowed, jnp.exp(scores - new_max[:, :, None]), 0.0), axis=2)
    return (new_max, running_sum * jnp.exp(running_max - new_max) + new_mass)


def grads_block(
    queries, out_grad, row_dots, log_totals, key_block, key_pos, query_pos, score_scale
):
    latent_width = out_grad.shape[2]
    scores = block_scores(queries, key_block, score_scale)
    allowed = (key_pos[None, :] <= query_pos[:, None])[None]
    weights = jnp.where(allowed, jnp.exp(scores - log_totals[:, :, None]), 0.0)
    rounded = weights.astype(jnp.bfloat16)
    value_grads = jnp.einsum(
        "ihc,jc->hij", out_grad, key_block[:, :latent_width], preferred_element_type=jnp.float32
    )
    score_grads = (score_scale * weights * (value_grads - row_dots[:, :, None])).astype(
        jnp.bfloat16
    )
    query_term = jnp.einsum(
        "hij,jc->ihc", score_grads, key_block, preferred_element_type=jnp.float32
    )
    key_term = jnp.einsum("hij,ihc->jc", score_grads, queries, preferred_element_type=jnp.float32)
    value_term = jnp.einsum("hij,ihc->jc", rounded, out_grad, preferred_element_type=jnp.float32)
    latent_term = key_term + jnp.pad(value_term, ((0, 0), (0, key_block.shape[1] - latent_width)))
    return (query_term, latent_term)


def shards(queries, latents, out_grad, outputs, span_map):
    row_count = queries.shape[0]
    head_count = queries.shape[1]
    kv_width = latents.shape[1]
    score_scale = QK_HEAD ** (-0.5)
    span_rows = row_count // 2
    loop_size = lax.axis_size("ctx")
    loop_index = lax.axis_index("ctx")
    all_pos = (
        span_map[:, None] * span_rows + jnp.arange(span_rows, dtype=jnp.int32)[None, :]
    ).reshape(-1)
    query_pos = lax.dynamic_slice_in_dim(all_pos, loop_index * row_count, row_count)
    row_dots = jnp.einsum("ihc,ihc->hi", out_grad, outputs, preferred_element_type=jnp.float32)
    start_stats = (
        jnp.full((head_count, row_count), LARGE_NEGATIVE, jnp.float32),
        jnp.zeros((head_count, row_count), jnp.float32),
    )

    def positions_at(source):
        return lax.dynamic_slice_in_dim(all_pos, source * row_count, row_count)

    def stats_of(carried, key_block, key_pos):
        return stats_update(carried, queries, key_block, key_pos, query_pos, score_scale)

    def grads_of(key_block, key_pos, log_totals):
        return grads_block(
            queries, out_grad, row_dots, log_totals, key_block, key_pos, query_pos, score_scale
        )

    every_row = lax.all_gather(latents, "ctx", axis=0, tiled=True)

    def stats_turn(source, carried):
        key_block = lax.dynamic_slice_in_dim(every_row, source * row_count, row_count)
        return stats_of(carried, key_block, positions_at(source))

    running_max, running_sum = lax.fori_loop(0, loop_size, stats_turn, start_stats)
    log_totals = running_max + jnp.log(running_sum)

    def grads_turn(source, carried):
        query_sum, latent_terms = carried
        key_block = lax.dynamic_slice_in_dim(every_row, source * row_count, row_count)
        query_term, latent_term = grads_of(key_block, positions_at(source), log_totals)
        latent_terms = lax.dynamic_update_slice_in_dim(
            latent_terms, latent_term, source * row_count, 0
        )
        return (query_sum + query_term, latent_terms)

    start_grads = (
        jnp.zeros((row_count, head_count, kv_width), jnp.float32),
        jnp.zeros((loop_size * row_count, kv_width), jnp.float32),
    )
    query_sum, latent_terms = lax.fori_loop(0, loop_size, grads_turn, start_grads)
    latent_grads = lax.psum_scatter(latent_terms, ("ctx", "head"), scatter_dimension=0, tiled=True)
    return (query_sum.astype(jnp.bfloat16), latent_grads)


def solution(mesh):
    placed = (
        P("ctx", "head", None),
        P("ctx", None),
        P("ctx", "head", None),
        P("ctx", "head", None),
        P(),
    )
    return jax.shard_map(
        shards,
        mesh=mesh,
        in_specs=placed,
        out_specs=(P("ctx", "head", None), P(("ctx", "head"), None)),
        check_vma=False,
    )
```

profile of v0, /device:TPU:0, one launch (start us, length us, event | category | flops | bytes accessed | tf_op | source)
XLA Modules:
  0.0 278.7 jit_solution(8024868281130331200)
XLA Ops:
  8.8 1.6 copy.11
  10.4 1.6 fusion.22
  12.2 41.6 %all-gather.2.cloned.1.call-done = bf16[1024,576]{0,1:T(8,128)(2,1)} async-done(((bf16[128,576]{0,1:T(8,128)(2,1)}), bf16[1024,576]{0,1:T(8,128)(2,1)}) %all-gather.2.cloned.1.call-update) | async-done | bytes 1179664 | tf_op jit(solution)/shard_map/all_gather | solution.py:81
  53.7 13.4 %while.34 = (s32[]{:T(128)}, f32[8,128]{1,0:T(8,128)S(1)}, f32[8,128]{1,0:T(8,128)S(1)}, s32[1024]{0:T(1024)S(1)}, s32[128]{0:T(128)S(1)}, /*index=5*/bf16[1024,...) while((s32[]{:T(128)}, f32[8,128]{1,0:T(8,128)S(1)}, ...), condition=%wide.region_3.4_spmd.clone, body=%wide.region_0.3_spmd.clone.sunk | while | flops 151802880 | bytes 2480310 | solution.py:87
  67.2 1.7 broadcast_in_dim.107
  68.9 62.8 %while.35 = (s32[]{:T(128)}, f32[128,8,576]{0,2,1:T(8,128)}, f32[1024,576]{0,1:T(8,128)}, bf16[1024,576]{0,1:T(8,128)(2,1)}, s32[1024]{0:T(1024)S(1)}, /*index=5...) while((s32[]{:T(128)}, f32[128,8,576]{0,2,1:T(8,128)}, ...), condition=%wide.region_5.6_spmd.clone, body=%wide.region_4.5_spmd.clone.sunk | while | flops 723738624 | bytes 31697168 | solution.py:103
  73.6 1.7 bitcast_add_fusion.2
  75.4 1.4 copy-done.2
  81.5 1.7 bitcast_add_fusion.2
  83.2 1.4 copy-done.2
  86.1 1.4 fusion.56
  89.3 1.7 bitcast_add_fusion.2
  91.1 1.4 copy-done.2
  97.2 1.7 bitcast_add_fusion.2
  105.0 1.7 bitcast_add_fusion.2
  106.8 1.4 copy-done.2
  109.7 1.4 fusion.56
  112.9 1.7 bitcast_add_fusion.2
  114.6 1.4 copy-done.2
  120.7 1.7 bitcast_add_fusion.2
  128.5 1.7 bitcast_add_fusion.2
  131.7 3.2 %copy.12 = f32[1024,576]{1,0:T(8,128)} copy(f32[1024,576]{0,1:T(8,128)} %get-tuple-element.373) | data formatting | bytes 4718592 | tf_op jit(solution)/shard_map/while | solution.py:103
  134.9 1.6 copy-done.3
  137.7 134.1 %reduce-scatter.2.cloned.1.call-done = f32[32,576]{1,0:T(8,128)} async-done(((f32[1024,576]{1,0:T(8,128)}), f32[32,576]{1,0:T(8,128)}) %reduce-scatter.2.cloned.1.call-update) | async-done | bytes 73744 | tf_op jit(solution)/shard_map/reduce_scatter | solution.py:104
  (148 shorter events, 54.5 us)
Async XLA Ops:
  7.2 3.3 %copy-start.4 = (bf16[128,8,512]{2,1,0:T(8,128)(2,1)S(1)}, bf16[128,8,512]{2,1,0:T(8,128)(2,1)}, u32[]{:S(2)}) copy-start(bf16[128,8,512]{2,1,0:T(8,128)(2,1)} %param.11) | copy-start | bytes 3145732
  7.2 46.6 %all-gather.2.cloned.1.call-start = ((), (), s32[]{:S(2)}) async-start(), calls=%async_computation.1 | async-start | bytes 1327104 | tf_op jit(solution)/shard_map/all_gather | solution.py:81
  7.9 263.9 %reduce-scatter.2.cloned.1.call-start = ((), (), s32[]{:S(2)}) async-start(), calls=%async_computation.2 | async-start | bytes 2703360 | tf_op jit(solution)/shard_map/reduce_scatter | solution.py:104
  8.8 44.9 %copy-start = (bf16[128,8,576]{0,2,1:T(8,128)(2,1)S(1)}, bf16[128,8,576]{0,2,1:T(8,128)(2,1)}, u32[]{:S(2)}) copy-start(bf16[128,8,576]{0,2,1:T(8,128)(2,1)} %param.9) | copy-start | bytes 3538948
  71.9 1.8 copy-start.1
  75.4 1.4 copy-start.2
  79.7 1.8 copy-start.1
  83.2 1.4 copy-start.2
  87.5 1.8 copy-start.1
  91.1 1.4 copy-start.2
  95.4 1.8 copy-start.1
  98.9 1.4 copy-start.2
  103.2 1.8 copy-start.1
  106.7 1.4 copy-start.2
  111.1 1.8 copy-start.1
  114.6 1.4 copy-start.2
  118.9 1.8 copy-start.1
  122.4 1.4 copy-start.2
  126.8 1.8 copy-start.1
  130.3 1.4 copy-start.2
  134.9 1.7 copy-start.3
Sparse Core Ops, SparseCore 0:
  10.1 43.6 all-gather.1
  135.0 136.7 reduce-scatter.1
where the time goes:
time: 280 us; the launch traced here: 279 us
  waiting for transfers between devices  176 us (63%)
  matrix products  60.5 us (22%)
  local copies, waits for them, and re-layouts  20.9 us (7%)
  between operations  14.1 us (5%)
  other arithmetic  5.88 us (2%)
    reduce_scatter x1, waiting for transfers between devices, shards(): lax.psum_scatter(latent_terms, ('ctx', 'head'), scatter_dimension=0, tile...  134 us
    all_gather x1, waiting for transfers between devices, shards(): every_row = lax.all_gather(latents, 'ctx', axis=0, tiled=True)  41.6 us
    dot_general x16, matrix products, block_scores(): jnp.einsum('ihc,jc->hij', queries, key_block, preferred_element_type=jnp....  21.4 us
    dot_general x8, matrix products, grads_block(): jnp.einsum('hij,jc->ihc', score_grads, key_block, preferred_element_type=...  13.9 us
    while x40, local copies, waits for them, and re-layouts  11.2 us
    dot_general x8, matrix products, grads_block(): jnp.einsum('ihc,jc->hij', out_grad, key_block[:, :latent_width], preferre...  11.2 us
    dot_general x8, matrix products, grads_block(): jnp.einsum('hij,ihc->jc', score_grads, queries, preferred_element_type=jn...  9.79 us
  transfers between devices with their start and end apart: 2, of which 2 were waited for; matrix products, arithmetic and copies ran while one was open for 2% of the time, Pallas kernels for 0%

commit v1 on v0

v1 whole, which is shorter than its diff:
```python
import jax
import jax.numpy as jnp
from jax import lax
from jax.experimental import pallas as pl
from jax.experimental.pallas import tpu as pltpu
from jax.sharding import PartitionSpec as P

QK_HEAD = 192
LARGE_NEGATIVE = -1e30
LOG2_E = 1.4426950408889634
LANES = 128
VMEM_LIMIT = 40 * 1024 * 1024

f32 = jnp.float32
bf16 = jnp.bfloat16
VMEM = pl.BlockSpec(memory_space=pltpu.VMEM)


def dot(a, b, a_dim, b_dim):
    return lax.dot_general(a, b, (((a_dim,), (b_dim,)), ((), ())), preferred_element_type=f32)


def side_by_side(blocks):
    return jnp.concatenate(blocks, axis=1)


def latent_rows(ds_ref, p_ref, qt, out_grad, rows):
    key_term = dot(ds_ref[rows, :], qt, 1, 1)
    value_term = dot(p_ref[rows, :], out_grad, 1, 0)
    width = value_term.shape[1]
    return key_term[:, :width] + value_term, key_term[:, width:]


def probs_kernel(qt_ref, og_ref, rd_ref, k_ref, kpos_ref, qpos_ref, p_ref, ds_ref, far_ref):
    heads, _, tokens = qt_ref.shape
    width = og_ref.shape[2]
    keys = k_ref.shape[0]
    scale = QK_HEAD**-0.5
    group = 2
    for g in range(0, heads, group):
        some = range(g, g + group)
        cols = slice(g * tokens, (g + group) * tokens)
        qt = side_by_side([qt_ref[h] for h in some])
        scores = dot(k_ref[...], qt, 1, 0)
        allowed = side_by_side([kpos_ref[...]] * group) <= side_by_side([qpos_ref[...]] * group)
        scores = jnp.where(allowed, scores * (scale * LOG2_E), LARGE_NEGATIVE)
        mass = jnp.exp2(scores - jnp.max(scores, axis=0, keepdims=True))
        weights = mass * (1.0 / jnp.sum(mass, axis=0, keepdims=True))
        out_grad = og_ref[g : g + group].reshape(group * tokens, width)
        value_grads = dot(k_ref[:, :width], out_grad, 1, 1)
        row_dots = side_by_side([rd_ref[h] for h in some])
        p_ref[:, cols] = weights.astype(bf16)
        ds_ref[:, cols] = (weights * ((value_grads - row_dots) * scale)).astype(bf16)
    qt = side_by_side([qt_ref[h] for h in range(heads)])
    out_grad = og_ref[...].reshape(heads * tokens, width)
    half = keys // 2
    for r in range(0, half, 256):
        left, right = latent_rows(ds_ref, p_ref, qt, out_grad, slice(half + r, half + r + 256))
        far_ref[r : r + 256, :width] = left.astype(bf16)
        far_ref[r : r + 256, width:] = right.astype(bf16)


def near_kernel(qt_ref, og_ref, p_ref, ds_ref, near_ref):
    heads, _, tokens = qt_ref.shape
    width = og_ref.shape[2]
    qt = side_by_side([qt_ref[h] for h in range(heads)])
    out_grad = og_ref[...].reshape(heads * tokens, width)
    for r in range(0, near_ref.shape[0], 256):
        left, right = latent_rows(ds_ref, p_ref, qt, out_grad, slice(r, r + 256))
        near_ref[r : r + 256, :width] = left
        near_ref[r : r + 256, width:] = right


def query_kernel(k_ref, ds_ref, dq_ref):
    heads, _, tokens = dq_ref.shape
    for g in range(0, heads, 2):
        grads = dot(k_ref[...], ds_ref[:, g * tokens : (g + 2) * tokens], 0, 0).astype(bf16)
        dq_ref[g] = grads[:, :tokens]
        dq_ref[g + 1] = grads[:, tokens:]


def call(kernel, outs, flops, operands):
    return pl.pallas_call(
        kernel,
        in_specs=[VMEM] * len(operands),
        out_specs=[VMEM] * len(outs),
        out_shape=outs,
        compiler_params=pltpu.CompilerParams(vmem_limit_bytes=VMEM_LIMIT),
        cost_estimate=pl.CostEstimate(flops=flops, bytes_accessed=4 << 20, transcendentals=0),
    )(*operands)


def phases_of(device_count):
    bits = device_count.bit_length() - 1
    phases, bit = [[1]], 1
    while bit < bits:
        pair = [1 << bit] if bit + 1 == bits else [1 << bit, 2 << bit, 3 << bit]
        phases.append(pair)
        bit += len(pair).bit_length()
    return phases


def shards(queries, latents, out_grad, outputs, span_map):
    tokens, heads, kv_width = queries.shape
    width = out_grad.shape[2]
    head_size = lax.axis_size("head")
    devices = lax.axis_size("ctx") * head_size
    keys = lax.axis_size("ctx") * tokens
    span_rows = keys // span_map.shape[0]
    ctx, head = lax.axis_index("ctx"), lax.axis_index("head")
    me = ctx * head_size + head
    piece = tokens // head_size
    phases = phases_of(devices)

    def exchange(value, mask):
        return lax.ppermute(
            value, ("ctx", "head"), [(i, i ^ mask) for i in range(devices)]
        )

    def positions(rows):
        spans = rows // span_rows
        mine = spans[:, None] == jnp.arange(span_map.shape[0], dtype=jnp.int32)[None, :]
        return jnp.sum(jnp.where(mine, span_map[None, :], 0), axis=1) * span_rows + rows % span_rows

    order = [0]
    for masks in reversed(phases):
        order = order + [m ^ o for m in masks for o in order]
    starts = (me ^ jnp.array(order, dtype=jnp.int32)) * piece
    key_rows = (starts[:, None] + jnp.arange(piece, dtype=jnp.int32)[None, :]).reshape(-1)
    key_pos = jnp.broadcast_to(positions(key_rows)[:, None], (keys, LANES))
    query_pos = positions(ctx * tokens + jnp.arange(tokens, dtype=jnp.int32))[None, :]

    gathered = lax.dynamic_slice_in_dim(latents, head * piece, piece)
    for masks in reversed(phases):
        gathered = jnp.concatenate([gathered] + [exchange(gathered, m) for m in masks])

    qt = queries.transpose(1, 2, 0)
    og = out_grad.transpose(1, 0, 2)
    row_dots = jnp.einsum("ihc,ihc->hi", out_grad, outputs, preferred_element_type=f32)
    row_dots = row_dots.reshape(heads, 1, tokens)
    rows = heads * tokens
    half = keys // 2

    weights, score_grads, far = call(
        probs_kernel,
        [
            pltpu.VMEM((keys, rows), bf16),
            pltpu.VMEM((keys, rows), bf16),
            jax.ShapeDtypeStruct((half, kv_width), bf16),
        ],
        2 * keys * rows * (kv_width + width) * 2,
        [qt, og, row_dots, gathered, key_pos, query_pos],
    )
    arrived = exchange(far, 1)
    (near,) = call(
        near_kernel,
        [jax.ShapeDtypeStruct((half, kv_width), f32)],
        2 * half * rows * (kv_width + width),
        [qt, og, weights, score_grads],
    )
    (query_grads,) = call(
        query_kernel,
        [jax.ShapeDtypeStruct((heads, kv_width, tokens), bf16)],
        2 * keys * rows * kv_width,
        [gathered, score_grads],
    )
    total = near + arrived.astype(f32)
    for masks in phases[1:]:
        size = total.shape[0] // (len(masks) + 1)
        sent = total.astype(bf16)
        parts = [exchange(sent[(j + 1) * size : (j + 2) * size], m) for j, m in enumerate(masks)]
        total = total[:size] + sum(part.astype(f32) for part in parts)
    return query_grads.transpose(2, 0, 1), total


def solution(mesh):
    placed = (
        P("ctx", "head", None),
        P("ctx", None),
        P("ctx", "head", None),
        P("ctx", "head", None),
        P(),
    )
    return jax.shard_map(
        shards,
        mesh=mesh,
        in_specs=placed,
        out_specs=(P("ctx", "head", None), P(("ctx", "head"), None)),
        check_vma=False,
    )
```

time: 280 us -> 69.6 us (0.25)
  waiting for transfers between devices: 176 us -> 17.6 us
  matrix products: 60.5 us -> 0 us
  starting transfers between devices: 0.08 us -> 16.6 us
  between operations: 14.1 us -> 0.86 us
  Pallas kernels: 0 us -> 10.1 us
    reduce_scatter x1 -> x0, waiting for transfers between devices: 134 us -> none  [shards(): lax.psum_scatter(latent_terms, ('ctx', 'head'), scatter_dimension=0, tile...]
    dot_general x48 -> x0, matrix products: 60.5 us -> none  [the longest x16 21.4 us: block_scores(): jnp.einsum('ihc,jc->hij', queries, key_block, preferred_element_type=jnp....]
    all_gather x1 -> x0, waiting for transfers between devices: 41.6 us -> none  [shards(): every_row = lax.all_gather(latents, 'ctx', axis=0, tiled=True)]
    ppermute x0 -> x14, waiting for transfers between devices: none -> 17.6 us  [exchange(): lax.ppermute(value, ('ctx', 'head'), [(i, i ^ mask) for i in range(device...]
    ppermute x0 -> x14, starting transfers between devices: none -> 16.6 us  [exchange(): lax.ppermute(value, ('ctx', 'head'), [(i, i ^ mask) for i in range(device...]
    while x41 -> x0, local copies, waits for them, and re-layouts: 14.4 us -> none
    pallas_call x0 -> x3, Pallas kernels: none -> 10.1 us  [call(): pl.pallas_call(kernel, in_specs=[VMEM] * len(operands), out_specs=[VMEM]...]
    unnamed x7 -> x32, local copies, waits for them, and re-layouts: 3.28 us -> 11.7 us
  transfers between devices with their start and end apart: 2 -> 14, of which waited for: 2 -> 7; matrix products, arithmetic and copies ran while one was open for 2% -> 7% of each run, Pallas kernels for 0% -> 6%
where the time goes in v1:
time: 69.6 us; the launch traced here: 69.1 us
  local copies, waits for them, and re-layouts  19 us (27%)
  waiting for transfers between devices  17.6 us (25%)
  starting transfers between devices  16.6 us (24%)
  Pallas kernels  10.1 us (15%)
  other arithmetic  4.84 us (7%)
  between operations  0.86 us (1%)
    ppermute x14, waiting for transfers between devices, exchange(): lax.ppermute(value, ('ctx', 'head'), [(i, i ^ mask) for i in range(device...  17.6 us
    ppermute x14, starting transfers between devices, exchange(): lax.ppermute(value, ('ctx', 'head'), [(i, i ^ mask) for i in range(device...  16.6 us
    unnamed x32, local copies, waits for them, and re-layouts  11.7 us
    pallas_call x3, Pallas kernels, call(): pl.pallas_call(kernel, in_specs=[VMEM] * len(operands), out_specs=[VMEM]...  10.1 us
    ppermute x2, local copies, waits for them, and re-layouts, exchange(): lax.ppermute(value, ('ctx', 'head'), [(i, i ^ mask) for i in range(device...  3.5 us
    pallas_call x1, local copies, waits for them, and re-layouts, call(): pl.pallas_call(kernel, in_specs=[VMEM] * len(operands), out_specs=[VMEM]...  2.13 us
    unnamed x1, other arithmetic  1.89 us
  transfers between devices with their start and end apart: 14, of which 7 were waited for; matrix products, arithmetic and copies ran while one was open for 7% of the time, Pallas kernels for 6%

profile of v1, /device:TPU:0, one launch (start us, length us, event | category | flops | bytes accessed | tf_op | source)
XLA Modules:
  0.0 69.1 jit_solution(12111247203459093496)
XLA Ops:
  1.8 5.1 %collective-permute-start.2 = (bf16[32,576]{1,0:T(8,128)(2,1)S(1)}, bf16[32,576]{1,0:T(8,128)(2,1)S(1)}, u32[]{:S(2)}, u32[]{:S(2)}) collective-permute-start(bf16[32,576]{1,0:T(8,128)(2,1)S(1)} %copy.30), channel_id=1, source_target_pairs={{0,24},{1,25},{2,26},{3,27},{4,28},{5,29},{6,30},{7,31},{8,16},{9,... | collective-permute-start | bytes 110600 | tf_op jit(solution)/shard_map/ppermute | solution.py:116
  8.4 1.9 %fusion = f32[8,128]{0,1:T(8,128)S(1)} fusion(bf16[128,8,512]{2,1,0:T(8,128)(2,1)} %param.9, bf16[128,8,512]{2,1,0:T(8,128)(2,1)} %param.8), kind=kLoop, calls=%fused_computation.1 | loop fusion | flops 2096128 | bytes 2101248
  10.3 1.5 %collective-permute-done.1 = bf16[32,576]{1,0:T(8,128)(2,1)S(1)} collective-permute-done((bf16[32,576]{1,0:T(8,128)(2,1)S(1)}, bf16[32,576]{1,0:T(8,128)(2,1)S(1)}, u32[]{:S(2)}, u32[]{:S(2)}) %collective-permute-start.1) | collective-permute-done | bytes 36896 | tf_op jit(solution)/shard_map/ppermute | solution.py:116
  11.8 2.5 %collective-permute-start.5 = (bf16[128,576]{1,0:T(8,128)(2,1)S(1)}, bf16[128,576]{1,0:T(8,128)(2,1)S(1)}, u32[]{:S(2)}, u32[]{:S(2)}) collective-permute-start(bf16[128,576]{1,0:T(8,128)(2,1)S(1)} %pad_maximum_fusion), channel_id=1, source_target_pairs={{0,6},{1,7},{2,4},{3,5},{4,2},{5,3},{6,0},{7,1},{8,14},{9,15},{10,... | collective-permute-start | bytes 442376 | tf_op jit(solution)/shard_map/ppermute | solution.py:116
  15.4 5.4 %collective-permute-done.3 = bf16[128,576]{1,0:T(8,128)(2,1)S(1)} collective-permute-done((bf16[128,576]{1,0:T(8,128)(2,1)S(1)}, bf16[128,576]{1,0:T(8,128)(2,1)S(1)}, u32[]{:S(2)}, u32[]{:S(2)}) %collective-permute-start.3) | collective-permute-done | bytes 147488 | tf_op jit(solution)/shard_map/ppermute | solution.py:116
  22.1 1.5 %copy.32 = bf16[128,8,512]{2,0,1:T(8,128)(2,1)S(1)} copy(bf16[128,8,512]{2,1,0:T(8,128)(2,1)} %param.8) | data formatting | bytes 2097152 | tf_op args[2]
  24.4 1.4 %copy.18 = bf16[512,576]{1,0:T(8,128)(2,1)S(1)} copy(bf16[512,576]{0,1:T(8,128)(2,1)} %collective-permute-done.6) | data formatting | bytes 1179648 | tf_op jit(solution)/shard_map/ppermute | solution.py:116
  27.5 1.3 %copy-done.6 = bf16[1024,576]{1,0:T(8,128)(2,1)S(1)} copy-done((bf16[1024,576]{1,0:T(8,128)(2,1)S(1)}, bf16[1024,576]{1,0:T(8,128)(2,1)}, u32[]{:S(2)}) %copy-start.6) | copy-done | bytes 1179672
  28.8 5.9 %shard_map.77 = (bf16[1024,1024]{1,0:T(8,128)(2,1)S(1)}, bf16[1024,1024]{1,0:T(8,128)(2,1)S(1)}, bf16[512,576]{1,0:T(8,128)(2,1)S(1)}) custom-call(bf16[8,576,128]{2,1,0:T(8,128)(2,1)S(1)} %bitcast.14, bf16[8,128,512]{2,1,0:T(8,128)(2,1)S(1)} %bitcast.12, f32[8,1,128]{2,1,0:T(1,128)S(1)} %bitcast.16, bf16[1024,576]{1,0:T(8,128)(2,1)S(1)} %copy-done.6, ...), custom_call_target="tpu_custom_call" | custom-call | flops 4563402752 | bytes 4194304 | tf_op jit(solution)/shard_map/pallas_call | solution.py:83
  34.7 1.3 %copy-done.3 = bf16[1024,1024]{1,0:T(8,128)(2,1)} copy-done((bf16[1024,1024]{1,0:T(8,128)(2,1)}, bf16[1024,1024]{1,0:T(8,128)(2,1)S(1)}, u32[]{:S(2)}) %copy-start.3) | copy-done | bytes 2097176
  36.9 2.1 %copy.20 = bf16[512,576]{0,1:T(8,128)(2,1)} copy(bf16[512,576]{1,0:T(8,128)(2,1)} %copy-done.10) | data formatting | bytes 1179648 | tf_op jit(solution)/shard_map/pallas_call | solution.py:83
  39.2 1.2 %copy-done.2 = bf16[128,8,512]{2,0,1:T(8,128)(2,1)S(1)} copy-done((bf16[128,8,512]{2,0,1:T(8,128)(2,1)S(1)}, bf16[128,8,512]{2,0,1:T(8,128)(2,1)}, u32[]{:S(2)}) %copy-start.2) | copy-done | bytes 1048600
  40.4 1.6 %copy-done.4 = bf16[1024,1024]{1,0:T(8,128)(2,1)S(1)} copy-done((bf16[1024,1024]{1,0:T(8,128)(2,1)S(1)}, bf16[1024,1024]{1,0:T(8,128)(2,1)}, u32[]{:S(2)}) %copy-start.4) | copy-done | bytes 2097176
  42.0 1.3 %copy-done.9 = bf16[128,8,576]{0,2,1:T(8,128)(2,1)S(1)} copy-done((bf16[128,8,576]{0,2,1:T(8,128)(2,1)S(1)}, bf16[128,8,576]{0,2,1:T(8,128)(2,1)}, u32[]{:S(2)}) %copy-start.9) | copy-done | bytes 1179672
  43.3 1.5 %shard_map.79 = f32[512,576]{1,0:T(8,128)S(1)} custom-call(bf16[8,576,128]{2,1,0:T(8,128)(2,1)S(1)} %bitcast.15, bf16[8,128,512]{2,1,0:T(8,128)(2,1)S(1)} %bitcast.13, bf16[1024,1024]{1,0:T(8,128)(2,1)S(1)} %copy-done.4, bf16[1024,1024]{1,0:T(8,128)(2,1)S(1)} %get-tuple-element.5.ds_ref), custom_call_target="tpu_custom_call" | custom-call | flops 1140850688 | bytes 4194304 | tf_op jit(solution)/shard_map/pallas_call | solution.py:83
  44.8 2.1 %copy.21 = bf16[512,576]{1,0:T(8,128)(2,1)} copy(bf16[512,576]{0,1:T(8,128)(2,1)} %collective-permute-done.7) | data formatting | bytes 1179648 | tf_op jit(solution)/shard_map/ppermute | solution.py:116
  47.0 1.2 %fusion.7 = (bf16[512,576]{1,0:T(8,128)(2,1)S(1)}, f32[512,576]{1,0:T(8,128)S(1)}) fusion(f32[512,576]{1,0:T(8,128)S(1)} %shard_map.79, bf16[512,576]{1,0:T(8,128)(2,1)} %copy.21), kind=kLoop, calls=%fused_computation.48 | loop fusion | flops 884736 | bytes 3538944 | tf_op jit(solution)/shard_map/convert_element_type | solution.py:170
  48.3 1.6 %collective-permute-start.8 = (bf16[128,576]{1,0:T(8,128)(2,1)S(1)}, bf16[128,576]{1,0:T(8,128)(2,1)S(1)}, u32[]{:S(2)}, u32[]{:S(2)}) collective-permute-start(bf16[128,576]{1,0:T(8,128)(2,1)S(1)} %get-tuple-element.12), channel_id=1, source_target_pairs={{0,2},{1,3},{2,0},{3,1},{4,6},{5,7},{6,4},{7,5},{8,10},{9,11},{10,... | collective-permute-start | bytes 442376 | tf_op jit(solution)/shard_map/ppermute | solution.py:116
  49.9 1.4 %collective-permute-start.10 = (bf16[128,576]{1,0:T(8,128)(2,1)S(1)}, bf16[128,576]{1,0:T(8,128)(2,1)S(1)}, u32[]{:S(2)}, u32[]{:S(2)}) collective-permute-start(bf16[128,576]{1,0:T(8,128)(2,1)S(1)} %get-tuple-element.13), channel_id=1, source_target_pairs={{0,6},{1,7},{2,4},{3,5},{4,2},{5,3},{6,0},{7,1},{8,14},{9,15},{10,... | collective-permute-start | bytes 442376 | tf_op jit(solution)/shard_map/ppermute | solution.py:116
  51.8 6.5 %collective-permute-done.8 = bf16[128,576]{1,0:T(8,128)(2,1)S(1)} collective-permute-done((bf16[128,576]{1,0:T(8,128)(2,1)S(1)}, bf16[128,576]{1,0:T(8,128)(2,1)S(1)}, u32[]{:S(2)}, u32[]{:S(2)}) %collective-permute-start.8) | collective-permute-done | bytes 147488 | tf_op jit(solution)/shard_map/ppermute | solution.py:116
  58.3 1.2 %collective-permute-done.9 = bf16[128,576]{1,0:T(8,128)(2,1)S(1)} collective-permute-done((bf16[128,576]{1,0:T(8,128)(2,1)S(1)}, bf16[128,576]{1,0:T(8,128)(2,1)S(1)}, u32[]{:S(2)}, u32[]{:S(2)}) %collective-permute-start.9) | collective-permute-done | bytes 147488 | tf_op jit(solution)/shard_map/ppermute | solution.py:116
  60.4 2.7 %collective-permute-start.13 = (bf16[32,576]{1,0:T(8,128)(2,1)S(1)}, bf16[32,576]{1,0:T(8,128)(2,1)S(1)}, u32[]{:S(2)}, u32[]{:S(2)}) collective-permute-start(bf16[32,576]{1,0:T(8,128)(2,1)S(1)} %get-tuple-element.16), channel_id=1, source_target_pairs={{0,24},{1,25},{2,26},{3,27},{4,28},{5,29},{6,30},{7,31},{8,16},{9,... | collective-permute-start | bytes 110600 | tf_op jit(solution)/shard_map/ppermute | solution.py:116
  63.2 2.7 %shard_map.78 = bf16[8,576,128]{2,1,0:T(8,128)(2,1)} custom-call(bf16[1024,576]{1,0:T(8,128)(2,1)S(1)} %copy-done.7, bf16[1024,1024]{1,0:T(8,128)(2,1)S(1)} %get-tuple-element.5.ds_ref), custom_call_target="tpu_custom_call" | custom-call | flops 1207959552 | bytes 4194304 | tf_op jit(solution)/shard_map/pallas_call | solution.py:83
  66.2 2.2 %collective-permute-done.12 = bf16[32,576]{1,0:T(8,128)(2,1)S(1)} collective-permute-done((bf16[32,576]{1,0:T(8,128)(2,1)S(1)}, bf16[32,576]{1,0:T(8,128)(2,1)S(1)}, u32[]{:S(2)}, u32[]{:S(2)}) %collective-permute-start.12) | collective-permute-done | bytes 36896 | tf_op jit(solution)/shard_map/ppermute | solution.py:116
  (64 shorter events, 10.9 us)
Async XLA Ops:
  1.8 8.5 %collective-permute-start.2 = (bf16[32,576]{1,0:T(8,128)(2,1)S(1)}, bf16[32,576]{1,0:T(8,128)(2,1)S(1)}, u32[]{:S(2)}, u32[]{:S(2)}) collective-permute-start(bf16[32,576]{1,0:T(8,128)(2,1)S(1)} %copy.30), channel_id=1, source_target_pairs={{0,24},{1,25},{2,26},{3,27},{4,28},{5,29},{6,30},{7,31},{8,16},{9,... | collective-permute-start | bytes 110600 | tf_op jit(solution)/shard_map/ppermute | solution.py:116
  6.9 4.9 %collective-permute-start.1 = (bf16[32,576]{1,0:T(8,128)(2,1)S(1)}, bf16[32,576]{1,0:T(8,128)(2,1)S(1)}, u32[]{:S(2)}, u32[]{:S(2)}) collective-permute-start(bf16[32,576]{1,0:T(8,128)(2,1)S(1)} %copy.30), channel_id=1, source_target_pairs={{0,16},{1,17},{2,18},{3,19},{4,20},{5,21},{6,22},{7,23},{8,24},{9,... | collective-permute-start | bytes 110600 | tf_op jit(solution)/shard_map/ppermute | solution.py:116
  6.9 4.9 %collective-permute-start = (bf16[32,576]{1,0:T(8,128)(2,1)S(1)}, bf16[32,576]{1,0:T(8,128)(2,1)S(1)}, u32[]{:S(2)}, u32[]{:S(2)}) collective-permute-start(bf16[32,576]{1,0:T(8,128)(2,1)S(1)} %copy.30), channel_id=1, source_target_pairs={{0,8},{1,9},{2,10},{3,11},{4,12},{5,13},{6,14},{7,15},{8,0},{9,1},... | collective-permute-start | bytes 110600 | tf_op jit(solution)/shard_map/ppermute | solution.py:116
  11.8 9.1 %collective-permute-start.5 = (bf16[128,576]{1,0:T(8,128)(2,1)S(1)}, bf16[128,576]{1,0:T(8,128)(2,1)S(1)}, u32[]{:S(2)}, u32[]{:S(2)}) collective-permute-start(bf16[128,576]{1,0:T(8,128)(2,1)S(1)} %pad_maximum_fusion), channel_id=1, source_target_pairs={{0,6},{1,7},{2,4},{3,5},{4,2},{5,3},{6,0},{7,1},{8,14},{9,15},{10,... | collective-permute-start | bytes 442376 | tf_op jit(solution)/shard_map/ppermute | solution.py:116
  14.3 6.5 %collective-permute-start.4 = (bf16[128,576]{1,0:T(8,128)(2,1)S(1)}, bf16[128,576]{1,0:T(8,128)(2,1)S(1)}, u32[]{:S(2)}, u32[]{:S(2)}) collective-permute-start(bf16[128,576]{1,0:T(8,128)(2,1)S(1)} %pad_maximum_fusion), channel_id=1, source_target_pairs={{0,4},{1,5},{2,6},{3,7},{4,0},{5,1},{6,2},{7,3},{8,12},{9,13},{10,... | collective-permute-start | bytes 442376 | tf_op jit(solution)/shard_map/ppermute | solution.py:116
  14.9 5.9 %collective-permute-start.3 = (bf16[128,576]{1,0:T(8,128)(2,1)S(1)}, bf16[128,576]{1,0:T(8,128)(2,1)S(1)}, u32[]{:S(2)}, u32[]{:S(2)}) collective-permute-start(bf16[128,576]{1,0:T(8,128)(2,1)S(1)} %pad_maximum_fusion), channel_id=1, source_target_pairs={{0,2},{1,3},{2,0},{3,1},{4,6},{5,7},{6,4},{7,5},{8,10},{9,11},{10,... | collective-permute-start | bytes 442376 | tf_op jit(solution)/shard_map/ppermute | solution.py:116
  20.8 1.2 %copy-start.11 = (s32[16]{0:T(128)S(1)}, s32[16]{0:T(128)}, u32[]{:S(2)}) copy-start(s32[16]{0:T(128)} %param.10) | copy-start | bytes 196
  22.1 2.3 %collective-permute-start.6 = (bf16[512,576]{0,1:T(8,128)(2,1)}, bf16[512,576]{0,1:T(8,128)(2,1)}, u32[]{:S(2)}, u32[]{:S(2)}) collective-permute-start(bf16[512,576]{0,1:T(8,128)(2,1)} %copy.17), channel_id=1, source_target_pairs={{0,1},{1,0},{2,3},{3,2},{4,5},{5,4},{6,7},{7,6},{8,9},{9,8},{10,11... | collective-permute-start | bytes 1769480 | tf_op jit(solution)/shard_map/ppermute | solution.py:116
  23.7 3.5 %copy-start.1 = (bf16[128,8,512]{2,0,1:T(8,128)(2,1)}, bf16[128,8,512]{2,0,1:T(8,128)(2,1)S(1)}, u32[]{:S(2)}) copy-start(bf16[128,8,512]{2,0,1:T(8,128)(2,1)S(1)} %copy.32) | copy-start | bytes 3145732
  25.8 1.7 %copy-start.8 = (bf16[128,8,576]{0,2,1:T(8,128)(2,1)S(1)}, bf16[128,8,576]{0,2,1:T(8,128)(2,1)}, u32[]{:S(2)}) copy-start(bf16[128,8,576]{0,2,1:T(8,128)(2,1)} %param.6) | copy-start | bytes 3538948
  25.9 1.1 %copy-start.5 = (bf16[1024,576]{1,0:T(8,128)(2,1)}, bf16[1024,576]{1,0:T(8,128)(2,1)S(1)}, u32[]{:S(2)}) copy-start(bf16[1024,576]{1,0:T(8,128)(2,1)S(1)} %constant_dynamic-update-slice_fusion.7.k_ref) | copy-start | bytes 3538948
  27.5 1.3 %copy-start.6 = (bf16[1024,576]{1,0:T(8,128)(2,1)S(1)}, bf16[1024,576]{1,0:T(8,128)(2,1)}, u32[]{:S(2)}) copy-start(bf16[1024,576]{1,0:T(8,128)(2,1)} %copy-done.5) | copy-start | bytes 3538948
  34.7 1.3 %copy-start.3 = (bf16[1024,1024]{1,0:T(8,128)(2,1)}, bf16[1024,1024]{1,0:T(8,128)(2,1)S(1)}, u32[]{:S(2)}) copy-start(bf16[1024,1024]{1,0:T(8,128)(2,1)S(1)} %get-tuple-element.6.p_ref) | copy-start | bytes 6291460
  39.0 5.8 %collective-permute-start.7 = (bf16[512,576]{0,1:T(8,128)(2,1)}, bf16[512,576]{0,1:T(8,128)(2,1)}, u32[]{:S(2)}, u32[]{:S(2)}) collective-permute-start(bf16[512,576]{0,1:T(8,128)(2,1)} %copy.20), channel_id=1, source_target_pairs={{0,1},{1,0},{2,3},{3,2},{4,5},{5,4},{6,7},{7,6},{8,9},{9,8},{10,11... | collective-permute-start | bytes 1769480 | tf_op jit(solution)/shard_map/ppermute | solution.py:116
  39.2 1.2 %copy-start.2 = (bf16[128,8,512]{2,0,1:T(8,128)(2,1)S(1)}, bf16[128,8,512]{2,0,1:T(8,128)(2,1)}, u32[]{:S(2)}) copy-start(bf16[128,8,512]{2,0,1:T(8,128)(2,1)} %copy-done.1) | copy-start | bytes 3145732
  40.4 1.6 %copy-start.4 = (bf16[1024,1024]{1,0:T(8,128)(2,1)S(1)}, bf16[1024,1024]{1,0:T(8,128)(2,1)}, u32[]{:S(2)}) copy-start(bf16[1024,1024]{1,0:T(8,128)(2,1)} %copy-done.3) | copy-start | bytes 6291460
  42.0 1.3 %copy-start.9 = (bf16[128,8,576]{0,2,1:T(8,128)(2,1)S(1)}, bf16[128,8,576]{0,2,1:T(8,128)(2,1)}, u32[]{:S(2)}) copy-start(bf16[128,8,576]{0,2,1:T(8,128)(2,1)} %param.6) | copy-start | bytes 3538948
  48.2 15.0 %copy-start.7 = (bf16[1024,576]{1,0:T(8,128)(2,1)S(1)}, bf16[1024,576]{1,0:T(8,128)(2,1)}, u32[]{:S(2)}) copy-start(bf16[1024,576]{1,0:T(8,128)(2,1)} %copy-done.5) | copy-start | bytes 3538948
  48.3 10.0 %collective-permute-start.8 = (bf16[128,576]{1,0:T(8,128)(2,1)S(1)}, bf16[128,576]{1,0:T(8,128)(2,1)S(1)}, u32[]{:S(2)}, u32[]{:S(2)}) collective-permute-start(bf16[128,576]{1,0:T(8,128)(2,1)S(1)} %get-tuple-element.12), channel_id=1, source_target_pairs={{0,2},{1,3},{2,0},{3,1},{4,6},{5,7},{6,4},{7,5},{8,10},{9,11},{10,... | collective-permute-start | bytes 442376 | tf_op jit(solution)/shard_map/ppermute | solution.py:116
  49.9 8.4 %collective-permute-start.10 = (bf16[128,576]{1,0:T(8,128)(2,1)S(1)}, bf16[128,576]{1,0:T(8,128)(2,1)S(1)}, u32[]{:S(2)}, u32[]{:S(2)}) collective-permute-start(bf16[128,576]{1,0:T(8,128)(2,1)S(1)} %get-tuple-element.13), channel_id=1, source_target_pairs={{0,6},{1,7},{2,4},{3,5},{4,2},{5,3},{6,0},{7,1},{8,14},{9,15},{10,... | collective-permute-start | bytes 442376 | tf_op jit(solution)/shard_map/ppermute | solution.py:116
  51.3 8.2 %collective-permute-start.9 = (bf16[128,576]{1,0:T(8,128)(2,1)S(1)}, bf16[128,576]{1,0:T(8,128)(2,1)S(1)}, u32[]{:S(2)}, u32[]{:S(2)}) collective-permute-start(bf16[128,576]{1,0:T(8,128)(2,1)S(1)} %get-tuple-element.14), channel_id=1, source_target_pairs={{0,4},{1,5},{2,6},{3,7},{4,0},{5,1},{6,2},{7,3},{8,12},{9,13},{10,... | collective-permute-start | bytes 442376 | tf_op jit(solution)/shard_map/ppermute | solution.py:116
  59.6 6.3 %collective-permute-start.11 = (bf16[32,576]{1,0:T(8,128)(2,1)S(1)}, bf16[32,576]{1,0:T(8,128)(2,1)S(1)}, u32[]{:S(2)}, u32[]{:S(2)}) collective-permute-start(bf16[32,576]{1,0:T(8,128)(2,1)S(1)} %get-tuple-element.15), channel_id=1, source_target_pairs={{0,8},{1,9},{2,10},{3,11},{4,12},{5,13},{6,14},{7,15},{8,0},{9,1},... | collective-permute-start | bytes 110600 | tf_op jit(solution)/shard_map/ppermute | solution.py:116
  60.4 5.8 %collective-permute-start.13 = (bf16[32,576]{1,0:T(8,128)(2,1)S(1)}, bf16[32,576]{1,0:T(8,128)(2,1)S(1)}, u32[]{:S(2)}, u32[]{:S(2)}) collective-permute-start(bf16[32,576]{1,0:T(8,128)(2,1)S(1)} %get-tuple-element.16), channel_id=1, source_target_pairs={{0,24},{1,25},{2,26},{3,27},{4,28},{5,29},{6,30},{7,31},{8,16},{9,... | collective-permute-start | bytes 110600 | tf_op jit(solution)/shard_map/ppermute | solution.py:116
  63.2 5.2 %collective-permute-start.12 = (bf16[32,576]{1,0:T(8,128)(2,1)S(1)}, bf16[32,576]{1,0:T(8,128)(2,1)S(1)}, u32[]{:S(2)}, u32[]{:S(2)}) collective-permute-start(bf16[32,576]{1,0:T(8,128)(2,1)S(1)} %get-tuple-element.17), channel_id=1, source_target_pairs={{0,16},{1,17},{2,18},{3,19},{4,20},{5,21},{6,22},{7,23},{8,24},{9,... | collective-permute-start | bytes 110600 | tf_op jit(solution)/shard_map/ppermute | solution.py:116
  (2 other events, 1.7 us)

commit v2 on v1

v2 whole, which is shorter than its diff:
```python
import jax
import jax.numpy as jnp
from jax import lax
from jax.experimental import pallas as pl
from jax.experimental.pallas import tpu as pltpu
from jax.sharding import PartitionSpec as P

QK_HEAD = 192
LARGE_NEGATIVE = -1e30
LOG2_E = 1.4426950408889634
LANES = 128
VMEM_LIMIT = 16 * 1024 * 1024

f32 = jnp.float32
bf16 = jnp.bfloat16
VMEM = pl.BlockSpec(memory_space=pltpu.VMEM)


def dot(a, b, a_dim, b_dim):
    return lax.dot_general(a, b, (((a_dim,), (b_dim,)), ((), ())), preferred_element_type=f32)


def side_by_side(blocks):
    return jnp.concatenate(blocks, axis=1)


def latent_rows(ds_ref, p_ref, qt, out_grad, rows):
    key_term = dot(ds_ref[rows, :], qt, 1, 1)
    value_term = dot(p_ref[rows, :], out_grad, 1, 0)
    width = value_term.shape[1]
    return key_term[:, :width] + value_term, key_term[:, width:]


def store_rows(out_ref, rows, left, right):
    width, used = left.shape[1], left.shape[1] + right.shape[1]
    out_ref[rows, :width] = left.astype(out_ref.dtype)
    out_ref[rows, width:used] = right.astype(out_ref.dtype)
    out_ref[rows, used:] = jnp.zeros((right.shape[0], out_ref.shape[1] - used), out_ref.dtype)


def latent_sums(out_ref, ds_ref, p_ref, qt, out_grad, first):
    step = min(256, out_ref.shape[0])
    for r in range(0, out_ref.shape[0], step):
        rows = slice(first + r, first + r + step)
        store_rows(out_ref, slice(r, r + step), *latent_rows(ds_ref, p_ref, qt, out_grad, rows))


GROUP = 2


def group_terms(qt_ref, og_ref, keys, kpos_ref, qpos_ref, g):
    _, kv_width, tokens = qt_ref.shape
    width = og_ref.shape[2]
    qt = side_by_side([qt_ref[h] for h in range(g, g + GROUP)])
    scores = dot(keys[:, :kv_width], qt, 1, 0)
    allowed = side_by_side([kpos_ref[...]] * GROUP) <= side_by_side([qpos_ref[...]] * GROUP)
    scores = jnp.where(allowed, scores * (QK_HEAD**-0.5 * LOG2_E), LARGE_NEGATIVE)
    out_grad = og_ref[g : g + GROUP].reshape(GROUP * tokens, width)
    return scores, dot(keys[:, :width], out_grad, 1, 1)


def stacked(refs):
    return jnp.concatenate([ref[...] for ref in refs])


def partial_kernel(qt_ref, og_ref, kpos_ref, qpos_ref, *refs):
    *piece_refs, mass_ref, vg_ref, peak_ref, sum_ref = refs
    heads, _, tokens = qt_ref.shape
    keys = stacked(piece_refs)
    for g in range(0, heads, GROUP):
        cols = slice(g * tokens, (g + GROUP) * tokens)
        scores, vg_ref[:, cols] = group_terms(qt_ref, og_ref, keys, kpos_ref, qpos_ref, g)
        peak = jnp.max(scores, axis=0, keepdims=True)
        mass = jnp.exp2(scores - peak)
        mass_ref[:, cols] = mass
        peak_ref[:, cols] = peak
        sum_ref[:, cols] = jnp.sum(mass, axis=0, keepdims=True)


def probs_kernel(qt_ref, og_ref, rd_ref, kpos_ref, qpos_ref, *refs):
    *refs, p_ref, ds_ref, far_ref = refs
    *piece_refs, mass0, vg0, peak0, sum0, mass1, vg1, peak1, sum1 = refs
    heads, _, tokens = qt_ref.shape
    width = og_ref.shape[2]
    half = p_ref.shape[0] // 2
    own = mass0.shape[0] // 2
    scale = QK_HEAD**-0.5
    keys = stacked(piece_refs)
    for g in range(0, heads, GROUP):
        cols = slice(g * tokens, (g + GROUP) * tokens)
        scores, grads = group_terms(qt_ref, og_ref, keys, kpos_ref, qpos_ref, g)
        last = jnp.max(scores, axis=0, keepdims=True)
        peak = jnp.maximum(jnp.maximum(peak0[:, cols], peak1[:, cols]), last)
        mass = jnp.exp2(scores - peak)
        ratio0, ratio1 = jnp.exp2(peak0[:, cols] - peak), jnp.exp2(peak1[:, cols] - peak)
        total = sum0[:, cols] * ratio0 + sum1[:, cols] * ratio1 + jnp.sum(mass, axis=0, keepdims=True)
        inverse = 1.0 / total
        row_dots = side_by_side([rd_ref[h] for h in range(g, g + GROUP)])
        parts = (
            (slice(0, own), mass0[:own, cols], vg0[:own, cols], inverse * ratio0),
            (slice(half, half + own), mass0[own:, cols], vg0[own:, cols], inverse * ratio0),
            (slice(own, half), mass1[:, cols], vg1[:, cols], inverse * ratio1),
            (slice(half + own, 2 * half), mass, grads, inverse),
        )
        for rows, part, value_grads, factor in parts:
            weights = part * factor
            p_ref[rows, cols] = weights.astype(bf16)
            ds_ref[rows, cols] = (weights * ((value_grads - row_dots) * scale)).astype(bf16)
    qt = side_by_side([qt_ref[h] for h in range(heads)])
    out_grad = og_ref[...].reshape(heads * tokens, width)
    latent_sums(far_ref, ds_ref, p_ref, qt, out_grad, half)


def first_kernel(qt_ref, og_ref, p_ref, ds_ref, near_ref, far_ref):
    heads, _, tokens = qt_ref.shape
    half = p_ref.shape[0] // 2
    qt = side_by_side([qt_ref[h] for h in range(heads)])
    out_grad = og_ref[...].reshape(heads * tokens, og_ref.shape[2])
    latent_sums(near_ref, ds_ref, p_ref, qt, out_grad, 0)
    latent_sums(far_ref, ds_ref, p_ref, qt, out_grad, half + half // 2)


def last_kernel(qt_ref, og_ref, p_ref, ds_ref, after_ref, near_ref):
    heads, _, tokens = qt_ref.shape
    half = p_ref.shape[0] // 2
    qt = side_by_side([qt_ref[h] for h in range(heads)])
    out_grad = og_ref[...].reshape(heads * tokens, og_ref.shape[2])
    latent_sums(near_ref, ds_ref, p_ref, qt, out_grad, half // 2)


def query_kernel(ds_ref, *refs):
    *piece_refs, dq_ref = refs
    heads, kv_width, tokens = dq_ref.shape
    keys = stacked(piece_refs)[:, :kv_width]
    for g in range(0, heads, GROUP):
        grads = dot(keys, ds_ref[:, g * tokens : (g + GROUP) * tokens], 0, 0).astype(bf16)
        for i in range(GROUP):
            dq_ref[g + i] = grads[:, i * tokens : (i + 1) * tokens]


def call(kernel, outs, flops, operands):
    return list(pl.pallas_call(
        kernel,
        in_specs=[VMEM] * len(operands),
        out_specs=[VMEM] * len(outs),
        out_shape=outs,
        compiler_params=pltpu.CompilerParams(vmem_limit_bytes=VMEM_LIMIT),
        cost_estimate=pl.CostEstimate(flops=flops, bytes_accessed=4 << 20, transcendentals=0),
    )(*operands))


def phases_of(device_count):
    bits = device_count.bit_length() - 1
    phases, bit = [[1]], 1
    while bit < bits:
        pair = [1 << bit] if bit + 1 == bits else [1 << bit, 2 << bit, 3 << bit]
        phases.append(pair)
        bit += 1 if len(pair) == 1 else 2
    return phases


def shards(queries, latents, out_grad, outputs, span_map):
    tokens, heads, kv_width = queries.shape
    width = out_grad.shape[2]
    head_size = lax.axis_size("head")
    devices = lax.axis_size("ctx") * head_size
    keys = lax.axis_size("ctx") * tokens
    span_rows = keys // span_map.shape[0]
    ctx, head = lax.axis_index("ctx"), lax.axis_index("head")
    me = ctx * head_size + head
    piece = tokens // head_size
    phases = phases_of(devices)
    around = phases[1][-1:] + phases[1][:-1]
    half_order = [0]
    for masks in [*reversed(phases[2:]), around]:
        half_order = half_order + [m ^ o for m in masks for o in half_order]

    def exchange(value, mask):
        return lax.ppermute(
            value, ("ctx", "head"), [(i, i ^ mask) for i in range(devices)]
        )

    def positions(spans, rows):
        at = rows // span_rows
        mine = at[:, None] == jnp.arange(spans.shape[0], dtype=jnp.int32)[None, :]
        return jnp.sum(jnp.where(mine, spans[None, :], 0), axis=1) * span_rows + rows % span_rows

    qt = queries.transpose(1, 2, 0)
    rows = heads * tokens
    half = keys // 2
    padded = -(-kv_width // LANES) * LANES
    pair_macs = half * rows * (kv_width + width)

    own = lax.dynamic_slice_in_dim(latents, head * piece, piece)
    own = jnp.pad(own, ((0, 0), (0, padded - kv_width)))
    for masks in reversed(phases[2:]):
        own = jnp.concatenate([own] + [exchange(own, m) for m in masks])
    own, out_grad, outputs, span_map = lax.optimization_barrier((own, out_grad, outputs, span_map))
    near = {m: exchange(own, m) for m in phases[1]}
    near = [near[m] for m in around]
    og = out_grad.transpose(1, 0, 2)
    row_dots = jnp.einsum("ihc,ihc->hi", out_grad, outputs, preferred_element_type=f32)
    row_dots = row_dots.reshape(heads, 1, tokens)
    starts = (me ^ jnp.array(half_order, dtype=jnp.int32)) * piece
    near_rows = (starts[:, None] + jnp.arange(piece, dtype=jnp.int32)[None, :]).reshape(-1)
    near_pos = positions(span_map, near_rows)
    far_pos = positions(span_map, near_rows + jnp.where(head % 2 == 0, piece, -piece))
    query_pos = positions(span_map, ctx * tokens + jnp.arange(tokens, dtype=jnp.int32))[None, :]
    owned = own.shape[0]
    own, row_dots = lax.optimization_barrier((own, row_dots))
    own_far = exchange(own, 1)

    def in_lanes(pos):
        return jnp.broadcast_to(pos[:, None], (pos.shape[0], LANES))

    def partial_terms(pos, pieces):
        count = sum(p.shape[0] for p in pieces)
        return call(
            partial_kernel,
            [
                pltpu.VMEM((count, rows), f32),
                pltpu.VMEM((count, rows), f32),
                pltpu.VMEM((1, rows), f32),
                pltpu.VMEM((1, rows), f32),
            ],
            2 * count * rows * (kv_width + width),
            [qt, og, pos, query_pos, *pieces],
        )

    own_lanes, near_lanes, far_lanes = lax.optimization_barrier(
        (
            in_lanes(jnp.concatenate([near_pos[:owned], far_pos[:owned]])),
            in_lanes(near_pos[owned:]),
            in_lanes(far_pos[owned:]),
        )
    )
    terms0 = partial_terms(own_lanes, [own, own_far])
    near, terms0[2] = lax.optimization_barrier((near, terms0[2]))
    far = [exchange(p, 1) for p in near]
    terms1 = partial_terms(near_lanes, near)
    weights, score_grads, far_a = call(
        probs_kernel,
        [
            pltpu.VMEM((keys, rows), bf16),
            pltpu.VMEM((keys, rows), bf16),
            jax.ShapeDtypeStruct((half // 2, padded), bf16),
        ],
        3 * pair_macs,
        [qt, og, row_dots, far_lanes, query_pos, *far, *terms0, *terms1],
    )
    arrived = exchange(far_a, 1)
    near_a, far_b = call(
        first_kernel,
        [
            jax.ShapeDtypeStruct((half // 2, padded), f32),
            jax.ShapeDtypeStruct((half // 2, padded), bf16),
        ],
        2 * pair_macs,
        [qt, og, weights, score_grads],
    )
    size = half // (len(around) + 1)
    kept = near_a + arrived.astype(f32)
    leading, after = lax.optimization_barrier((kept[size:].astype(bf16), terms0[2]))
    parts = [exchange(leading, around[0])]
    kept = kept[:size]
    arrived = exchange(far_b, 1)
    (near_b,) = call(
        last_kernel,
        [jax.ShapeDtypeStruct((half // 2, padded), f32)],
        pair_macs,
        [qt, og, weights, score_grads, after],
    )
    if len(around) > 1:
        sent = (near_b + arrived.astype(f32)).astype(bf16)
        parts += [exchange(sent[j * size : (j + 1) * size], m) for j, m in enumerate(around[1:])]
    total = kept + sum(part.astype(f32) for part in parts)
    (query_grads,) = call(
        query_kernel,
        [jax.ShapeDtypeStruct((heads, kv_width, tokens), bf16)],
        4 * half * rows * kv_width,
        [score_grads, own, *near, own_far, *far],
    )
    total, query_grads = lax.optimization_barrier((total, query_grads))
    for masks in phases[2:]:
        size = total.shape[0] // (len(masks) + 1)
        sent = total.astype(bf16)
        parts = {j: sent[(j + 1) * size : (j + 2) * size] for j in range(len(masks))}
        far_first = [len(masks) - 1, *range(len(masks) - 1)]
        total = total[:size] + sum(exchange(parts[j], masks[j]).astype(f32) for j in far_first)
    return query_grads.transpose(2, 0, 1), total[:, :kv_width]


def solution(mesh):
    placed = (
        P("ctx", "head", None),
        P("ctx", None),
        P("ctx", "head", None),
        P("ctx", "head", None),
        P(),
    )
    return jax.shard_map(
        shards,
        mesh=mesh,
        in_specs=placed,
        out_specs=(P("ctx", "head", None), P(("ctx", "head"), None)),
        check_vma=False,
    )
```

time: 69.6 us -> 48.7 us (0.70)
  local copies, waits for them, and re-layouts: 19 us -> 1.97 us
  waiting for transfers between devices: 17.6 us -> 12.9 us
  starting transfers between devices: 16.6 us -> 18.6 us
  other arithmetic: 4.84 us -> 3.75 us
    unnamed x32 -> x9, local copies, waits for them, and re-layouts: 11.7 us -> 1.02 us
    ppermute x14 -> x18, waiting for transfers between devices: 17.6 us -> 12.9 us  [exchange(): lax.ppermute(value, ('ctx', 'head'), [(i, i ^ mask) for i in range(device...]
    ppermute x2 -> x0, local copies, waits for them, and re-layouts: 3.5 us -> none  [exchange(): lax.ppermute(value, ('ctx', 'head'), [(i, i ^ mask) for i in range(device...]
    pallas_call x1 -> x0, local copies, waits for them, and re-layouts: 2.13 us -> none  [call(): pl.pallas_call(kernel, in_specs=[VMEM] * len(operands), out_specs=[VMEM]...]
    ppermute x14 -> x18, starting transfers between devices: 16.6 us -> 18.6 us  [exchange(): lax.ppermute(value, ('ctx', 'head'), [(i, i ^ mask) for i in range(device...]
    convert_element_type x2 -> x1, other arithmetic: 1.31 us -> 0.02 us  [shards(): sent = total.astype(bf16)]
    concatenate x3 -> x0, local copies, waits for them, and re-layouts: 1.21 us -> none  [shards(): jnp.concatenate([gathered] + [exchange(gathered, m) for m in masks])]
    pallas_call x3 -> x6, Pallas kernels: 10.1 us -> 10.4 us  [call(): pl.pallas_call(kernel, in_specs=[VMEM] * len(operands), out_specs=[VMEM]...]
  transfers between devices with their start and end apart: 14 -> 18, of which waited for: 7 -> 8; matrix products, arithmetic and copies ran while one was open for 7% -> 8% of each run, Pallas kernels for 6% -> 15%
where the time goes in v2:
time: 48.7 us; the launch traced here: 48.5 us
  starting transfers between devices  18.6 us (38%)
  waiting for transfers between devices  12.9 us (26%)
  Pallas kernels  10.4 us (21%)
  other arithmetic  3.75 us (8%)
  local copies, waits for them, and re-layouts  1.97 us (4%)
  between operations  0.92 us (2%)
    ppermute x18, starting transfers between devices, exchange(): lax.ppermute(value, ('ctx', 'head'), [(i, i ^ mask) for i in range(device...  18.6 us
    ppermute x18, waiting for transfers between devices, exchange(): lax.ppermute(value, ('ctx', 'head'), [(i, i ^ mask) for i in range(device...  12.9 us
    pallas_call x6, Pallas kernels, call(): pl.pallas_call(kernel, in_specs=[VMEM] * len(operands), out_specs=[VMEM]...  10.4 us
    unnamed x1, other arithmetic  1.89 us
    unnamed x9, local copies, waits for them, and re-layouts  1.02 us
  transfers between devices with their start and end apart: 18, of which 8 were waited for; matrix products, arithmetic and copies ran while one was open for 8% of the time, Pallas kernels for 15%

profile of v2, /device:TPU:0, one launch (start us, length us, event | category | flops | bytes accessed | tf_op | source)
XLA Modules:
  0.0 48.5 jit_solution(16695095860425936436)
XLA Ops:
  0.7 0.9 %copy-done = bf16[128,576]{0,1:T(8,128)(2,1)S(1)} copy-done((bf16[128,576]{0,1:T(8,128)(2,1)S(1)}, bf16[128,576]{0,1:T(8,128)(2,1)}, u32[]{:S(2)}) %copy-start) | copy-done | bytes 147480
  1.8 5.1 %collective-permute-start.2 = (bf16[32,640]{1,0:T(8,128)(2,1)S(1)}, bf16[32,640]{1,0:T(8,128)(2,1)S(1)}, u32[]{:S(2)}, u32[]{:S(2)}) collective-permute-start(bf16[32,640]{1,0:T(8,128)(2,1)S(1)} %pad.4), channel_id=1, source_target_pairs={{0,24},{1,25},{2,26},{3,27},{4,28},{5,29},{6,30},{7,31},{8,16},{9,... | collective-permute-start | bytes 122888 | tf_op jit(solution)/shard_map/ppermute | solution.py:179
  7.6 0.7 %xor_multiply_fusion = s32[16]{0:T(128)S(1)} fusion(s32[16]{0:T(128)} %constant.93.clone, s32[]{:T(128)S(6)} %add.146), kind=kLoop, calls=%fused_computation.45 | loop fusion | flops 32 | bytes 132 | tf_op jit(solution)/shard_map/mul | solution.py:204
  8.9 2.9 %collective-permute-done.1 = bf16[32,640]{1,0:T(8,128)(2,1)S(1)} collective-permute-done((bf16[32,640]{1,0:T(8,128)(2,1)S(1)}, bf16[32,640]{1,0:T(8,128)(2,1)S(1)}, u32[]{:S(2)}, u32[]{:S(2)}) %collective-permute-start.1) | collective-permute-done | bytes 40992 | tf_op jit(solution)/shard_map/ppermute | solution.py:179
  11.9 1.6 %collective-permute-start.5 = (bf16[128,640]{1,0:T(8,128)(2,1)S(1)}, bf16[128,640]{1,0:T(8,128)(2,1)S(1)}, u32[]{:S(2)}, u32[]{:S(2)}) collective-permute-start(bf16[128,640]{1,0:T(8,128)(2,1)S(1)} %pad_maximum_fusion.refs_0_), channel_id=1, source_target_pairs={{0,4},{1,5},{2,6},{3,7},{4,0},{5,1},{6,2},{7,3},{8,12},{9,13},{10,... | collective-permute-start | bytes 491528 | tf_op jit(solution)/shard_map/ppermute | solution.py:179
  13.4 1.5 %collective-permute-start.4 = (bf16[128,640]{1,0:T(8,128)(2,1)S(1)}, bf16[128,640]{1,0:T(8,128)(2,1)S(1)}, u32[]{:S(2)}, u32[]{:S(2)}) collective-permute-start(bf16[128,640]{1,0:T(8,128)(2,1)S(1)} %pad_maximum_fusion.refs_0_), channel_id=1, source_target_pairs={{0,2},{1,3},{2,0},{3,1},{4,6},{5,7},{6,4},{7,5},{8,10},{9,11},{10,... | collective-permute-start | bytes 491528 | tf_op jit(solution)/shard_map/ppermute | solution.py:179
  15.4 1.9 %fusion = f32[8,128]{0,1:T(8,128)S(1)} fusion(bf16[128,8,512]{2,1,0:T(8,128)(2,1)} %param.9, bf16[128,8,512]{2,1,0:T(8,128)(2,1)} %param.8), kind=kLoop, calls=%fused_computation.1 | loop fusion | flops 2096128 | bytes 2101248
  18.8 0.9 %shard_map.77 = (f32[256,1024]{1,0:T(8,128)S(1)}, f32[256,1024]{1,0:T(8,128)S(1)}, f32[1,1024]{1,0:T(1,128)S(1)}, f32[1,1024]{1,0:T(1,128)S(1)}) custom-call(bf16[8,576,128]{2,1,0:T(8,128)(2,1)S(1)} %bitcast.17, bf16[8,128,512]{2,1,0:T(8,128)(2,1)S(1)} %bitcast.12, s32[256,128]{1,0:T(8,128)S(1)} %broadcast_in_dim.36.kpos_ref, s32[1,128]{1,0:T(1,128)S(1)} %fusion.5.qpos_ref, ...), custom_call_target="tpu_custom_call" | custom-call | flops 570425344 | bytes 4194304 | tf_op jit(solution)/shard_map/pallas_call | solution.py:142
  19.7 2.1 %collective-permute-done.4.refs_1_.refs_2_ = bf16[128,640]{1,0:T(8,128)(2,1)S(1)} collective-permute-done((bf16[128,640]{1,0:T(8,128)(2,1)S(1)}, bf16[128,640]{1,0:T(8,128)(2,1)S(1)}, u32[]{:S(2)}, u32[]{:S(2)}) %collective-permute-start.4) | collective-permute-done | bytes 163872 | tf_op jit(solution)/shard_map/ppermute | solution.py:179
  22.3 1.3 %shard_map.78 = (f32[384,1024]{1,0:T(8,128)S(1)}, f32[384,1024]{1,0:T(8,128)S(1)}, f32[1,1024]{1,0:T(1,128)S(1)}, f32[1,1024]{1,0:T(1,128)S(1)}) custom-call(bf16[8,576,128]{2,1,0:T(8,128)(2,1)S(1)} %bitcast.18, bf16[8,128,512]{2,1,0:T(8,128)(2,1)S(1)} %bitcast.13, s32[384,128]{1,0:T(8,128)S(1)} %broadcast_in_dim.37.kpos_ref, s32[1,128]{1,0:T(1,128)S(1)} %fusion.5.qpos_ref, ...), custom_call_target="tpu_custom_call" | custom-call | flops 855638016 | bytes 4194304 | tf_op jit(solution)/shard_map/pallas_call | solution.py:142
  23.7 3.2 %shard_map.79 = (bf16[1024,1024]{1,0:T(8,128)(2,1)S(1)}, bf16[1024,1024]{1,0:T(8,128)(2,1)S(1)}, bf16[256,640]{1,0:T(8,128)(2,1)S(1)}) custom-call(bf16[8,576,128]{2,1,0:T(8,128)(2,1)S(1)} %bitcast.19, bf16[8,128,512]{2,1,0:T(8,128)(2,1)S(1)} %bitcast.14, f32[8,1,128]{2,1,0:T(1,128)S(1)} %bitcast.22, s32[384,128]{1,0:T(8,128)S(1)} %broadcast_in_dim.38.kpos_ref, ...), custom_call_target="tpu_custom_call" | custom-call | flops 1711276032 | bytes 4194304 | tf_op jit(solution)/shard_map/pallas_call | solution.py:142
  27.5 1.6 %shard_map.80 = (f32[256,640]{1,0:T(8,128)S(1)}, bf16[256,640]{1,0:T(8,128)(2,1)S(1)}) custom-call(bf16[8,576,128]{2,1,0:T(8,128)(2,1)S(1)} %bitcast.20, bf16[8,128,512]{2,1,0:T(8,128)(2,1)S(1)} %bitcast.15, bf16[1024,1024]{1,0:T(8,128)(2,1)S(1)} %get-tuple-element.53.p_ref, bf16[1024,1024]{1,0:T(8,128)(2,1)S(1)} %get-tuple-element.54.ds_ref), custom_call_target="tpu_custom_call" | custom-call | flops 1140850688 | bytes 4194304 | tf_op jit(solution)/shard_map/pallas_call | solution.py:142
  29.3 0.9 %collective-permute-start.11 = (bf16[128,640]{1,0:T(8,128)(2,1)S(1)}, bf16[128,640]{1,0:T(8,128)(2,1)S(1)}, u32[]{:S(2)}, u32[]{:S(2)}) collective-permute-start(bf16[128,640]{1,0:T(8,128)(2,1)S(1)} %slice.70), channel_id=1, source_target_pairs={{0,6},{1,7},{2,4},{3,5},{4,2},{5,3},{6,0},{7,1},{8,14},{9,15},{10,... | collective-permute-start | bytes 491528 | tf_op jit(solution)/shard_map/ppermute | solution.py:179
  30.2 0.9 %shard_map.81 = f32[256,640]{1,0:T(8,128)S(1)} custom-call(bf16[8,576,128]{2,1,0:T(8,128)(2,1)S(1)} %bitcast.21, bf16[8,128,512]{2,1,0:T(8,128)(2,1)S(1)} %bitcast.16, bf16[1024,1024]{1,0:T(8,128)(2,1)S(1)} %get-tuple-element.53.p_ref, bf16[1024,1024]{1,0:T(8,128)(2,1)S(1)} %get-tuple-element.54.ds_ref, f32[1,1024]{1,0:T(1,128)S(1)} %get-tuple-element.58.refs_5_.after_ref), custom_call_target="tpu_custom_call" | custom-call | flops 570425344 | bytes 4194304 | tf_op jit(solution)/shard_map/pallas_call | solution.py:142
  31.2 1.3 %collective-permute-start.13 = (bf16[128,640]{1,0:T(8,128)(2,1)S(1)}, bf16[128,640]{1,0:T(8,128)(2,1)S(1)}, u32[]{:S(2)}, u32[]{:S(2)}) collective-permute-start(bf16[128,640]{1,0:T(8,128)(2,1)S(1)} %get-tuple-element.64), channel_id=1, source_target_pairs={{0,2},{1,3},{2,0},{3,1},{4,6},{5,7},{6,4},{7,5},{8,10},{9,11},{10,... | collective-permute-start | bytes 491528 | tf_op jit(solution)/shard_map/ppermute | solution.py:179
  32.4 1.4 %collective-permute-start.14 = (bf16[128,640]{1,0:T(8,128)(2,1)S(1)}, bf16[128,640]{1,0:T(8,128)(2,1)S(1)}, u32[]{:S(2)}, u32[]{:S(2)}) collective-permute-start(bf16[128,640]{1,0:T(8,128)(2,1)S(1)} %get-tuple-element.65), channel_id=1, source_target_pairs={{0,4},{1,5},{2,6},{3,7},{4,0},{5,1},{6,2},{7,3},{8,12},{9,13},{10,... | collective-permute-start | bytes 491528 | tf_op jit(solution)/shard_map/ppermute | solution.py:179
  33.9 2.5 %shard_map.82 = bf16[8,576,128]{2,1,0:T(8,128)(2,1)} custom-call(bf16[1024,1024]{1,0:T(8,128)(2,1)S(1)} %get-tuple-element.54.ds_ref, bf16[128,640]{1,0:T(8,128)(2,1)S(1)} %pad_maximum_fusion.refs_0_, bf16[128,640]{1,0:T(8,128)(2,1)S(1)} %collective-permute-done.3.refs_0_.refs_1_, bf16[128,640]{1,0:T(8,128)(2,1)S(1)} %collective-permute-done.4.refs_1_.refs_2_, ...), custom_call_target="tpu_custom_call" | custom-call | flops 1207959552 | bytes 4194304 | tf_op jit(solution)/shard_map/pallas_call | solution.py:142
  36.3 0.9 %collective-permute-done.11 = bf16[128,640]{1,0:T(8,128)(2,1)S(1)} collective-permute-done((bf16[128,640]{1,0:T(8,128)(2,1)S(1)}, bf16[128,640]{1,0:T(8,128)(2,1)S(1)}, u32[]{:S(2)}, u32[]{:S(2)}) %collective-permute-start.11) | collective-permute-done | bytes 163872 | tf_op jit(solution)/shard_map/ppermute | solution.py:179
  37.3 3.0 %collective-permute-done.13 = bf16[128,640]{1,0:T(8,128)(2,1)S(1)} collective-permute-done((bf16[128,640]{1,0:T(8,128)(2,1)S(1)}, bf16[128,640]{1,0:T(8,128)(2,1)S(1)}, u32[]{:S(2)}, u32[]{:S(2)}) %collective-permute-start.13) | collective-permute-done | bytes 163872 | tf_op jit(solution)/shard_map/ppermute | solution.py:179
  40.4 1.9 %collective-permute-start.15 = (bf16[32,640]{1,0:T(8,128)(2,1)S(1)}, bf16[32,640]{1,0:T(8,128)(2,1)S(1)}, u32[]{:S(2)}, u32[]{:S(2)}) collective-permute-start(bf16[32,640]{1,0:T(8,128)(2,1)S(1)} %get-tuple-element.66), channel_id=1, source_target_pairs={{0,24},{1,25},{2,26},{3,27},{4,28},{5,29},{6,30},{7,31},{8,16},{9,... | collective-permute-start | bytes 122888 | tf_op jit(solution)/shard_map/ppermute | solution.py:179
  42.6 2.3 %collective-permute-start.16 = (bf16[32,640]{1,0:T(8,128)(2,1)S(1)}, bf16[32,640]{1,0:T(8,128)(2,1)S(1)}, u32[]{:S(2)}, u32[]{:S(2)}) collective-permute-start(bf16[32,640]{1,0:T(8,128)(2,1)S(1)} %get-tuple-element.68), channel_id=1, source_target_pairs={{0,8},{1,9},{2,10},{3,11},{4,12},{5,13},{6,14},{7,15},{8,0},{9,1},... | collective-permute-start | bytes 122888 | tf_op jit(solution)/shard_map/ppermute | solution.py:179
  44.9 1.9 %collective-permute-done.15 = bf16[32,640]{1,0:T(8,128)(2,1)S(1)} collective-permute-done((bf16[32,640]{1,0:T(8,128)(2,1)S(1)}, bf16[32,640]{1,0:T(8,128)(2,1)S(1)}, u32[]{:S(2)}, u32[]{:S(2)}) %collective-permute-start.15) | collective-permute-done | bytes 40992 | tf_op jit(solution)/shard_map/ppermute | solution.py:179
  46.8 1.0 %collective-permute-done.17 = bf16[32,640]{1,0:T(8,128)(2,1)S(1)} collective-permute-done((bf16[32,640]{1,0:T(8,128)(2,1)S(1)}, bf16[32,640]{1,0:T(8,128)(2,1)S(1)}, u32[]{:S(2)}, u32[]{:S(2)}) %collective-permute-start.17) | collective-permute-done | bytes 40992 | tf_op jit(solution)/shard_map/ppermute | solution.py:179
  47.8 0.7 %slice_add_fusion.1 = f32[32,576]{1,0:T(8,128)} fusion(f32[32,640]{1,0:T(8,128)S(1)} %slice.48, bf16[32,640]{1,0:T(8,128)(2,1)S(1)} %collective-permute-done.17, bf16[32,640]{1,0:T(8,128)(2,1)S(1)} %collective-permute-done.16, bf16[32,640]{1,0:T(8,128)(2,1)S(1)} %collective-permute-done.15), kind=kLoop, calls=%fused_computation.8 | loop fusion | flops 110592 | bytes 258048 | tf_op jit(solution)/shard_map/add | solution.py:289
  (59 shorter events, 5.2 us)
Async XLA Ops:
  0.6 0.9 %copy-start = (bf16[128,576]{0,1:T(8,128)(2,1)S(1)}, bf16[128,576]{0,1:T(8,128)(2,1)}, u32[]{:S(2)}) copy-start(bf16[128,576]{0,1:T(8,128)(2,1)} %param.7) | copy-start | bytes 442372
  0.6 16.8 %copy-start.3 = (s32[16]{0:T(128)S(1)}, s32[16]{0:T(128)}, u32[]{:S(2)}) copy-start(s32[16]{0:T(128)} %param.10) | copy-start | bytes 196
  0.7 17.0 %copy-start.2 = (bf16[128,8,512]{2,1,0:T(8,128)(2,1)S(1)}, bf16[128,8,512]{2,1,0:T(8,128)(2,1)}, u32[]{:S(2)}) copy-start(bf16[128,8,512]{2,1,0:T(8,128)(2,1)} %param.8) | copy-start | bytes 3145732
  1.8 7.1 %collective-permute-start.2 = (bf16[32,640]{1,0:T(8,128)(2,1)S(1)}, bf16[32,640]{1,0:T(8,128)(2,1)S(1)}, u32[]{:S(2)}, u32[]{:S(2)}) collective-permute-start(bf16[32,640]{1,0:T(8,128)(2,1)S(1)} %pad.4), channel_id=1, source_target_pairs={{0,24},{1,25},{2,26},{3,27},{4,28},{5,29},{6,30},{7,31},{8,16},{9,... | collective-permute-start | bytes 122888 | tf_op jit(solution)/shard_map/ppermute | solution.py:179
  6.9 4.9 %collective-permute-start.1 = (bf16[32,640]{1,0:T(8,128)(2,1)S(1)}, bf16[32,640]{1,0:T(8,128)(2,1)S(1)}, u32[]{:S(2)}, u32[]{:S(2)}) collective-permute-start(bf16[32,640]{1,0:T(8,128)(2,1)S(1)} %pad.4), channel_id=1, source_target_pairs={{0,16},{1,17},{2,18},{3,19},{4,20},{5,21},{6,22},{7,23},{8,24},{9,... | collective-permute-start | bytes 122888 | tf_op jit(solution)/shard_map/ppermute | solution.py:179
  6.9 4.9 %collective-permute-start = (bf16[32,640]{1,0:T(8,128)(2,1)S(1)}, bf16[32,640]{1,0:T(8,128)(2,1)S(1)}, u32[]{:S(2)}, u32[]{:S(2)}) collective-permute-start(bf16[32,640]{1,0:T(8,128)(2,1)S(1)} %pad.4), channel_id=1, source_target_pairs={{0,8},{1,9},{2,10},{3,11},{4,12},{5,13},{6,14},{7,15},{8,0},{9,1},... | collective-permute-start | bytes 122888 | tf_op jit(solution)/shard_map/ppermute | solution.py:179
  11.8 6.9 %copy-start.1 = (bf16[128,8,576]{0,2,1:T(8,128)(2,1)S(1)}, bf16[128,8,576]{0,2,1:T(8,128)(2,1)}, u32[]{:S(2)}) copy-start(bf16[128,8,576]{0,2,1:T(8,128)(2,1)} %param.6) | copy-start | bytes 3538948
  11.9 7.9 %collective-permute-start.5 = (bf16[128,640]{1,0:T(8,128)(2,1)S(1)}, bf16[128,640]{1,0:T(8,128)(2,1)S(1)}, u32[]{:S(2)}, u32[]{:S(2)}) collective-permute-start(bf16[128,640]{1,0:T(8,128)(2,1)S(1)} %pad_maximum_fusion.refs_0_), channel_id=1, source_target_pairs={{0,4},{1,5},{2,6},{3,7},{4,0},{5,1},{6,2},{7,3},{8,12},{9,13},{10,... | collective-permute-start | bytes 491528 | tf_op jit(solution)/shard_map/ppermute | solution.py:179
  13.4 8.4 %collective-permute-start.4 = (bf16[128,640]{1,0:T(8,128)(2,1)S(1)}, bf16[128,640]{1,0:T(8,128)(2,1)S(1)}, u32[]{:S(2)}, u32[]{:S(2)}) collective-permute-start(bf16[128,640]{1,0:T(8,128)(2,1)S(1)} %pad_maximum_fusion.refs_0_), channel_id=1, source_target_pairs={{0,2},{1,3},{2,0},{3,1},{4,6},{5,7},{6,4},{7,5},{8,10},{9,11},{10,... | collective-permute-start | bytes 491528 | tf_op jit(solution)/shard_map/ppermute | solution.py:179
  14.9 6.9 %collective-permute-start.3 = (bf16[128,640]{1,0:T(8,128)(2,1)S(1)}, bf16[128,640]{1,0:T(8,128)(2,1)S(1)}, u32[]{:S(2)}, u32[]{:S(2)}) collective-permute-start(bf16[128,640]{1,0:T(8,128)(2,1)S(1)} %pad_maximum_fusion.refs_0_), channel_id=1, source_target_pairs={{0,6},{1,7},{2,4},{3,5},{4,2},{5,3},{6,0},{7,1},{8,14},{9,15},{10,... | collective-permute-start | bytes 491528 | tf_op jit(solution)/shard_map/ppermute | solution.py:179
  17.3 1.4 %collective-permute-start.6 = (bf16[128,640]{1,0:T(8,128)(2,1)S(1)}, bf16[128,640]{1,0:T(8,128)(2,1)S(1)}, u32[]{:S(2)}, u32[]{:S(2)}) collective-permute-start(bf16[128,640]{1,0:T(8,128)(2,1)S(1)} %pad_maximum_fusion.refs_0_), channel_id=1, source_target_pairs={{0,1},{1,0},{2,3},{3,2},{4,5},{5,4},{6,7},{7,6},{8,9},{9,8},{10,11... | collective-permute-start | bytes 491528 | tf_op jit(solution)/shard_map/ppermute | solution.py:179
  21.8 1.8 %collective-permute-start.7 = (bf16[128,640]{1,0:T(8,128)(2,1)S(1)}, bf16[128,640]{1,0:T(8,128)(2,1)S(1)}, u32[]{:S(2)}, u32[]{:S(2)}) collective-permute-start(bf16[128,640]{1,0:T(8,128)(2,1)S(1)} %collective-permute-done.3.refs_0_.refs_1_), channel_id=1, source_target_pairs={{0,1},{1,0},{2,3},{3,2},{4,5},{5,4},{6,7},{7,6},{8,9},{9,8},{10,11... | collective-permute-start | bytes 491528 | tf_op jit(solution)/shard_map/ppermute | solution.py:179
  21.8 1.8 %collective-permute-start.8 = (bf16[128,640]{1,0:T(8,128)(2,1)S(1)}, bf16[128,640]{1,0:T(8,128)(2,1)S(1)}, u32[]{:S(2)}, u32[]{:S(2)}) collective-permute-start(bf16[128,640]{1,0:T(8,128)(2,1)S(1)} %collective-permute-done.4.refs_1_.refs_2_), channel_id=1, source_target_pairs={{0,1},{1,0},{2,3},{3,2},{4,5},{5,4},{6,7},{7,6},{8,9},{9,8},{10,11... | collective-permute-start | bytes 491528 | tf_op jit(solution)/shard_map/ppermute | solution.py:179
  22.3 1.4 %collective-permute-start.9 = (bf16[128,640]{1,0:T(8,128)(2,1)S(1)}, bf16[128,640]{1,0:T(8,128)(2,1)S(1)}, u32[]{:S(2)}, u32[]{:S(2)}) collective-permute-start(bf16[128,640]{1,0:T(8,128)(2,1)S(1)} %collective-permute-done.5.refs_2_.refs_3_), channel_id=1, source_target_pairs={{0,1},{1,0},{2,3},{3,2},{4,5},{5,4},{6,7},{7,6},{8,9},{9,8},{10,11... | collective-permute-start | bytes 491528 | tf_op jit(solution)/shard_map/ppermute | solution.py:179
  26.9 2.2 %collective-permute-start.10 = (bf16[256,640]{1,0:T(8,128)(2,1)S(1)}, bf16[256,640]{1,0:T(8,128)(2,1)S(1)}, u32[]{:S(2)}, u32[]{:S(2)}) collective-permute-start(bf16[256,640]{1,0:T(8,128)(2,1)S(1)} %get-tuple-element.56), channel_id=1, source_target_pairs={{0,1},{1,0},{2,3},{3,2},{4,5},{5,4},{6,7},{7,6},{8,9},{9,8},{10,11... | collective-permute-start | bytes 983048 | tf_op jit(solution)/shard_map/ppermute | solution.py:179
  29.1 2.0 %collective-permute-start.12 = (bf16[256,640]{1,0:T(8,128)(2,1)S(1)}, bf16[256,640]{1,0:T(8,128)(2,1)S(1)}, u32[]{:S(2)}, u32[]{:S(2)}) collective-permute-start(bf16[256,640]{1,0:T(8,128)(2,1)S(1)} %get-tuple-element.59), channel_id=1, source_target_pairs={{0,1},{1,0},{2,3},{3,2},{4,5},{5,4},{6,7},{7,6},{8,9},{9,8},{10,11... | collective-permute-start | bytes 983048 | tf_op jit(solution)/shard_map/ppermute | solution.py:179
  29.3 8.0 %collective-permute-start.11 = (bf16[128,640]{1,0:T(8,128)(2,1)S(1)}, bf16[128,640]{1,0:T(8,128)(2,1)S(1)}, u32[]{:S(2)}, u32[]{:S(2)}) collective-permute-start(bf16[128,640]{1,0:T(8,128)(2,1)S(1)} %slice.70), channel_id=1, source_target_pairs={{0,6},{1,7},{2,4},{3,5},{4,2},{5,3},{6,0},{7,1},{8,14},{9,15},{10,... | collective-permute-start | bytes 491528 | tf_op jit(solution)/shard_map/ppermute | solution.py:179
  31.2 9.1 %collective-permute-start.13 = (bf16[128,640]{1,0:T(8,128)(2,1)S(1)}, bf16[128,640]{1,0:T(8,128)(2,1)S(1)}, u32[]{:S(2)}, u32[]{:S(2)}) collective-permute-start(bf16[128,640]{1,0:T(8,128)(2,1)S(1)} %get-tuple-element.64), channel_id=1, source_target_pairs={{0,2},{1,3},{2,0},{3,1},{4,6},{5,7},{6,4},{7,5},{8,10},{9,11},{10,... | collective-permute-start | bytes 491528 | tf_op jit(solution)/shard_map/ppermute | solution.py:179
  32.4 7.9 %collective-permute-start.14 = (bf16[128,640]{1,0:T(8,128)(2,1)S(1)}, bf16[128,640]{1,0:T(8,128)(2,1)S(1)}, u32[]{:S(2)}, u32[]{:S(2)}) collective-permute-start(bf16[128,640]{1,0:T(8,128)(2,1)S(1)} %get-tuple-element.65), channel_id=1, source_target_pairs={{0,4},{1,5},{2,6},{3,7},{4,0},{5,1},{6,2},{7,3},{8,12},{9,13},{10,... | collective-permute-start | bytes 491528 | tf_op jit(solution)/shard_map/ppermute | solution.py:179
  40.4 6.3 %collective-permute-start.15 = (bf16[32,640]{1,0:T(8,128)(2,1)S(1)}, bf16[32,640]{1,0:T(8,128)(2,1)S(1)}, u32[]{:S(2)}, u32[]{:S(2)}) collective-permute-start(bf16[32,640]{1,0:T(8,128)(2,1)S(1)} %get-tuple-element.66), channel_id=1, source_target_pairs={{0,24},{1,25},{2,26},{3,27},{4,28},{5,29},{6,30},{7,31},{8,16},{9,... | collective-permute-start | bytes 122888 | tf_op jit(solution)/shard_map/ppermute | solution.py:179
  42.4 5.4 %collective-permute-start.17 = (bf16[32,640]{1,0:T(8,128)(2,1)S(1)}, bf16[32,640]{1,0:T(8,128)(2,1)S(1)}, u32[]{:S(2)}, u32[]{:S(2)}) collective-permute-start(bf16[32,640]{1,0:T(8,128)(2,1)S(1)} %get-tuple-element.67), channel_id=1, source_target_pairs={{0,16},{1,17},{2,18},{3,19},{4,20},{5,21},{6,22},{7,23},{8,24},{9,... | collective-permute-start | bytes 122888 | tf_op jit(solution)/shard_map/ppermute | solution.py:179
  42.6 5.2 %collective-permute-start.16 = (bf16[32,640]{1,0:T(8,128)(2,1)S(1)}, bf16[32,640]{1,0:T(8,128)(2,1)S(1)}, u32[]{:S(2)}, u32[]{:S(2)}) collective-permute-start(bf16[32,640]{1,0:T(8,128)(2,1)S(1)} %get-tuple-element.68), channel_id=1, source_target_pairs={{0,8},{1,9},{2,10},{3,11},{4,12},{5,13},{6,14},{7,15},{8,0},{9,1},... | collective-permute-start | bytes 122888 | tf_op jit(solution)/shard_map/ppermute | solution.py:179

commit v3 on v2

--- a/solution.py
+++ b/solution.py
@@ -1,3 +1,5 @@
+import functools
+
 import jax
 import jax.numpy as jnp
 from jax import lax
@@ -9,7 +11,7 @@
 LARGE_NEGATIVE = -1e30
 LOG2_E = 1.4426950408889634
 LANES = 128
-VMEM_LIMIT = 16 * 1024 * 1024
+VMEM_LIMIT = 8 * 1024 * 1024
 
 f32 = jnp.float32
 bf16 = jnp.bfloat16
@@ -31,42 +33,88 @@
     return key_term[:, :width] + value_term, key_term[:, width:]
 
 
-def store_rows(out_ref, rows, left, right):
-    width, used = left.shape[1], left.shape[1] + right.shape[1]
-    out_ref[rows, :width] = left.astype(out_ref.dtype)
-    out_ref[rows, width:used] = right.astype(out_ref.dtype)
-    out_ref[rows, used:] = jnp.zeros((right.shape[0], out_ref.shape[1] - used), out_ref.dtype)
-
-
-def latent_sums(out_ref, ds_ref, p_ref, qt, out_grad, first):
-    step = min(256, out_ref.shape[0])
-    for r in range(0, out_ref.shape[0], step):
+def packed(rows):
+    count, width = rows.shape
+    whole = width // LANES * LANES
+    blocks = [rows[:, c : c + LANES] for c in range(0, whole, LANES)]
+    if whole < width:
+        rest = rows[:, whole:]
+        blocks.append(jnp.concatenate([rest[: count // 2], rest[count // 2 :]], axis=1))
+    return jnp.concatenate(blocks)
+
+
+def unpacked(blocks, count, width):
+    whole = width // LANES
+    columns = [blocks[c * count : (c + 1) * count] for c in range(whole)]
+    if whole * LANES < width:
+        rest = blocks[whole * count :]
+        half = LANES // 2
+        columns.append(jnp.concatenate([rest[:, :half], rest[:, half:]]))
+    return jnp.concatenate(columns, axis=1)
+
+
+def stored_pieces(out_ref, first, piece, left, right):
+    width, rest = left.shape[1], right.shape[1]
+    if not piece:
+        rows = slice(first, first + left.shape[0])
+        out_ref[rows, :width] = left.astype(out_ref.dtype)
+        out_ref[rows, width : width + rest] = right.astype(out_ref.dtype)
+        unused = out_ref.shape[1] - width - rest
+        out_ref[rows, width + rest :] = jnp.zeros((left.shape[0], unused), out_ref.dtype)
+        return
+    high = piece * (width + rest) // LANES
+    for r in range(0, left.shape[0], piece):
+        base = (first + r) // piece * high
+        for c in range(0, width, LANES):
+            at = base + c // LANES * piece
+            out_ref[at : at + piece, :] = left[r : r + piece, c : c + LANES].astype(out_ref.dtype)
+        middle = r + piece // 2
+        folded = jnp.concatenate([right[r:middle], right[middle : r + piece]], axis=1)
+        out_ref[base + width // LANES * piece : base + high, :] = folded.astype(out_ref.dtype)
+
+
+def key_rows(refs, piece, kv_width):
+    if not piece:
+        return jnp.concatenate([ref[:, :kv_width] for ref in refs])
+    high = piece * kv_width // LANES
+    return jnp.concatenate(
+        [
+            unpacked(ref[r : r + high, :], piece, kv_width)
+            for ref in refs
+            for r in range(0, ref.shape[0], high)
+        ]
+    )
+
+
+def latent_sums(out_ref, piece, count, ds_ref, p_ref, qt, out_grad, first):
+    step = min(256, count)
+    for r in range(0, count, step):
         rows = slice(first + r, first + r + step)
-        store_rows(out_ref, slice(r, r + step), *latent_rows(ds_ref, p_ref, qt, out_grad, rows))
+        stored_pieces(out_ref, r, piece, *latent_rows(ds_ref, p_ref, qt, out_grad, rows))
 
 
 GROUP = 2
 
 
 def group_terms(qt_ref, og_ref, keys, kpos_ref, qpos_ref, g):
-    _, kv_width, tokens = qt_ref.shape
+    tokens = qt_ref.shape[2]
     width = og_ref.shape[2]
     qt = side_by_side([qt_ref[h] for h in range(g, g + GROUP)])
-    scores = dot(keys[:, :kv_width], qt, 1, 0)
+    scores = dot(keys, qt, 1, 0)
     allowed = side_by_side([kpos_ref[...]] * GROUP) <= side_by_side([qpos_ref[...]] * GROUP)
     scores = jnp.where(allowed, scores * (QK_HEAD**-0.5 * LOG2_E), LARGE_NEGATIVE)
     out_grad = og_ref[g : g + GROUP].reshape(GROUP * tokens, width)
     return scores, dot(keys[:, :width], out_grad, 1, 1)
 
 
-def stacked(refs):
-    return jnp.concatenate([ref[...] for ref in refs])
-
-
-def partial_kernel(qt_ref, og_ref, kpos_ref, qpos_ref, *refs):
+def pack_kernel(piece, rows_ref, out_ref):
+    out_ref[...] = packed(rows_ref[...])
+
+
+def partial_kernel(piece, qt_ref, og_ref, kpos_ref, qpos_ref, *refs):
     *piece_refs, mass_ref, vg_ref, peak_ref, sum_ref = refs
     heads, _, tokens = qt_ref.shape
-    keys = stacked(piece_refs)
+    keys = key_rows(piece_refs, piece, qt_ref.shape[1])
     for g in range(0, heads, GROUP):
         cols = slice(g * tokens, (g + GROUP) * tokens)
         scores, vg_ref[:, cols] = group_terms(qt_ref, og_ref, keys, kpos_ref, qpos_ref, g)
@@ -77,7 +125,7 @@
         sum_ref[:, cols] = jnp.sum(mass, axis=0, keepdims=True)
 
 
-def probs_kernel(qt_ref, og_ref, rd_ref, kpos_ref, qpos_ref, *refs):
+def probs_kernel(piece, qt_ref, og_ref, rd_ref, kpos_ref, qpos_ref, *refs):
     *refs, p_ref, ds_ref, far_ref = refs
     *piece_refs, mass0, vg0, peak0, sum0, mass1, vg1, peak1, sum1 = refs
     heads, _, tokens = qt_ref.shape
@@ -85,7 +133,7 @@
     half = p_ref.shape[0] // 2
     own = mass0.shape[0] // 2
     scale = QK_HEAD**-0.5
-    keys = stacked(piece_refs)
+    keys = key_rows(piece_refs, piece, qt_ref.shape[1])
     for g in range(0, heads, GROUP):
         cols = slice(g * tokens, (g + GROUP) * tokens)
         scores, grads = group_terms(qt_ref, og_ref, keys, kpos_ref, qpos_ref, g)
@@ -108,30 +156,30 @@
             ds_ref[rows, cols] = (weights * ((value_grads - row_dots) * scale)).astype(bf16)
     qt = side_by_side([qt_ref[h] for h in range(heads)])
     out_grad = og_ref[...].reshape(heads * tokens, width)
-    latent_sums(far_ref, ds_ref, p_ref, qt, out_grad, half)
-
-
-def first_kernel(qt_ref, og_ref, p_ref, ds_ref, near_ref, far_ref):
+    latent_sums(far_ref, piece, half // 2, ds_ref, p_ref, qt, out_grad, half)
+
+
+def first_kernel(piece, qt_ref, og_ref, p_ref, ds_ref, near_ref, far_ref):
     heads, _, tokens = qt_ref.shape
     half = p_ref.shape[0] // 2
     qt = side_by_side([qt_ref[h] for h in range(heads)])
     out_grad = og_ref[...].reshape(heads * tokens, og_ref.shape[2])
-    latent_sums(near_ref, ds_ref, p_ref, qt, out_grad, 0)
-    latent_sums(far_ref, ds_ref, p_ref, qt, out_grad, half + half // 2)
-
-
-def last_kernel(qt_ref, og_ref, p_ref, ds_ref, after_ref, near_ref):
+    latent_sums(near_ref, piece, half // 2, ds_ref, p_ref, qt, out_grad, 0)
+    latent_sums(far_ref, piece, half // 2, ds_ref, p_ref, qt, out_grad, half + half // 2)
+
+
+def last_kernel(piece, qt_ref, og_ref, p_ref, ds_ref, after_ref, near_ref):
     heads, _, tokens = qt_ref.shape
     half = p_ref.shape[0] // 2
     qt = side_by_side([qt_ref[h] for h in range(heads)])
     out_grad = og_ref[...].reshape(heads * tokens, og_ref.shape[2])
-    latent_sums(near_ref, ds_ref, p_ref, qt, out_grad, half // 2)
-
-
-def query_kernel(ds_ref, *refs):
+    latent_sums(near_ref, piece, half // 2, ds_ref, p_ref, qt, out_grad, half // 2)
+
+
+def query_kernel(piece, ds_ref, *refs):
     *piece_refs, dq_ref = refs
     heads, kv_width, tokens = dq_ref.shape
-    keys = stacked(piece_refs)[:, :kv_width]
+    keys = key_rows(piece_refs, piece, kv_width)
     for g in range(0, heads, GROUP):
         grads = dot(keys, ds_ref[:, g * tokens : (g + GROUP) * tokens], 0, 0).astype(bf16)
         for i in range(GROUP):
@@ -188,11 +236,23 @@
     qt = queries.transpose(1, 2, 0)
     rows = heads * tokens
     half = keys // 2
-    padded = -(-kv_width // LANES) * LANES
+    unit = piece if piece % 32 == 0 and kv_width % LANES == LANES // 2 else 0
+    columns = LANES if unit else -(-kv_width // LANES) * LANES
+
+    def high(count):
+        return count * kv_width // LANES if unit else count
+
+    def kernel(body):
+        return functools.partial(body, unit)
+
     pair_macs = half * rows * (kv_width + width)
 
     own = lax.dynamic_slice_in_dim(latents, head * piece, piece)
-    own = jnp.pad(own, ((0, 0), (0, padded - kv_width)))
+    if unit:
+        packed_shape = jax.ShapeDtypeStruct((high(piece), LANES), bf16)
+        (own,) = call(kernel(pack_kernel), [packed_shape], 0, [own])
+    else:
+        own = jnp.pad(own, ((0, 0), (0, columns - kv_width)))
     for masks in reversed(phases[2:]):
         own = jnp.concatenate([own] + [exchange(own, m) for m in masks])
     own, out_grad, outputs, span_map = lax.optimization_barrier((own, out_grad, outputs, span_map))
@@ -206,7 +266,7 @@
     near_pos = positions(span_map, near_rows)
     far_pos = positions(span_map, near_rows + jnp.where(head % 2 == 0, piece, -piece))
     query_pos = positions(span_map, ctx * tokens + jnp.arange(tokens, dtype=jnp.int32))[None, :]
-    owned = own.shape[0]
+    owned = half // (len(around) + 1)
     own, row_dots = lax.optimization_barrier((own, row_dots))
     own_far = exchange(own, 1)
 
@@ -214,9 +274,9 @@
         return jnp.broadcast_to(pos[:, None], (pos.shape[0], LANES))
 
     def partial_terms(pos, pieces):
-        count = sum(p.shape[0] for p in pieces)
+        count = pos.shape[0]
         return call(
-            partial_kernel,
+            kernel(partial_kernel),
             [
                 pltpu.VMEM((count, rows), f32),
                 pltpu.VMEM((count, rows), f32),
@@ -239,34 +299,34 @@
     far = [exchange(p, 1) for p in near]
     terms1 = partial_terms(near_lanes, near)
     weights, score_grads, far_a = call(
-        probs_kernel,
+        kernel(probs_kernel),
         [
             pltpu.VMEM((keys, rows), bf16),
             pltpu.VMEM((keys, rows), bf16),
-            jax.ShapeDtypeStruct((half // 2, padded), bf16),
+            jax.ShapeDtypeStruct((high(half // 2), columns), bf16),
         ],
         3 * pair_macs,
         [qt, og, row_dots, far_lanes, query_pos, *far, *terms0, *terms1],
     )
     arrived = exchange(far_a, 1)
     near_a, far_b = call(
-        first_kernel,
+        kernel(first_kernel),
         [
-            jax.ShapeDtypeStruct((half // 2, padded), f32),
-            jax.ShapeDtypeStruct((half // 2, padded), bf16),
+            jax.ShapeDtypeStruct((high(half // 2), columns), f32),
+            jax.ShapeDtypeStruct((high(half // 2), columns), bf16),
         ],
         2 * pair_macs,
         [qt, og, weights, score_grads],
     )
-    size = half // (len(around) + 1)
+    size = high(owned)
     kept = near_a + arrived.astype(f32)
     leading, after = lax.optimization_barrier((kept[size:].astype(bf16), terms0[2]))
     parts = [exchange(leading, around[0])]
     kept = kept[:size]
     arrived = exchange(far_b, 1)
     (near_b,) = call(
-        last_kernel,
-        [jax.ShapeDtypeStruct((half // 2, padded), f32)],
+        kernel(last_kernel),
+        [jax.ShapeDtypeStruct((high(half // 2), columns), f32)],
         pair_macs,
         [qt, og, weights, score_grads, after],
     )
@@ -275,7 +335,7 @@
         parts += [exchange(sent[j * size : (j + 1) * size], m) for j, m in enumerate(around[1:])]
     total = kept + sum(part.astype(f32) for part in parts)
     (query_grads,) = call(
-        query_kernel,
+        kernel(query_kernel),
         [jax.ShapeDtypeStruct((heads, kv_width, tokens), bf16)],
         4 * half * rows * kv_width,
         [score_grads, own, *near, own_far, *far],
@@ -287,7 +347,8 @@
         parts = {j: sent[(j + 1) * size : (j + 2) * size] for j in range(len(masks))}
         far_first = [len(masks) - 1, *range(len(masks) - 1)]
         total = total[:size] + sum(exchange(parts[j], masks[j]).astype(f32) for j in far_first)
-    return query_grads.transpose(2, 0, 1), total[:, :kv_width]
+    latent_grads = unpacked(total, piece, kv_width) if unit else total[:, :kv_width]
+    return query_grads.transpose(2, 0, 1), latent_grads
 
 
 def solution(mesh):

time: 48.7 us -> 47.1 us (0.967)
  waiting for transfers between devices: 12.9 us -> 11.3 us
  local copies, waits for them, and re-layouts: 1.97 us -> 2.65 us
  other arithmetic: 3.75 us -> 3.09 us
    ppermute x18, waiting for transfers between devices: 12.9 us -> 11.3 us  [exchange(): lax.ppermute(value, ('ctx', 'head'), [(i, i ^ mask) for i in range(device...]
    unnamed x9 -> x15, local copies, waits for them, and re-layouts: 1.02 us -> 1.66 us
    add x1, other arithmetic: 0.66 us -> 0.02 us  [shards(): total[:size]]
    pallas_call x6 -> x7, Pallas kernels: 10.4 us -> 10.4 us  [call(): pl.pallas_call(kernel, in_specs=[VMEM] * len(operands), out_specs=[VMEM]...]
where the time goes in v3:
time: 47.1 us; the launch traced here: 46.9 us
  starting transfers between devices  18.5 us (39%)
  waiting for transfers between devices  11.3 us (24%)
  Pallas kernels  10.4 us (22%)
  other arithmetic  3.09 us (7%)
  local copies, waits for them, and re-layouts  2.65 us (6%)
  between operations  0.95 us (2%)
    ppermute x18, starting transfers between devices, exchange(): lax.ppermute(value, ('ctx', 'head'), [(i, i ^ mask) for i in range(device...  18.5 us
    ppermute x18, waiting for transfers between devices, exchange(): lax.ppermute(value, ('ctx', 'head'), [(i, i ^ mask) for i in range(device...  11.3 us
    pallas_call x7, Pallas kernels, call(): pl.pallas_call(kernel, in_specs=[VMEM] * len(operands), out_specs=[VMEM]...  10.4 us
    unnamed x1, other arithmetic  1.89 us
    unnamed x15, local copies, waits for them, and re-layouts  1.66 us
  transfers between devices with their start and end apart: 18, of which 8 were waited for; matrix products, arithmetic and copies ran while one was open for 8% of the time, Pallas kernels for 15%

profile of v3, /device:TPU:0, one launch (start us, length us, event | category | flops | bytes accessed | tf_op | source)
XLA Modules:
  0.0 46.9 jit_solution(1995338896363260897)
XLA Ops:
  0.7 0.9 %copy-done = bf16[128,576]{0,1:T(8,128)(2,1)S(1)} copy-done((bf16[128,576]{0,1:T(8,128)(2,1)S(1)}, bf16[128,576]{0,1:T(8,128)(2,1)}, u32[]{:S(2)}) %copy-start) | copy-done | bytes 147480
  1.9 5.1 %collective-permute-start.2 = (bf16[144,128]{1,0:T(8,128)(2,1)S(1)}, bf16[144,128]{1,0:T(8,128)(2,1)S(1)}, u32[]{:S(2)}, u32[]{:S(2)}) collective-permute-start(bf16[144,128]{1,0:T(8,128)(2,1)S(1)} %shard_map.77), channel_id=1, source_target_pairs={{0,24},{1,25},{2,26},{3,27},{4,28},{5,29},{6,30},{7,31},{8,16},{9,... | collective-permute-start | bytes 110600 | tf_op jit(solution)/shard_map/ppermute | solution.py:227
  6.9 0.6 %collective-permute-start = (bf16[144,128]{1,0:T(8,128)(2,1)S(1)}, bf16[144,128]{1,0:T(8,128)(2,1)S(1)}, u32[]{:S(2)}, u32[]{:S(2)}) collective-permute-start(bf16[144,128]{1,0:T(8,128)(2,1)S(1)} %shard_map.77), channel_id=1, source_target_pairs={{0,8},{1,9},{2,10},{3,11},{4,12},{5,13},{6,14},{7,15},{8,0},{9,1},... | collective-permute-start | bytes 110600 | tf_op jit(solution)/shard_map/ppermute | solution.py:227
  7.6 0.7 %xor_multiply_fusion = s32[16]{0:T(128)S(1)} fusion(s32[16]{0:T(128)} %constant.91.clone, s32[]{:T(128)S(6)} %add.144), kind=kLoop, calls=%fused_computation.50 | loop fusion | flops 32 | bytes 132 | tf_op jit(solution)/shard_map/mul | solution.py:264
  8.9 2.9 %collective-permute-done.1 = bf16[144,128]{1,0:T(8,128)(2,1)S(1)} collective-permute-done((bf16[144,128]{1,0:T(8,128)(2,1)S(1)}, bf16[144,128]{1,0:T(8,128)(2,1)S(1)}, u32[]{:S(2)}, u32[]{:S(2)}) %collective-permute-start.1) | collective-permute-done | bytes 36896 | tf_op jit(solution)/shard_map/ppermute | solution.py:227
  11.8 1.6 %collective-permute-start.5 = (bf16[576,128]{1,0:T(8,128)(2,1)S(1)}, bf16[576,128]{1,0:T(8,128)(2,1)S(1)}, u32[]{:S(2)}, u32[]{:S(2)}) collective-permute-start(bf16[576,128]{1,0:T(8,128)(2,1)S(1)} %pad_maximum_fusion.refs_0_), channel_id=1, source_target_pairs={{0,4},{1,5},{2,6},{3,7},{4,0},{5,1},{6,2},{7,3},{8,12},{9,13},{10,... | collective-permute-start | bytes 442376 | tf_op jit(solution)/shard_map/ppermute | solution.py:227
  13.4 1.5 %collective-permute-start.4 = (bf16[576,128]{1,0:T(8,128)(2,1)S(1)}, bf16[576,128]{1,0:T(8,128)(2,1)S(1)}, u32[]{:S(2)}, u32[]{:S(2)}) collective-permute-start(bf16[576,128]{1,0:T(8,128)(2,1)S(1)} %pad_maximum_fusion.refs_0_), channel_id=1, source_target_pairs={{0,2},{1,3},{2,0},{3,1},{4,6},{5,7},{6,4},{7,5},{8,10},{9,11},{10,... | collective-permute-start | bytes 442376 | tf_op jit(solution)/shard_map/ppermute | solution.py:227
  15.4 1.9 %fusion = f32[8,128]{0,1:T(8,128)S(1)} fusion(bf16[128,8,512]{2,1,0:T(8,128)(2,1)} %param.9, bf16[128,8,512]{2,1,0:T(8,128)(2,1)} %param.8), kind=kLoop, calls=%fused_computation.1 | loop fusion | flops 2096128 | bytes 2101248
  18.7 1.0 %shard_map.78 = (f32[256,1024]{1,0:T(8,128)S(1)}, f32[256,1024]{1,0:T(8,128)S(1)}, f32[1,1024]{1,0:T(1,128)S(1)}, f32[1,1024]{1,0:T(1,128)S(1)}) custom-call(bf16[8,576,128]{2,1,0:T(8,128)(2,1)S(1)} %bitcast.17, bf16[8,128,512]{2,1,0:T(8,128)(2,1)S(1)} %bitcast.12, s32[256,128]{1,0:T(8,128)S(1)} %broadcast_in_dim.36.kpos_ref, s32[1,128]{1,0:T(1,128)S(1)} %fusion.5.qpos_ref, ...), custom_call_target="tpu_custom_call" | custom-call | flops 570425344 | bytes 4194304 | tf_op jit(solution)/shard_map/pallas_call | solution.py:190
  19.7 1.6 %collective-permute-done.4.refs_1_.refs_2_ = bf16[576,128]{1,0:T(8,128)(2,1)S(1)} collective-permute-done((bf16[576,128]{1,0:T(8,128)(2,1)S(1)}, bf16[576,128]{1,0:T(8,128)(2,1)S(1)}, u32[]{:S(2)}, u32[]{:S(2)}) %collective-permute-start.4) | collective-permute-done | bytes 147488 | tf_op jit(solution)/shard_map/ppermute | solution.py:227
  21.8 1.3 %shard_map.79 = (f32[384,1024]{1,0:T(8,128)S(1)}, f32[384,1024]{1,0:T(8,128)S(1)}, f32[1,1024]{1,0:T(1,128)S(1)}, f32[1,1024]{1,0:T(1,128)S(1)}) custom-call(bf16[8,576,128]{2,1,0:T(8,128)(2,1)S(1)} %bitcast.18, bf16[8,128,512]{2,1,0:T(8,128)(2,1)S(1)} %bitcast.13, s32[384,128]{1,0:T(8,128)S(1)} %broadcast_in_dim.37.kpos_ref, s32[1,128]{1,0:T(1,128)S(1)} %fusion.5.qpos_ref, ...), custom_call_target="tpu_custom_call" | custom-call | flops 855638016 | bytes 4194304 | tf_op jit(solution)/shard_map/pallas_call | solution.py:190
  23.1 3.2 %shard_map.80 = (bf16[1024,1024]{1,0:T(8,128)(2,1)S(1)}, bf16[1024,1024]{1,0:T(8,128)(2,1)S(1)}, bf16[1152,128]{1,0:T(8,128)(2,1)S(1)}) custom-call(bf16[8,576,128]{2,1,0:T(8,128)(2,1)S(1)} %bitcast.19, bf16[8,128,512]{2,1,0:T(8,128)(2,1)S(1)} %bitcast.14, f32[8,1,128]{2,1,0:T(1,128)S(1)} %bitcast.22, s32[384,128]{1,0:T(8,128)S(1)} %broadcast_in_dim.38.kpos_ref, ...), custom_call_target="tpu_custom_call" | custom-call | flops 1711276032 | bytes 4194304 | tf_op jit(solution)/shard_map/pallas_call | solution.py:190
  26.8 1.6 %shard_map.81 = (f32[1152,128]{1,0:T(8,128)S(1)}, bf16[1152,128]{1,0:T(8,128)(2,1)S(1)}) custom-call(bf16[8,576,128]{2,1,0:T(8,128)(2,1)S(1)} %bitcast.20, bf16[8,128,512]{2,1,0:T(8,128)(2,1)S(1)} %bitcast.15, bf16[1024,1024]{1,0:T(8,128)(2,1)S(1)} %get-tuple-element.53.p_ref, bf16[1024,1024]{1,0:T(8,128)(2,1)S(1)} %get-tuple-element.54.ds_ref), custom_call_target="tpu_custom_call" | custom-call | flops 1140850688 | bytes 4194304 | tf_op jit(solution)/shard_map/pallas_call | solution.py:190
  28.6 1.2 %collective-permute-start.11 = (bf16[576,128]{1,0:T(8,128)(2,1)S(1)}, bf16[576,128]{1,0:T(8,128)(2,1)S(1)}, u32[]{:S(2)}, u32[]{:S(2)}) collective-permute-start(bf16[576,128]{1,0:T(8,128)(2,1)S(1)} %slice.96), channel_id=1, source_target_pairs={{0,6},{1,7},{2,4},{3,5},{4,2},{5,3},{6,0},{7,1},{8,14},{9,15},{10,... | collective-permute-start | bytes 442376 | tf_op jit(solution)/shard_map/ppermute | solution.py:227
  29.8 0.9 %shard_map.82 = f32[1152,128]{1,0:T(8,128)S(1)} custom-call(bf16[8,576,128]{2,1,0:T(8,128)(2,1)S(1)} %bitcast.21, bf16[8,128,512]{2,1,0:T(8,128)(2,1)S(1)} %bitcast.16, bf16[1024,1024]{1,0:T(8,128)(2,1)S(1)} %get-tuple-element.53.p_ref, bf16[1024,1024]{1,0:T(8,128)(2,1)S(1)} %get-tuple-element.54.ds_ref, f32[1,1024]{1,0:T(1,128)S(1)} %get-tuple-element.58.refs_5_.after_ref), custom_call_target="tpu_custom_call" | custom-call | flops 570425344 | bytes 4194304 | tf_op jit(solution)/shard_map/pallas_call | solution.py:190
  30.8 0.8 %collective-permute-start.13 = (bf16[576,128]{1,0:T(8,128)(2,1)S(1)}, bf16[576,128]{1,0:T(8,128)(2,1)S(1)}, u32[]{:S(2)}, u32[]{:S(2)}) collective-permute-start(bf16[576,128]{1,0:T(8,128)(2,1)S(1)} %get-tuple-element.64), channel_id=1, source_target_pairs={{0,2},{1,3},{2,0},{3,1},{4,6},{5,7},{6,4},{7,5},{8,10},{9,11},{10,... | collective-permute-start | bytes 442376 | tf_op jit(solution)/shard_map/ppermute | solution.py:227
  31.6 1.6 %collective-permute-start.14 = (bf16[576,128]{1,0:T(8,128)(2,1)S(1)}, bf16[576,128]{1,0:T(8,128)(2,1)S(1)}, u32[]{:S(2)}, u32[]{:S(2)}) collective-permute-start(bf16[576,128]{1,0:T(8,128)(2,1)S(1)} %get-tuple-element.65), channel_id=1, source_target_pairs={{0,4},{1,5},{2,6},{3,7},{4,0},{5,1},{6,2},{7,3},{8,12},{9,13},{10,... | collective-permute-start | bytes 442376 | tf_op jit(solution)/shard_map/ppermute | solution.py:227
  33.2 2.4 %shard_map.83 = bf16[8,576,128]{2,1,0:T(8,128)(2,1)} custom-call(bf16[1024,1024]{1,0:T(8,128)(2,1)S(1)} %get-tuple-element.54.ds_ref, bf16[576,128]{1,0:T(8,128)(2,1)S(1)} %pad_maximum_fusion.refs_0_, bf16[576,128]{1,0:T(8,128)(2,1)S(1)} %collective-permute-done.3.refs_0_.refs_1_, bf16[576,128]{1,0:T(8,128)(2,1)S(1)} %collective-permute-done.4.refs_1_.refs_2_, ...), custom_call_target="tpu_custom_call" | custom-call | flops 1207959552 | bytes 4194304 | tf_op jit(solution)/shard_map/pallas_call | solution.py:190
  36.2 2.7 %collective-permute-done.13 = bf16[576,128]{1,0:T(8,128)(2,1)S(1)} collective-permute-done((bf16[576,128]{1,0:T(8,128)(2,1)S(1)}, bf16[576,128]{1,0:T(8,128)(2,1)S(1)}, u32[]{:S(2)}, u32[]{:S(2)}) %collective-permute-start.13) | collective-permute-done | bytes 147488 | tf_op jit(solution)/shard_map/ppermute | solution.py:227
  39.1 1.8 %collective-permute-start.15 = (bf16[144,128]{1,0:T(8,128)(2,1)S(1)}, bf16[144,128]{1,0:T(8,128)(2,1)S(1)}, u32[]{:S(2)}, u32[]{:S(2)}) collective-permute-start(bf16[144,128]{1,0:T(8,128)(2,1)S(1)} %get-tuple-element.66), channel_id=1, source_target_pairs={{0,24},{1,25},{2,26},{3,27},{4,28},{5,29},{6,30},{7,31},{8,16},{9,... | collective-permute-start | bytes 110600 | tf_op jit(solution)/shard_map/ppermute | solution.py:227
  41.3 2.3 %collective-permute-start.16 = (bf16[144,128]{1,0:T(8,128)(2,1)S(1)}, bf16[144,128]{1,0:T(8,128)(2,1)S(1)}, u32[]{:S(2)}, u32[]{:S(2)}) collective-permute-start(bf16[144,128]{1,0:T(8,128)(2,1)S(1)} %get-tuple-element.68), channel_id=1, source_target_pairs={{0,8},{1,9},{2,10},{3,11},{4,12},{5,13},{6,14},{7,15},{8,0},{9,1},... | collective-permute-start | bytes 110600 | tf_op jit(solution)/shard_map/ppermute | solution.py:227
  43.5 1.8 %collective-permute-done.15 = bf16[144,128]{1,0:T(8,128)(2,1)S(1)} collective-permute-done((bf16[144,128]{1,0:T(8,128)(2,1)S(1)}, bf16[144,128]{1,0:T(8,128)(2,1)S(1)}, u32[]{:S(2)}, u32[]{:S(2)}) %collective-permute-start.15) | collective-permute-done | bytes 36896 | tf_op jit(solution)/shard_map/ppermute | solution.py:227
  45.3 0.8 %collective-permute-done.17 = bf16[144,128]{1,0:T(8,128)(2,1)S(1)} collective-permute-done((bf16[144,128]{1,0:T(8,128)(2,1)S(1)}, bf16[144,128]{1,0:T(8,128)(2,1)S(1)}, u32[]{:S(2)}, u32[]{:S(2)}) %collective-permute-start.17) | collective-permute-done | bytes 36896 | tf_op jit(solution)/shard_map/ppermute | solution.py:227
  46.3 0.6 %copy-done.3 = f32[32,576]{1,0:T(8,128)} copy-done((f32[32,576]{1,0:T(8,128)}, f32[32,576]{1,0:T(8,128)S(1)}, u32[]{:S(2)}) %copy-start.3) | copy-done | bytes 73752
  (66 shorter events, 5.3 us)
Async XLA Ops:
  0.6 0.9 %copy-start = (bf16[128,576]{0,1:T(8,128)(2,1)S(1)}, bf16[128,576]{0,1:T(8,128)(2,1)}, u32[]{:S(2)}) copy-start(bf16[128,576]{0,1:T(8,128)(2,1)} %param.7) | copy-start | bytes 442372
  0.6 16.7 %copy-start.4 = (s32[16]{0:T(128)S(1)}, s32[16]{0:T(128)}, u32[]{:S(2)}) copy-start(s32[16]{0:T(128)} %param.10) | copy-start | bytes 196
  0.7 17.0 %copy-start.2 = (bf16[128,8,512]{2,1,0:T(8,128)(2,1)S(1)}, bf16[128,8,512]{2,1,0:T(8,128)(2,1)}, u32[]{:S(2)}) copy-start(bf16[128,8,512]{2,1,0:T(8,128)(2,1)} %param.8) | copy-start | bytes 3145732
  1.9 7.0 %collective-permute-start.2 = (bf16[144,128]{1,0:T(8,128)(2,1)S(1)}, bf16[144,128]{1,0:T(8,128)(2,1)S(1)}, u32[]{:S(2)}, u32[]{:S(2)}) collective-permute-start(bf16[144,128]{1,0:T(8,128)(2,1)S(1)} %shard_map.77), channel_id=1, source_target_pairs={{0,24},{1,25},{2,26},{3,27},{4,28},{5,29},{6,30},{7,31},{8,16},{9,... | collective-permute-start | bytes 110600 | tf_op jit(solution)/shard_map/ppermute | solution.py:227
  6.9 4.9 %collective-permute-start.1 = (bf16[144,128]{1,0:T(8,128)(2,1)S(1)}, bf16[144,128]{1,0:T(8,128)(2,1)S(1)}, u32[]{:S(2)}, u32[]{:S(2)}) collective-permute-start(bf16[144,128]{1,0:T(8,128)(2,1)S(1)} %shard_map.77), channel_id=1, source_target_pairs={{0,16},{1,17},{2,18},{3,19},{4,20},{5,21},{6,22},{7,23},{8,24},{9,... | collective-permute-start | bytes 110600 | tf_op jit(solution)/shard_map/ppermute | solution.py:227
  6.9 4.9 %collective-permute-start = (bf16[144,128]{1,0:T(8,128)(2,1)S(1)}, bf16[144,128]{1,0:T(8,128)(2,1)S(1)}, u32[]{:S(2)}, u32[]{:S(2)}) collective-permute-start(bf16[144,128]{1,0:T(8,128)(2,1)S(1)} %shard_map.77), channel_id=1, source_target_pairs={{0,8},{1,9},{2,10},{3,11},{4,12},{5,13},{6,14},{7,15},{8,0},{9,1},... | collective-permute-start | bytes 110600 | tf_op jit(solution)/shard_map/ppermute | solution.py:227
  11.8 6.9 %copy-start.1 = (bf16[128,8,576]{0,2,1:T(8,128)(2,1)S(1)}, bf16[128,8,576]{0,2,1:T(8,128)(2,1)}, u32[]{:S(2)}) copy-start(bf16[128,8,576]{0,2,1:T(8,128)(2,1)} %param.6) | copy-start | bytes 3538948
  11.8 7.9 %collective-permute-start.5 = (bf16[576,128]{1,0:T(8,128)(2,1)S(1)}, bf16[576,128]{1,0:T(8,128)(2,1)S(1)}, u32[]{:S(2)}, u32[]{:S(2)}) collective-permute-start(bf16[576,128]{1,0:T(8,128)(2,1)S(1)} %pad_maximum_fusion.refs_0_), channel_id=1, source_target_pairs={{0,4},{1,5},{2,6},{3,7},{4,0},{5,1},{6,2},{7,3},{8,12},{9,13},{10,... | collective-permute-start | bytes 442376 | tf_op jit(solution)/shard_map/ppermute | solution.py:227
  13.4 7.9 %collective-permute-start.4 = (bf16[576,128]{1,0:T(8,128)(2,1)S(1)}, bf16[576,128]{1,0:T(8,128)(2,1)S(1)}, u32[]{:S(2)}, u32[]{:S(2)}) collective-permute-start(bf16[576,128]{1,0:T(8,128)(2,1)S(1)} %pad_maximum_fusion.refs_0_), channel_id=1, source_target_pairs={{0,2},{1,3},{2,0},{3,1},{4,6},{5,7},{6,4},{7,5},{8,10},{9,11},{10,... | collective-permute-start | bytes 442376 | tf_op jit(solution)/shard_map/ppermute | solution.py:227
  14.9 6.3 %collective-permute-start.3 = (bf16[576,128]{1,0:T(8,128)(2,1)S(1)}, bf16[576,128]{1,0:T(8,128)(2,1)S(1)}, u32[]{:S(2)}, u32[]{:S(2)}) collective-permute-start(bf16[576,128]{1,0:T(8,128)(2,1)S(1)} %pad_maximum_fusion.refs_0_), channel_id=1, source_target_pairs={{0,6},{1,7},{2,4},{3,5},{4,2},{5,3},{6,0},{7,1},{8,14},{9,15},{10,... | collective-permute-start | bytes 442376 | tf_op jit(solution)/shard_map/ppermute | solution.py:227
  17.3 1.4 %collective-permute-start.6 = (bf16[576,128]{1,0:T(8,128)(2,1)S(1)}, bf16[576,128]{1,0:T(8,128)(2,1)S(1)}, u32[]{:S(2)}, u32[]{:S(2)}) collective-permute-start(bf16[576,128]{1,0:T(8,128)(2,1)S(1)} %pad_maximum_fusion.refs_0_), channel_id=1, source_target_pairs={{0,1},{1,0},{2,3},{3,2},{4,5},{5,4},{6,7},{7,6},{8,9},{9,8},{10,11... | collective-permute-start | bytes 442376 | tf_op jit(solution)/shard_map/ppermute | solution.py:227
  21.2 1.8 %collective-permute-start.7 = (bf16[576,128]{1,0:T(8,128)(2,1)S(1)}, bf16[576,128]{1,0:T(8,128)(2,1)S(1)}, u32[]{:S(2)}, u32[]{:S(2)}) collective-permute-start(bf16[576,128]{1,0:T(8,128)(2,1)S(1)} %collective-permute-done.3.refs_0_.refs_1_), channel_id=1, source_target_pairs={{0,1},{1,0},{2,3},{3,2},{4,5},{5,4},{6,7},{7,6},{8,9},{9,8},{10,11... | collective-permute-start | bytes 442376 | tf_op jit(solution)/shard_map/ppermute | solution.py:227
  21.2 1.8 %collective-permute-start.8 = (bf16[576,128]{1,0:T(8,128)(2,1)S(1)}, bf16[576,128]{1,0:T(8,128)(2,1)S(1)}, u32[]{:S(2)}, u32[]{:S(2)}) collective-permute-start(bf16[576,128]{1,0:T(8,128)(2,1)S(1)} %collective-permute-done.4.refs_1_.refs_2_), channel_id=1, source_target_pairs={{0,1},{1,0},{2,3},{3,2},{4,5},{5,4},{6,7},{7,6},{8,9},{9,8},{10,11... | collective-permute-start | bytes 442376 | tf_op jit(solution)/shard_map/ppermute | solution.py:227
  21.7 1.4 %collective-permute-start.9 = (bf16[576,128]{1,0:T(8,128)(2,1)S(1)}, bf16[576,128]{1,0:T(8,128)(2,1)S(1)}, u32[]{:S(2)}, u32[]{:S(2)}) collective-permute-start(bf16[576,128]{1,0:T(8,128)(2,1)S(1)} %collective-permute-done.5.refs_2_.refs_3_), channel_id=1, source_target_pairs={{0,1},{1,0},{2,3},{3,2},{4,5},{5,4},{6,7},{7,6},{8,9},{9,8},{10,11... | collective-permute-start | bytes 442376 | tf_op jit(solution)/shard_map/ppermute | solution.py:227
  26.3 2.2 %collective-permute-start.10 = (bf16[1152,128]{1,0:T(8,128)(2,1)S(1)}, bf16[1152,128]{1,0:T(8,128)(2,1)S(1)}, u32[]{:S(2)}, u32[]{:S(2)}) collective-permute-start(bf16[1152,128]{1,0:T(8,128)(2,1)S(1)} %get-tuple-element.56), channel_id=1, source_target_pairs={{0,1},{1,0},{2,3},{3,2},{4,5},{5,4},{6,7},{7,6},{8,9},{9,8},{10,11... | collective-permute-start | bytes 884744 | tf_op jit(solution)/shard_map/ppermute | solution.py:227
  28.4 2.2 %collective-permute-start.12 = (bf16[1152,128]{1,0:T(8,128)(2,1)S(1)}, bf16[1152,128]{1,0:T(8,128)(2,1)S(1)}, u32[]{:S(2)}, u32[]{:S(2)}) collective-permute-start(bf16[1152,128]{1,0:T(8,128)(2,1)S(1)} %get-tuple-element.59), channel_id=1, source_target_pairs={{0,1},{1,0},{2,3},{3,2},{4,5},{5,4},{6,7},{7,6},{8,9},{9,8},{10,11... | collective-permute-start | bytes 884744 | tf_op jit(solution)/shard_map/ppermute | solution.py:227
  28.6 7.7 %collective-permute-start.11 = (bf16[576,128]{1,0:T(8,128)(2,1)S(1)}, bf16[576,128]{1,0:T(8,128)(2,1)S(1)}, u32[]{:S(2)}, u32[]{:S(2)}) collective-permute-start(bf16[576,128]{1,0:T(8,128)(2,1)S(1)} %slice.96), channel_id=1, source_target_pairs={{0,6},{1,7},{2,4},{3,5},{4,2},{5,3},{6,0},{7,1},{8,14},{9,15},{10,... | collective-permute-start | bytes 442376 | tf_op jit(solution)/shard_map/ppermute | solution.py:227
  30.8 8.2 %collective-permute-start.13 = (bf16[576,128]{1,0:T(8,128)(2,1)S(1)}, bf16[576,128]{1,0:T(8,128)(2,1)S(1)}, u32[]{:S(2)}, u32[]{:S(2)}) collective-permute-start(bf16[576,128]{1,0:T(8,128)(2,1)S(1)} %get-tuple-element.64), channel_id=1, source_target_pairs={{0,2},{1,3},{2,0},{3,1},{4,6},{5,7},{6,4},{7,5},{8,10},{9,11},{10,... | collective-permute-start | bytes 442376 | tf_op jit(solution)/shard_map/ppermute | solution.py:227
  31.6 7.4 %collective-permute-start.14 = (bf16[576,128]{1,0:T(8,128)(2,1)S(1)}, bf16[576,128]{1,0:T(8,128)(2,1)S(1)}, u32[]{:S(2)}, u32[]{:S(2)}) collective-permute-start(bf16[576,128]{1,0:T(8,128)(2,1)S(1)} %get-tuple-element.65), channel_id=1, source_target_pairs={{0,4},{1,5},{2,6},{3,7},{4,0},{5,1},{6,2},{7,3},{8,12},{9,13},{10,... | collective-permute-start | bytes 442376 | tf_op jit(solution)/shard_map/ppermute | solution.py:227
  39.1 6.2 %collective-permute-start.15 = (bf16[144,128]{1,0:T(8,128)(2,1)S(1)}, bf16[144,128]{1,0:T(8,128)(2,1)S(1)}, u32[]{:S(2)}, u32[]{:S(2)}) collective-permute-start(bf16[144,128]{1,0:T(8,128)(2,1)S(1)} %get-tuple-element.66), channel_id=1, source_target_pairs={{0,24},{1,25},{2,26},{3,27},{4,28},{5,29},{6,30},{7,31},{8,16},{9,... | collective-permute-start | bytes 110600 | tf_op jit(solution)/shard_map/ppermute | solution.py:227
  40.9 5.3 %collective-permute-start.17 = (bf16[144,128]{1,0:T(8,128)(2,1)S(1)}, bf16[144,128]{1,0:T(8,128)(2,1)S(1)}, u32[]{:S(2)}, u32[]{:S(2)}) collective-permute-start(bf16[144,128]{1,0:T(8,128)(2,1)S(1)} %get-tuple-element.67), channel_id=1, source_target_pairs={{0,16},{1,17},{2,18},{3,19},{4,20},{5,21},{6,22},{7,23},{8,24},{9,... | collective-permute-start | bytes 110600 | tf_op jit(solution)/shard_map/ppermute | solution.py:227
  41.3 4.9 %collective-permute-start.16 = (bf16[144,128]{1,0:T(8,128)(2,1)S(1)}, bf16[144,128]{1,0:T(8,128)(2,1)S(1)}, u32[]{:S(2)}, u32[]{:S(2)}) collective-permute-start(bf16[144,128]{1,0:T(8,128)(2,1)S(1)} %get-tuple-element.68), channel_id=1, source_target_pairs={{0,8},{1,9},{2,10},{3,11},{4,12},{5,13},{6,14},{7,15},{8,0},{9,1},... | collective-permute-start | bytes 110600 | tf_op jit(solution)/shard_map/ppermute | solution.py:227
  46.3 0.6 %copy-start.3 = (f32[32,576]{1,0:T(8,128)}, f32[32,576]{1,0:T(8,128)S(1)}, u32[]{:S(2)}) copy-start(f32[32,576]{1,0:T(8,128)S(1)} %maximum_dynamic-update-slice_fusion) | copy-start | bytes 221188

commit v4 on v3

--- a/solution.py
+++ b/solution.py
@@ -93,7 +93,7 @@
         stored_pieces(out_ref, r, piece, *latent_rows(ds_ref, p_ref, qt, out_grad, rows))
 
 
-GROUP = 2
+GROUP = 4
 
 
 def group_terms(qt_ref, og_ref, keys, kpos_ref, qpos_ref, g):

time: 47.1 us -> 47.1 us (level)
  transfers between devices with their start and end apart: 18 -> 18, of which waited for: 8 -> 9; matrix products, arithmetic and copies ran while one was open for 8% -> 8% of each run, Pallas kernels for 15% -> 15%
where the time goes in v4:
time: 47.1 us; the launch traced here: 46.9 us
  starting transfers between devices  18.5 us (39%)
  waiting for transfers between devices  11.4 us (24%)
  Pallas kernels  10.3 us (22%)
  other arithmetic  3.09 us (7%)
  local copies, waits for them, and re-layouts  2.65 us (6%)
  between operations  0.95 us (2%)
    ppermute x18, starting transfers between devices, exchange(): lax.ppermute(value, ('ctx', 'head'), [(i, i ^ mask) for i in range(device...  18.5 us
    ppermute x18, waiting for transfers between devices, exchange(): lax.ppermute(value, ('ctx', 'head'), [(i, i ^ mask) for i in range(device...  11.4 us
    pallas_call x7, Pallas kernels, call(): pl.pallas_call(kernel, in_specs=[VMEM] * len(operands), out_specs=[VMEM]...  10.3 us
    unnamed x1, other arithmetic  1.89 us
    unnamed x15, local copies, waits for them, and re-layouts  1.66 us
  transfers between devices with their start and end apart: 18, of which 9 were waited for; matrix products, arithmetic and copies ran while one was open for 8% of the time, Pallas kernels for 15%

profile of v4, /device:TPU:0, one launch (start us, length us, event | category | flops | bytes accessed | tf_op | source)
XLA Modules:
  0.0 46.9 jit_solution(7003790295731401691)
XLA Ops:
  0.7 0.9 %copy-done = bf16[128,576]{0,1:T(8,128)(2,1)S(1)} copy-done((bf16[128,576]{0,1:T(8,128)(2,1)S(1)}, bf16[128,576]{0,1:T(8,128)(2,1)}, u32[]{:S(2)}) %copy-start) | copy-done | bytes 147480
  1.9 5.1 %collective-permute-start.2 = (bf16[144,128]{1,0:T(8,128)(2,1)S(1)}, bf16[144,128]{1,0:T(8,128)(2,1)S(1)}, u32[]{:S(2)}, u32[]{:S(2)}) collective-permute-start(bf16[144,128]{1,0:T(8,128)(2,1)S(1)} %shard_map.77), channel_id=1, source_target_pairs={{0,24},{1,25},{2,26},{3,27},{4,28},{5,29},{6,30},{7,31},{8,16},{9,... | collective-permute-start | bytes 110600 | tf_op jit(solution)/shard_map/ppermute | solution.py:227
  6.9 0.6 %collective-permute-start = (bf16[144,128]{1,0:T(8,128)(2,1)S(1)}, bf16[144,128]{1,0:T(8,128)(2,1)S(1)}, u32[]{:S(2)}, u32[]{:S(2)}) collective-permute-start(bf16[144,128]{1,0:T(8,128)(2,1)S(1)} %shard_map.77), channel_id=1, source_target_pairs={{0,8},{1,9},{2,10},{3,11},{4,12},{5,13},{6,14},{7,15},{8,0},{9,1},... | collective-permute-start | bytes 110600 | tf_op jit(solution)/shard_map/ppermute | solution.py:227
  7.6 0.7 %xor_multiply_fusion = s32[16]{0:T(128)S(1)} fusion(s32[16]{0:T(128)} %constant.91.clone, s32[]{:T(128)S(6)} %add.144), kind=kLoop, calls=%fused_computation.50 | loop fusion | flops 32 | bytes 132 | tf_op jit(solution)/shard_map/mul | solution.py:264
  8.9 2.9 %collective-permute-done.1 = bf16[144,128]{1,0:T(8,128)(2,1)S(1)} collective-permute-done((bf16[144,128]{1,0:T(8,128)(2,1)S(1)}, bf16[144,128]{1,0:T(8,128)(2,1)S(1)}, u32[]{:S(2)}, u32[]{:S(2)}) %collective-permute-start.1) | collective-permute-done | bytes 36896 | tf_op jit(solution)/shard_map/ppermute | solution.py:227
  11.8 1.6 %collective-permute-start.5 = (bf16[576,128]{1,0:T(8,128)(2,1)S(1)}, bf16[576,128]{1,0:T(8,128)(2,1)S(1)}, u32[]{:S(2)}, u32[]{:S(2)}) collective-permute-start(bf16[576,128]{1,0:T(8,128)(2,1)S(1)} %pad_maximum_fusion.refs_0_), channel_id=1, source_target_pairs={{0,4},{1,5},{2,6},{3,7},{4,0},{5,1},{6,2},{7,3},{8,12},{9,13},{10,... | collective-permute-start | bytes 442376 | tf_op jit(solution)/shard_map/ppermute | solution.py:227
  13.4 1.5 %collective-permute-start.4 = (bf16[576,128]{1,0:T(8,128)(2,1)S(1)}, bf16[576,128]{1,0:T(8,128)(2,1)S(1)}, u32[]{:S(2)}, u32[]{:S(2)}) collective-permute-start(bf16[576,128]{1,0:T(8,128)(2,1)S(1)} %pad_maximum_fusion.refs_0_), channel_id=1, source_target_pairs={{0,2},{1,3},{2,0},{3,1},{4,6},{5,7},{6,4},{7,5},{8,10},{9,11},{10,... | collective-permute-start | bytes 442376 | tf_op jit(solution)/shard_map/ppermute | solution.py:227
  15.4 1.9 %fusion = f32[8,128]{0,1:T(8,128)S(1)} fusion(bf16[128,8,512]{2,1,0:T(8,128)(2,1)} %param.9, bf16[128,8,512]{2,1,0:T(8,128)(2,1)} %param.8), kind=kLoop, calls=%fused_computation.1 | loop fusion | flops 2096128 | bytes 2101248
  18.7 0.9 %shard_map.78 = (f32[256,1024]{1,0:T(8,128)S(1)}, f32[256,1024]{1,0:T(8,128)S(1)}, f32[1,1024]{1,0:T(1,128)S(1)}, f32[1,1024]{1,0:T(1,128)S(1)}) custom-call(bf16[8,576,128]{2,1,0:T(8,128)(2,1)S(1)} %bitcast.17, bf16[8,128,512]{2,1,0:T(8,128)(2,1)S(1)} %bitcast.12, s32[256,128]{1,0:T(8,128)S(1)} %broadcast_in_dim.36.kpos_ref, s32[1,128]{1,0:T(1,128)S(1)} %fusion.5.qpos_ref, ...), custom_call_target="tpu_custom_call" | custom-call | flops 570425344 | bytes 4194304 | tf_op jit(solution)/shard_map/pallas_call | solution.py:190
  19.6 1.6 %collective-permute-done.4.refs_1_.refs_2_ = bf16[576,128]{1,0:T(8,128)(2,1)S(1)} collective-permute-done((bf16[576,128]{1,0:T(8,128)(2,1)S(1)}, bf16[576,128]{1,0:T(8,128)(2,1)S(1)}, u32[]{:S(2)}, u32[]{:S(2)}) %collective-permute-start.4) | collective-permute-done | bytes 147488 | tf_op jit(solution)/shard_map/ppermute | solution.py:227
  21.8 1.3 %shard_map.79 = (f32[384,1024]{1,0:T(8,128)S(1)}, f32[384,1024]{1,0:T(8,128)S(1)}, f32[1,1024]{1,0:T(1,128)S(1)}, f32[1,1024]{1,0:T(1,128)S(1)}) custom-call(bf16[8,576,128]{2,1,0:T(8,128)(2,1)S(1)} %bitcast.18, bf16[8,128,512]{2,1,0:T(8,128)(2,1)S(1)} %bitcast.13, s32[384,128]{1,0:T(8,128)S(1)} %broadcast_in_dim.37.kpos_ref, s32[1,128]{1,0:T(1,128)S(1)} %fusion.5.qpos_ref, ...), custom_call_target="tpu_custom_call" | custom-call | flops 855638016 | bytes 4194304 | tf_op jit(solution)/shard_map/pallas_call | solution.py:190
  23.1 3.1 %shard_map.80 = (bf16[1024,1024]{1,0:T(8,128)(2,1)S(1)}, bf16[1024,1024]{1,0:T(8,128)(2,1)S(1)}, bf16[1152,128]{1,0:T(8,128)(2,1)S(1)}) custom-call(bf16[8,576,128]{2,1,0:T(8,128)(2,1)S(1)} %bitcast.19, bf16[8,128,512]{2,1,0:T(8,128)(2,1)S(1)} %bitcast.14, f32[8,1,128]{2,1,0:T(1,128)S(1)} %bitcast.22, s32[384,128]{1,0:T(8,128)S(1)} %broadcast_in_dim.38.kpos_ref, ...), custom_call_target="tpu_custom_call" | custom-call | flops 1711276032 | bytes 4194304 | tf_op jit(solution)/shard_map/pallas_call | solution.py:190
  26.8 1.6 %shard_map.81 = (f32[1152,128]{1,0:T(8,128)S(1)}, bf16[1152,128]{1,0:T(8,128)(2,1)S(1)}) custom-call(bf16[8,576,128]{2,1,0:T(8,128)(2,1)S(1)} %bitcast.20, bf16[8,128,512]{2,1,0:T(8,128)(2,1)S(1)} %bitcast.15, bf16[1024,1024]{1,0:T(8,128)(2,1)S(1)} %get-tuple-element.53.p_ref, bf16[1024,1024]{1,0:T(8,128)(2,1)S(1)} %get-tuple-element.54.ds_ref), custom_call_target="tpu_custom_call" | custom-call | flops 1140850688 | bytes 4194304 | tf_op jit(solution)/shard_map/pallas_call | solution.py:190
  28.6 1.1 %collective-permute-start.11 = (bf16[576,128]{1,0:T(8,128)(2,1)S(1)}, bf16[576,128]{1,0:T(8,128)(2,1)S(1)}, u32[]{:S(2)}, u32[]{:S(2)}) collective-permute-start(bf16[576,128]{1,0:T(8,128)(2,1)S(1)} %slice.96), channel_id=1, source_target_pairs={{0,6},{1,7},{2,4},{3,5},{4,2},{5,3},{6,0},{7,1},{8,14},{9,15},{10,... | collective-permute-start | bytes 442376 | tf_op jit(solution)/shard_map/ppermute | solution.py:227
  29.6 0.9 %shard_map.82 = f32[1152,128]{1,0:T(8,128)S(1)} custom-call(bf16[8,576,128]{2,1,0:T(8,128)(2,1)S(1)} %bitcast.21, bf16[8,128,512]{2,1,0:T(8,128)(2,1)S(1)} %bitcast.16, bf16[1024,1024]{1,0:T(8,128)(2,1)S(1)} %get-tuple-element.53.p_ref, bf16[1024,1024]{1,0:T(8,128)(2,1)S(1)} %get-tuple-element.54.ds_ref, f32[1,1024]{1,0:T(1,128)S(1)} %get-tuple-element.58.refs_5_.after_ref), custom_call_target="tpu_custom_call" | custom-call | flops 570425344 | bytes 4194304 | tf_op jit(solution)/shard_map/pallas_call | solution.py:190
  30.6 0.9 %collective-permute-start.13 = (bf16[576,128]{1,0:T(8,128)(2,1)S(1)}, bf16[576,128]{1,0:T(8,128)(2,1)S(1)}, u32[]{:S(2)}, u32[]{:S(2)}) collective-permute-start(bf16[576,128]{1,0:T(8,128)(2,1)S(1)} %get-tuple-element.64), channel_id=1, source_target_pairs={{0,2},{1,3},{2,0},{3,1},{4,6},{5,7},{6,4},{7,5},{8,10},{9,11},{10,... | collective-permute-start | bytes 442376 | tf_op jit(solution)/shard_map/ppermute | solution.py:227
  31.6 1.6 %collective-permute-start.14 = (bf16[576,128]{1,0:T(8,128)(2,1)S(1)}, bf16[576,128]{1,0:T(8,128)(2,1)S(1)}, u32[]{:S(2)}, u32[]{:S(2)}) collective-permute-start(bf16[576,128]{1,0:T(8,128)(2,1)S(1)} %get-tuple-element.65), channel_id=1, source_target_pairs={{0,4},{1,5},{2,6},{3,7},{4,0},{5,1},{6,2},{7,3},{8,12},{9,13},{10,... | collective-permute-start | bytes 442376 | tf_op jit(solution)/shard_map/ppermute | solution.py:227
  33.2 2.4 %shard_map.83 = bf16[8,576,128]{2,1,0:T(8,128)(2,1)} custom-call(bf16[1024,1024]{1,0:T(8,128)(2,1)S(1)} %get-tuple-element.54.ds_ref, bf16[576,128]{1,0:T(8,128)(2,1)S(1)} %pad_maximum_fusion.refs_0_, bf16[576,128]{1,0:T(8,128)(2,1)S(1)} %collective-permute-done.3.refs_0_.refs_1_, bf16[576,128]{1,0:T(8,128)(2,1)S(1)} %collective-permute-done.4.refs_1_.refs_2_, ...), custom_call_target="tpu_custom_call" | custom-call | flops 1207959552 | bytes 4194304 | tf_op jit(solution)/shard_map/pallas_call | solution.py:190
  36.2 2.7 %collective-permute-done.13 = bf16[576,128]{1,0:T(8,128)(2,1)S(1)} collective-permute-done((bf16[576,128]{1,0:T(8,128)(2,1)S(1)}, bf16[576,128]{1,0:T(8,128)(2,1)S(1)}, u32[]{:S(2)}, u32[]{:S(2)}) %collective-permute-start.13) | collective-permute-done | bytes 147488 | tf_op jit(solution)/shard_map/ppermute | solution.py:227
  39.0 1.8 %collective-permute-start.15 = (bf16[144,128]{1,0:T(8,128)(2,1)S(1)}, bf16[144,128]{1,0:T(8,128)(2,1)S(1)}, u32[]{:S(2)}, u32[]{:S(2)}) collective-permute-start(bf16[144,128]{1,0:T(8,128)(2,1)S(1)} %get-tuple-element.66), channel_id=1, source_target_pairs={{0,24},{1,25},{2,26},{3,27},{4,28},{5,29},{6,30},{7,31},{8,16},{9,... | collective-permute-start | bytes 110600 | tf_op jit(solution)/shard_map/ppermute | solution.py:227
  41.2 2.3 %collective-permute-start.16 = (bf16[144,128]{1,0:T(8,128)(2,1)S(1)}, bf16[144,128]{1,0:T(8,128)(2,1)S(1)}, u32[]{:S(2)}, u32[]{:S(2)}) collective-permute-start(bf16[144,128]{1,0:T(8,128)(2,1)S(1)} %get-tuple-element.68), channel_id=1, source_target_pairs={{0,8},{1,9},{2,10},{3,11},{4,12},{5,13},{6,14},{7,15},{8,0},{9,1},... | collective-permute-start | bytes 110600 | tf_op jit(solution)/shard_map/ppermute | solution.py:227
  43.5 1.8 %collective-permute-done.15 = bf16[144,128]{1,0:T(8,128)(2,1)S(1)} collective-permute-done((bf16[144,128]{1,0:T(8,128)(2,1)S(1)}, bf16[144,128]{1,0:T(8,128)(2,1)S(1)}, u32[]{:S(2)}, u32[]{:S(2)}) %collective-permute-start.15) | collective-permute-done | bytes 36896 | tf_op jit(solution)/shard_map/ppermute | solution.py:227
  45.3 0.8 %collective-permute-done.17 = bf16[144,128]{1,0:T(8,128)(2,1)S(1)} collective-permute-done((bf16[144,128]{1,0:T(8,128)(2,1)S(1)}, bf16[144,128]{1,0:T(8,128)(2,1)S(1)}, u32[]{:S(2)}, u32[]{:S(2)}) %collective-permute-start.17) | collective-permute-done | bytes 36896 | tf_op jit(solution)/shard_map/ppermute | solution.py:227
  46.3 0.6 %copy-done.3 = f32[32,576]{1,0:T(8,128)} copy-done((f32[32,576]{1,0:T(8,128)}, f32[32,576]{1,0:T(8,128)S(1)}, u32[]{:S(2)}) %copy-start.3) | copy-done | bytes 73752
  (66 shorter events, 5.3 us)
Async XLA Ops:
  0.6 0.9 %copy-start = (bf16[128,576]{0,1:T(8,128)(2,1)S(1)}, bf16[128,576]{0,1:T(8,128)(2,1)}, u32[]{:S(2)}) copy-start(bf16[128,576]{0,1:T(8,128)(2,1)} %param.7) | copy-start | bytes 442372
  0.6 16.7 %copy-start.4 = (s32[16]{0:T(128)S(1)}, s32[16]{0:T(128)}, u32[]{:S(2)}) copy-start(s32[16]{0:T(128)} %param.10) | copy-start | bytes 196
  0.7 17.0 %copy-start.2 = (bf16[128,8,512]{2,1,0:T(8,128)(2,1)S(1)}, bf16[128,8,512]{2,1,0:T(8,128)(2,1)}, u32[]{:S(2)}) copy-start(bf16[128,8,512]{2,1,0:T(8,128)(2,1)} %param.8) | copy-start | bytes 3145732
  1.9 7.0 %collective-permute-start.2 = (bf16[144,128]{1,0:T(8,128)(2,1)S(1)}, bf16[144,128]{1,0:T(8,128)(2,1)S(1)}, u32[]{:S(2)}, u32[]{:S(2)}) collective-permute-start(bf16[144,128]{1,0:T(8,128)(2,1)S(1)} %shard_map.77), channel_id=1, source_target_pairs={{0,24},{1,25},{2,26},{3,27},{4,28},{5,29},{6,30},{7,31},{8,16},{9,... | collective-permute-start | bytes 110600 | tf_op jit(solution)/shard_map/ppermute | solution.py:227
  6.9 4.9 %collective-permute-start.1 = (bf16[144,128]{1,0:T(8,128)(2,1)S(1)}, bf16[144,128]{1,0:T(8,128)(2,1)S(1)}, u32[]{:S(2)}, u32[]{:S(2)}) collective-permute-start(bf16[144,128]{1,0:T(8,128)(2,1)S(1)} %shard_map.77), channel_id=1, source_target_pairs={{0,16},{1,17},{2,18},{3,19},{4,20},{5,21},{6,22},{7,23},{8,24},{9,... | collective-permute-start | bytes 110600 | tf_op jit(solution)/shard_map/ppermute | solution.py:227
  6.9 4.9 %collective-permute-start = (bf16[144,128]{1,0:T(8,128)(2,1)S(1)}, bf16[144,128]{1,0:T(8,128)(2,1)S(1)}, u32[]{:S(2)}, u32[]{:S(2)}) collective-permute-start(bf16[144,128]{1,0:T(8,128)(2,1)S(1)} %shard_map.77), channel_id=1, source_target_pairs={{0,8},{1,9},{2,10},{3,11},{4,12},{5,13},{6,14},{7,15},{8,0},{9,1},... | collective-permute-start | bytes 110600 | tf_op jit(solution)/shard_map/ppermute | solution.py:227
  11.8 6.9 %copy-start.1 = (bf16[128,8,576]{0,2,1:T(8,128)(2,1)S(1)}, bf16[128,8,576]{0,2,1:T(8,128)(2,1)}, u32[]{:S(2)}) copy-start(bf16[128,8,576]{0,2,1:T(8,128)(2,1)} %param.6) | copy-start | bytes 3538948
  11.8 7.8 %collective-permute-start.5 = (bf16[576,128]{1,0:T(8,128)(2,1)S(1)}, bf16[576,128]{1,0:T(8,128)(2,1)S(1)}, u32[]{:S(2)}, u32[]{:S(2)}) collective-permute-start(bf16[576,128]{1,0:T(8,128)(2,1)S(1)} %pad_maximum_fusion.refs_0_), channel_id=1, source_target_pairs={{0,4},{1,5},{2,6},{3,7},{4,0},{5,1},{6,2},{7,3},{8,12},{9,13},{10,... | collective-permute-start | bytes 442376 | tf_op jit(solution)/shard_map/ppermute | solution.py:227
  13.4 7.9 %collective-permute-start.4 = (bf16[576,128]{1,0:T(8,128)(2,1)S(1)}, bf16[576,128]{1,0:T(8,128)(2,1)S(1)}, u32[]{:S(2)}, u32[]{:S(2)}) collective-permute-start(bf16[576,128]{1,0:T(8,128)(2,1)S(1)} %pad_maximum_fusion.refs_0_), channel_id=1, source_target_pairs={{0,2},{1,3},{2,0},{3,1},{4,6},{5,7},{6,4},{7,5},{8,10},{9,11},{10,... | collective-permute-start | bytes 442376 | tf_op jit(solution)/shard_map/ppermute | solution.py:227
  14.9 6.3 %collective-permute-start.3 = (bf16[576,128]{1,0:T(8,128)(2,1)S(1)}, bf16[576,128]{1,0:T(8,128)(2,1)S(1)}, u32[]{:S(2)}, u32[]{:S(2)}) collective-permute-start(bf16[576,128]{1,0:T(8,128)(2,1)S(1)} %pad_maximum_fusion.refs_0_), channel_id=1, source_target_pairs={{0,6},{1,7},{2,4},{3,5},{4,2},{5,3},{6,0},{7,1},{8,14},{9,15},{10,... | collective-permute-start | bytes 442376 | tf_op jit(solution)/shard_map/ppermute | solution.py:227
  17.3 1.4 %collective-permute-start.6 = (bf16[576,128]{1,0:T(8,128)(2,1)S(1)}, bf16[576,128]{1,0:T(8,128)(2,1)S(1)}, u32[]{:S(2)}, u32[]{:S(2)}) collective-permute-start(bf16[576,128]{1,0:T(8,128)(2,1)S(1)} %pad_maximum_fusion.refs_0_), channel_id=1, source_target_pairs={{0,1},{1,0},{2,3},{3,2},{4,5},{5,4},{6,7},{7,6},{8,9},{9,8},{10,11... | collective-permute-start | bytes 442376 | tf_op jit(solution)/shard_map/ppermute | solution.py:227
  21.2 1.8 %collective-permute-start.7 = (bf16[576,128]{1,0:T(8,128)(2,1)S(1)}, bf16[576,128]{1,0:T(8,128)(2,1)S(1)}, u32[]{:S(2)}, u32[]{:S(2)}) collective-permute-start(bf16[576,128]{1,0:T(8,128)(2,1)S(1)} %collective-permute-done.3.refs_0_.refs_1_), channel_id=1, source_target_pairs={{0,1},{1,0},{2,3},{3,2},{4,5},{5,4},{6,7},{7,6},{8,9},{9,8},{10,11... | collective-permute-start | bytes 442376 | tf_op jit(solution)/shard_map/ppermute | solution.py:227
  21.2 1.8 %collective-permute-start.8 = (bf16[576,128]{1,0:T(8,128)(2,1)S(1)}, bf16[576,128]{1,0:T(8,128)(2,1)S(1)}, u32[]{:S(2)}, u32[]{:S(2)}) collective-permute-start(bf16[576,128]{1,0:T(8,128)(2,1)S(1)} %collective-permute-done.4.refs_1_.refs_2_), channel_id=1, source_target_pairs={{0,1},{1,0},{2,3},{3,2},{4,5},{5,4},{6,7},{7,6},{8,9},{9,8},{10,11... | collective-permute-start | bytes 442376 | tf_op jit(solution)/shard_map/ppermute | solution.py:227
  21.7 1.4 %collective-permute-start.9 = (bf16[576,128]{1,0:T(8,128)(2,1)S(1)}, bf16[576,128]{1,0:T(8,128)(2,1)S(1)}, u32[]{:S(2)}, u32[]{:S(2)}) collective-permute-start(bf16[576,128]{1,0:T(8,128)(2,1)S(1)} %collective-permute-done.5.refs_2_.refs_3_), channel_id=1, source_target_pairs={{0,1},{1,0},{2,3},{3,2},{4,5},{5,4},{6,7},{7,6},{8,9},{9,8},{10,11... | collective-permute-start | bytes 442376 | tf_op jit(solution)/shard_map/ppermute | solution.py:227
  26.3 2.2 %collective-permute-start.10 = (bf16[1152,128]{1,0:T(8,128)(2,1)S(1)}, bf16[1152,128]{1,0:T(8,128)(2,1)S(1)}, u32[]{:S(2)}, u32[]{:S(2)}) collective-permute-start(bf16[1152,128]{1,0:T(8,128)(2,1)S(1)} %get-tuple-element.56), channel_id=1, source_target_pairs={{0,1},{1,0},{2,3},{3,2},{4,5},{5,4},{6,7},{7,6},{8,9},{9,8},{10,11... | collective-permute-start | bytes 884744 | tf_op jit(solution)/shard_map/ppermute | solution.py:227
  28.4 2.1 %collective-permute-start.12 = (bf16[1152,128]{1,0:T(8,128)(2,1)S(1)}, bf16[1152,128]{1,0:T(8,128)(2,1)S(1)}, u32[]{:S(2)}, u32[]{:S(2)}) collective-permute-start(bf16[1152,128]{1,0:T(8,128)(2,1)S(1)} %get-tuple-element.59), channel_id=1, source_target_pairs={{0,1},{1,0},{2,3},{3,2},{4,5},{5,4},{6,7},{7,6},{8,9},{9,8},{10,11... | collective-permute-start | bytes 884744 | tf_op jit(solution)/shard_map/ppermute | solution.py:227
  28.6 7.7 %collective-permute-start.11 = (bf16[576,128]{1,0:T(8,128)(2,1)S(1)}, bf16[576,128]{1,0:T(8,128)(2,1)S(1)}, u32[]{:S(2)}, u32[]{:S(2)}) collective-permute-start(bf16[576,128]{1,0:T(8,128)(2,1)S(1)} %slice.96), channel_id=1, source_target_pairs={{0,6},{1,7},{2,4},{3,5},{4,2},{5,3},{6,0},{7,1},{8,14},{9,15},{10,... | collective-permute-start | bytes 442376 | tf_op jit(solution)/shard_map/ppermute | solution.py:227
  30.6 8.3 %collective-permute-start.13 = (bf16[576,128]{1,0:T(8,128)(2,1)S(1)}, bf16[576,128]{1,0:T(8,128)(2,1)S(1)}, u32[]{:S(2)}, u32[]{:S(2)}) collective-permute-start(bf16[576,128]{1,0:T(8,128)(2,1)S(1)} %get-tuple-element.64), channel_id=1, source_target_pairs={{0,2},{1,3},{2,0},{3,1},{4,6},{5,7},{6,4},{7,5},{8,10},{9,11},{10,... | collective-permute-start | bytes 442376 | tf_op jit(solution)/shard_map/ppermute | solution.py:227
  31.6 7.4 %collective-permute-start.14 = (bf16[576,128]{1,0:T(8,128)(2,1)S(1)}, bf16[576,128]{1,0:T(8,128)(2,1)S(1)}, u32[]{:S(2)}, u32[]{:S(2)}) collective-permute-start(bf16[576,128]{1,0:T(8,128)(2,1)S(1)} %get-tuple-element.65), channel_id=1, source_target_pairs={{0,4},{1,5},{2,6},{3,7},{4,0},{5,1},{6,2},{7,3},{8,12},{9,13},{10,... | collective-permute-start | bytes 442376 | tf_op jit(solution)/shard_map/ppermute | solution.py:227
  39.0 6.2 %collective-permute-start.15 = (bf16[144,128]{1,0:T(8,128)(2,1)S(1)}, bf16[144,128]{1,0:T(8,128)(2,1)S(1)}, u32[]{:S(2)}, u32[]{:S(2)}) collective-permute-start(bf16[144,128]{1,0:T(8,128)(2,1)S(1)} %get-tuple-element.66), channel_id=1, source_target_pairs={{0,24},{1,25},{2,26},{3,27},{4,28},{5,29},{6,30},{7,31},{8,16},{9,... | collective-permute-start | bytes 110600 | tf_op jit(solution)/shard_map/ppermute | solution.py:227
  40.9 5.3 %collective-permute-start.17 = (bf16[144,128]{1,0:T(8,128)(2,1)S(1)}, bf16[144,128]{1,0:T(8,128)(2,1)S(1)}, u32[]{:S(2)}, u32[]{:S(2)}) collective-permute-start(bf16[144,128]{1,0:T(8,128)(2,1)S(1)} %get-tuple-element.67), channel_id=1, source_target_pairs={{0,16},{1,17},{2,18},{3,19},{4,20},{5,21},{6,22},{7,23},{8,24},{9,... | collective-permute-start | bytes 110600 | tf_op jit(solution)/shard_map/ppermute | solution.py:227
  41.2 4.9 %collective-permute-start.16 = (bf16[144,128]{1,0:T(8,128)(2,1)S(1)}, bf16[144,128]{1,0:T(8,128)(2,1)S(1)}, u32[]{:S(2)}, u32[]{:S(2)}) collective-permute-start(bf16[144,128]{1,0:T(8,128)(2,1)S(1)} %get-tuple-element.68), channel_id=1, source_target_pairs={{0,8},{1,9},{2,10},{3,11},{4,12},{5,13},{6,14},{7,15},{8,0},{9,1},... | collective-permute-start | bytes 110600 | tf_op jit(solution)/shard_map/ppermute | solution.py:227
  46.2 0.6 %copy-start.3 = (f32[32,576]{1,0:T(8,128)}, f32[32,576]{1,0:T(8,128)S(1)}, u32[]{:S(2)}) copy-start(f32[32,576]{1,0:T(8,128)S(1)} %maximum_dynamic-update-slice_fusion) | copy-start | bytes 221188

commit v5 on v4

--- a/solution.py
+++ b/solution.py
@@ -111,13 +111,15 @@
     out_ref[...] = packed(rows_ref[...])
 
 
-def partial_kernel(piece, qt_ref, og_ref, kpos_ref, qpos_ref, *refs):
+def partial_kernel(piece, qt_ref, og_ref, rd_ref, kpos_ref, qpos_ref, *refs):
     *piece_refs, mass_ref, vg_ref, peak_ref, sum_ref = refs
     heads, _, tokens = qt_ref.shape
     keys = key_rows(piece_refs, piece, qt_ref.shape[1])
     for g in range(0, heads, GROUP):
         cols = slice(g * tokens, (g + GROUP) * tokens)
-        scores, vg_ref[:, cols] = group_terms(qt_ref, og_ref, keys, kpos_ref, qpos_ref, g)
+        scores, value_grads = group_terms(qt_ref, og_ref, keys, kpos_ref, qpos_ref, g)
+        row_dots = side_by_side([rd_ref[h] for h in range(g, g + GROUP)])
+        vg_ref[:, cols] = (value_grads - row_dots) * QK_HEAD**-0.5
         peak = jnp.max(scores, axis=0, keepdims=True)
         mass = jnp.exp2(scores - peak)
         mass_ref[:, cols] = mass
@@ -148,12 +150,12 @@
             (slice(0, own), mass0[:own, cols], vg0[:own, cols], inverse * ratio0),
             (slice(half, half + own), mass0[own:, cols], vg0[own:, cols], inverse * ratio0),
             (slice(own, half), mass1[:, cols], vg1[:, cols], inverse * ratio1),
-            (slice(half + own, 2 * half), mass, grads, inverse),
+            (slice(half + own, 2 * half), mass, (grads - row_dots) * scale, inverse),
         )
         for rows, part, value_grads, factor in parts:
             weights = part * factor
             p_ref[rows, cols] = weights.astype(bf16)
-            ds_ref[rows, cols] = (weights * ((value_grads - row_dots) * scale)).astype(bf16)
+            ds_ref[rows, cols] = (weights * value_grads).astype(bf16)
     qt = side_by_side([qt_ref[h] for h in range(heads)])
     out_grad = og_ref[...].reshape(heads * tokens, width)
     latent_sums(far_ref, piece, half // 2, ds_ref, p_ref, qt, out_grad, half)
@@ -284,7 +286,7 @@
                 pltpu.VMEM((1, rows), f32),
             ],
             2 * count * rows * (kv_width + width),
-            [qt, og, pos, query_pos, *pieces],
+            [qt, og, row_dots, pos, query_pos, *pieces],
         )
 
     own_lanes, near_lanes, far_lanes = lax.optimization_barrier(

time: 47.1 us -> 46.8 us (level)
  transfers between devices with their start and end apart: 18 -> 18, of which waited for: 9 -> 8; matrix products, arithmetic and copies ran while one was open for 8% -> 8% of each run, Pallas kernels for 15% -> 15%
where the time goes in v5:
time: 46.8 us; the launch traced here: 46.6 us
  starting transfers between devices  18.5 us (40%)
  waiting for transfers between devices  11.4 us (24%)
  Pallas kernels  10 us (21%)
  other arithmetic  3.09 us (7%)
  local copies, waits for them, and re-layouts  2.65 us (6%)
  between operations  0.97 us (2%)
    ppermute x18, starting transfers between devices, exchange(): lax.ppermute(value, ('ctx', 'head'), [(i, i ^ mask) for i in range(device...  18.5 us
    ppermute x18, waiting for transfers between devices, exchange(): lax.ppermute(value, ('ctx', 'head'), [(i, i ^ mask) for i in range(device...  11.4 us
    pallas_call x7, Pallas kernels, call(): pl.pallas_call(kernel, in_specs=[VMEM] * len(operands), out_specs=[VMEM]...  10 us
    unnamed x1, other arithmetic  1.89 us
    unnamed x15, local copies, waits for them, and re-layouts  1.66 us
  transfers between devices with their start and end apart: 18, of which 8 were waited for; matrix products, arithmetic and copies ran while one was open for 8% of the time, Pallas kernels for 15%

profile of v5, /device:TPU:0, one launch (start us, length us, event | category | flops | bytes accessed | tf_op | source)
XLA Modules:
  0.0 46.6 jit_solution(9779466538483485229)
XLA Ops:
  0.7 0.9 %copy-done = bf16[128,576]{0,1:T(8,128)(2,1)S(1)} copy-done((bf16[128,576]{0,1:T(8,128)(2,1)S(1)}, bf16[128,576]{0,1:T(8,128)(2,1)}, u32[]{:S(2)}) %copy-start) | copy-done | bytes 147480
  1.9 5.1 %collective-permute-start.2 = (bf16[144,128]{1,0:T(8,128)(2,1)S(1)}, bf16[144,128]{1,0:T(8,128)(2,1)S(1)}, u32[]{:S(2)}, u32[]{:S(2)}) collective-permute-start(bf16[144,128]{1,0:T(8,128)(2,1)S(1)} %shard_map.77), channel_id=1, source_target_pairs={{0,24},{1,25},{2,26},{3,27},{4,28},{5,29},{6,30},{7,31},{8,16},{9,... | collective-permute-start | bytes 110600 | tf_op jit(solution)/shard_map/ppermute | solution.py:229
  6.9 0.6 %collective-permute-start = (bf16[144,128]{1,0:T(8,128)(2,1)S(1)}, bf16[144,128]{1,0:T(8,128)(2,1)S(1)}, u32[]{:S(2)}, u32[]{:S(2)}) collective-permute-start(bf16[144,128]{1,0:T(8,128)(2,1)S(1)} %shard_map.77), channel_id=1, source_target_pairs={{0,8},{1,9},{2,10},{3,11},{4,12},{5,13},{6,14},{7,15},{8,0},{9,1},... | collective-permute-start | bytes 110600 | tf_op jit(solution)/shard_map/ppermute | solution.py:229
  7.6 0.7 %xor_multiply_fusion = s32[16]{0:T(128)S(1)} fusion(s32[16]{0:T(128)} %constant.91.clone, s32[]{:T(128)S(6)} %add.144), kind=kLoop, calls=%fused_computation.50 | loop fusion | flops 32 | bytes 132 | tf_op jit(solution)/shard_map/mul | solution.py:266
  8.9 2.9 %collective-permute-done.1 = bf16[144,128]{1,0:T(8,128)(2,1)S(1)} collective-permute-done((bf16[144,128]{1,0:T(8,128)(2,1)S(1)}, bf16[144,128]{1,0:T(8,128)(2,1)S(1)}, u32[]{:S(2)}, u32[]{:S(2)}) %collective-permute-start.1) | collective-permute-done | bytes 36896 | tf_op jit(solution)/shard_map/ppermute | solution.py:229
  11.8 1.6 %collective-permute-start.5 = (bf16[576,128]{1,0:T(8,128)(2,1)S(1)}, bf16[576,128]{1,0:T(8,128)(2,1)S(1)}, u32[]{:S(2)}, u32[]{:S(2)}) collective-permute-start(bf16[576,128]{1,0:T(8,128)(2,1)S(1)} %pad_maximum_fusion.refs_0_), channel_id=1, source_target_pairs={{0,4},{1,5},{2,6},{3,7},{4,0},{5,1},{6,2},{7,3},{8,12},{9,13},{10,... | collective-permute-start | bytes 442376 | tf_op jit(solution)/shard_map/ppermute | solution.py:229
  13.4 1.5 %collective-permute-start.4 = (bf16[576,128]{1,0:T(8,128)(2,1)S(1)}, bf16[576,128]{1,0:T(8,128)(2,1)S(1)}, u32[]{:S(2)}, u32[]{:S(2)}) collective-permute-start(bf16[576,128]{1,0:T(8,128)(2,1)S(1)} %pad_maximum_fusion.refs_0_), channel_id=1, source_target_pairs={{0,2},{1,3},{2,0},{3,1},{4,6},{5,7},{6,4},{7,5},{8,10},{9,11},{10,... | collective-permute-start | bytes 442376 | tf_op jit(solution)/shard_map/ppermute | solution.py:229
  15.4 1.9 %fusion = f32[8,128]{0,1:T(8,128)S(1)} fusion(bf16[128,8,512]{2,1,0:T(8,128)(2,1)} %param.9, bf16[128,8,512]{2,1,0:T(8,128)(2,1)} %param.8), kind=kLoop, calls=%fused_computation.1 | loop fusion | flops 2096128 | bytes 2101248
  18.7 0.9 %shard_map.78 = (f32[256,1024]{1,0:T(8,128)S(1)}, f32[256,1024]{1,0:T(8,128)S(1)}, f32[1,1024]{1,0:T(1,128)S(1)}, f32[1,1024]{1,0:T(1,128)S(1)}) custom-call(bf16[8,576,128]{2,1,0:T(8,128)(2,1)S(1)} %bitcast.17, bf16[8,128,512]{2,1,0:T(8,128)(2,1)S(1)} %bitcast.12, f32[8,1,128]{2,1,0:T(1,128)S(1)} %bitcast.22, s32[256,128]{1,0:T(8,128)S(1)} %broadcast_in_dim.36.kpos_ref, ...), custom_call_target="tpu_custom_call" | custom-call | flops 570425344 | bytes 4194304 | tf_op jit(solution)/shard_map/pallas_call | solution.py:192
  19.6 1.6 %collective-permute-done.4.refs_1_.refs_2_ = bf16[576,128]{1,0:T(8,128)(2,1)S(1)} collective-permute-done((bf16[576,128]{1,0:T(8,128)(2,1)S(1)}, bf16[576,128]{1,0:T(8,128)(2,1)S(1)}, u32[]{:S(2)}, u32[]{:S(2)}) %collective-permute-start.4) | collective-permute-done | bytes 147488 | tf_op jit(solution)/shard_map/ppermute | solution.py:229
  21.8 1.3 %shard_map.79 = (f32[384,1024]{1,0:T(8,128)S(1)}, f32[384,1024]{1,0:T(8,128)S(1)}, f32[1,1024]{1,0:T(1,128)S(1)}, f32[1,1024]{1,0:T(1,128)S(1)}) custom-call(bf16[8,576,128]{2,1,0:T(8,128)(2,1)S(1)} %bitcast.18, bf16[8,128,512]{2,1,0:T(8,128)(2,1)S(1)} %bitcast.13, f32[8,1,128]{2,1,0:T(1,128)S(1)} %bitcast.23, s32[384,128]{1,0:T(8,128)S(1)} %broadcast_in_dim.37.kpos_ref, ...), custom_call_target="tpu_custom_call" | custom-call | flops 855638016 | bytes 4194304 | tf_op jit(solution)/shard_map/pallas_call | solution.py:192
  23.1 2.9 %shard_map.80 = (bf16[1024,1024]{1,0:T(8,128)(2,1)S(1)}, bf16[1024,1024]{1,0:T(8,128)(2,1)S(1)}, bf16[1152,128]{1,0:T(8,128)(2,1)S(1)}) custom-call(bf16[8,576,128]{2,1,0:T(8,128)(2,1)S(1)} %bitcast.19, bf16[8,128,512]{2,1,0:T(8,128)(2,1)S(1)} %bitcast.14, f32[8,1,128]{2,1,0:T(1,128)S(1)} %bitcast.24, s32[384,128]{1,0:T(8,128)S(1)} %broadcast_in_dim.38.kpos_ref, ...), custom_call_target="tpu_custom_call" | custom-call | flops 1711276032 | bytes 4194304 | tf_op jit(solution)/shard_map/pallas_call | solution.py:192
  26.6 1.6 %shard_map.81 = (f32[1152,128]{1,0:T(8,128)S(1)}, bf16[1152,128]{1,0:T(8,128)(2,1)S(1)}) custom-call(bf16[8,576,128]{2,1,0:T(8,128)(2,1)S(1)} %bitcast.20, bf16[8,128,512]{2,1,0:T(8,128)(2,1)S(1)} %bitcast.15, bf16[1024,1024]{1,0:T(8,128)(2,1)S(1)} %get-tuple-element.53.p_ref, bf16[1024,1024]{1,0:T(8,128)(2,1)S(1)} %get-tuple-element.54.ds_ref), custom_call_target="tpu_custom_call" | custom-call | flops 1140850688 | bytes 4194304 | tf_op jit(solution)/shard_map/pallas_call | solution.py:192
  28.3 1.1 %collective-permute-start.11 = (bf16[576,128]{1,0:T(8,128)(2,1)S(1)}, bf16[576,128]{1,0:T(8,128)(2,1)S(1)}, u32[]{:S(2)}, u32[]{:S(2)}) collective-permute-start(bf16[576,128]{1,0:T(8,128)(2,1)S(1)} %slice.96), channel_id=1, source_target_pairs={{0,6},{1,7},{2,4},{3,5},{4,2},{5,3},{6,0},{7,1},{8,14},{9,15},{10,... | collective-permute-start | bytes 442376 | tf_op jit(solution)/shard_map/ppermute | solution.py:229
  29.4 0.9 %shard_map.82 = f32[1152,128]{1,0:T(8,128)S(1)} custom-call(bf16[8,576,128]{2,1,0:T(8,128)(2,1)S(1)} %bitcast.21, bf16[8,128,512]{2,1,0:T(8,128)(2,1)S(1)} %bitcast.16, bf16[1024,1024]{1,0:T(8,128)(2,1)S(1)} %get-tuple-element.53.p_ref, bf16[1024,1024]{1,0:T(8,128)(2,1)S(1)} %get-tuple-element.54.ds_ref, f32[1,1024]{1,0:T(1,128)S(1)} %get-tuple-element.58.refs_5_.after_ref), custom_call_target="tpu_custom_call" | custom-call | flops 570425344 | bytes 4194304 | tf_op jit(solution)/shard_map/pallas_call | solution.py:192
  30.4 0.9 %collective-permute-start.13 = (bf16[576,128]{1,0:T(8,128)(2,1)S(1)}, bf16[576,128]{1,0:T(8,128)(2,1)S(1)}, u32[]{:S(2)}, u32[]{:S(2)}) collective-permute-start(bf16[576,128]{1,0:T(8,128)(2,1)S(1)} %get-tuple-element.64), channel_id=1, source_target_pairs={{0,2},{1,3},{2,0},{3,1},{4,6},{5,7},{6,4},{7,5},{8,10},{9,11},{10,... | collective-permute-start | bytes 442376 | tf_op jit(solution)/shard_map/ppermute | solution.py:229
  31.3 1.6 %collective-permute-start.14 = (bf16[576,128]{1,0:T(8,128)(2,1)S(1)}, bf16[576,128]{1,0:T(8,128)(2,1)S(1)}, u32[]{:S(2)}, u32[]{:S(2)}) collective-permute-start(bf16[576,128]{1,0:T(8,128)(2,1)S(1)} %get-tuple-element.65), channel_id=1, source_target_pairs={{0,4},{1,5},{2,6},{3,7},{4,0},{5,1},{6,2},{7,3},{8,12},{9,13},{10,... | collective-permute-start | bytes 442376 | tf_op jit(solution)/shard_map/ppermute | solution.py:229
  32.9 2.4 %shard_map.83 = bf16[8,576,128]{2,1,0:T(8,128)(2,1)} custom-call(bf16[1024,1024]{1,0:T(8,128)(2,1)S(1)} %get-tuple-element.54.ds_ref, bf16[576,128]{1,0:T(8,128)(2,1)S(1)} %pad_maximum_fusion.refs_0_, bf16[576,128]{1,0:T(8,128)(2,1)S(1)} %collective-permute-done.3.refs_0_.refs_1_, bf16[576,128]{1,0:T(8,128)(2,1)S(1)} %collective-permute-done.4.refs_1_.refs_2_, ...), custom_call_target="tpu_custom_call" | custom-call | flops 1207959552 | bytes 4194304 | tf_op jit(solution)/shard_map/pallas_call | solution.py:192
  36.0 2.7 %collective-permute-done.13 = bf16[576,128]{1,0:T(8,128)(2,1)S(1)} collective-permute-done((bf16[576,128]{1,0:T(8,128)(2,1)S(1)}, bf16[576,128]{1,0:T(8,128)(2,1)S(1)}, u32[]{:S(2)}, u32[]{:S(2)}) %collective-permute-start.13) | collective-permute-done | bytes 147488 | tf_op jit(solution)/shard_map/ppermute | solution.py:229
  38.8 1.8 %collective-permute-start.15 = (bf16[144,128]{1,0:T(8,128)(2,1)S(1)}, bf16[144,128]{1,0:T(8,128)(2,1)S(1)}, u32[]{:S(2)}, u32[]{:S(2)}) collective-permute-start(bf16[144,128]{1,0:T(8,128)(2,1)S(1)} %get-tuple-element.66), channel_id=1, source_target_pairs={{0,24},{1,25},{2,26},{3,27},{4,28},{5,29},{6,30},{7,31},{8,16},{9,... | collective-permute-start | bytes 110600 | tf_op jit(solution)/shard_map/ppermute | solution.py:229
  41.0 2.3 %collective-permute-start.16 = (bf16[144,128]{1,0:T(8,128)(2,1)S(1)}, bf16[144,128]{1,0:T(8,128)(2,1)S(1)}, u32[]{:S(2)}, u32[]{:S(2)}) collective-permute-start(bf16[144,128]{1,0:T(8,128)(2,1)S(1)} %get-tuple-element.68), channel_id=1, source_target_pairs={{0,8},{1,9},{2,10},{3,11},{4,12},{5,13},{6,14},{7,15},{8,0},{9,1},... | collective-permute-start | bytes 110600 | tf_op jit(solution)/shard_map/ppermute | solution.py:229
  43.2 1.8 %collective-permute-done.15 = bf16[144,128]{1,0:T(8,128)(2,1)S(1)} collective-permute-done((bf16[144,128]{1,0:T(8,128)(2,1)S(1)}, bf16[144,128]{1,0:T(8,128)(2,1)S(1)}, u32[]{:S(2)}, u32[]{:S(2)}) %collective-permute-start.15) | collective-permute-done | bytes 36896 | tf_op jit(solution)/shard_map/ppermute | solution.py:229
  45.0 0.8 %collective-permute-done.17 = bf16[144,128]{1,0:T(8,128)(2,1)S(1)} collective-permute-done((bf16[144,128]{1,0:T(8,128)(2,1)S(1)}, bf16[144,128]{1,0:T(8,128)(2,1)S(1)}, u32[]{:S(2)}, u32[]{:S(2)}) %collective-permute-start.17) | collective-permute-done | bytes 36896 | tf_op jit(solution)/shard_map/ppermute | solution.py:229
  46.0 0.6 %copy-done.3 = f32[32,576]{1,0:T(8,128)} copy-done((f32[32,576]{1,0:T(8,128)}, f32[32,576]{1,0:T(8,128)S(1)}, u32[]{:S(2)}) %copy-start.3) | copy-done | bytes 73752
  (66 shorter events, 5.3 us)
Async XLA Ops:
  0.6 0.9 %copy-start = (bf16[128,576]{0,1:T(8,128)(2,1)S(1)}, bf16[128,576]{0,1:T(8,128)(2,1)}, u32[]{:S(2)}) copy-start(bf16[128,576]{0,1:T(8,128)(2,1)} %param.7) | copy-start | bytes 442372
  0.6 16.7 %copy-start.4 = (s32[16]{0:T(128)S(1)}, s32[16]{0:T(128)}, u32[]{:S(2)}) copy-start(s32[16]{0:T(128)} %param.10) | copy-start | bytes 196
  0.7 17.0 %copy-start.2 = (bf16[128,8,512]{2,1,0:T(8,128)(2,1)S(1)}, bf16[128,8,512]{2,1,0:T(8,128)(2,1)}, u32[]{:S(2)}) copy-start(bf16[128,8,512]{2,1,0:T(8,128)(2,1)} %param.8) | copy-start | bytes 3145732
  1.9 7.0 %collective-permute-start.2 = (bf16[144,128]{1,0:T(8,128)(2,1)S(1)}, bf16[144,128]{1,0:T(8,128)(2,1)S(1)}, u32[]{:S(2)}, u32[]{:S(2)}) collective-permute-start(bf16[144,128]{1,0:T(8,128)(2,1)S(1)} %shard_map.77), channel_id=1, source_target_pairs={{0,24},{1,25},{2,26},{3,27},{4,28},{5,29},{6,30},{7,31},{8,16},{9,... | collective-permute-start | bytes 110600 | tf_op jit(solution)/shard_map/ppermute | solution.py:229
  6.9 4.9 %collective-permute-start.1 = (bf16[144,128]{1,0:T(8,128)(2,1)S(1)}, bf16[144,128]{1,0:T(8,128)(2,1)S(1)}, u32[]{:S(2)}, u32[]{:S(2)}) collective-permute-start(bf16[144,128]{1,0:T(8,128)(2,1)S(1)} %shard_map.77), channel_id=1, source_target_pairs={{0,16},{1,17},{2,18},{3,19},{4,20},{5,21},{6,22},{7,23},{8,24},{9,... | collective-permute-start | bytes 110600 | tf_op jit(solution)/shard_map/ppermute | solution.py:229
  6.9 4.9 %collective-permute-start = (bf16[144,128]{1,0:T(8,128)(2,1)S(1)}, bf16[144,128]{1,0:T(8,128)(2,1)S(1)}, u32[]{:S(2)}, u32[]{:S(2)}) collective-permute-start(bf16[144,128]{1,0:T(8,128)(2,1)S(1)} %shard_map.77), channel_id=1, source_target_pairs={{0,8},{1,9},{2,10},{3,11},{4,12},{5,13},{6,14},{7,15},{8,0},{9,1},... | collective-permute-start | bytes 110600 | tf_op jit(solution)/shard_map/ppermute | solution.py:229
  11.8 6.9 %copy-start.1 = (bf16[128,8,576]{0,2,1:T(8,128)(2,1)S(1)}, bf16[128,8,576]{0,2,1:T(8,128)(2,1)}, u32[]{:S(2)}) copy-start(bf16[128,8,576]{0,2,1:T(8,128)(2,1)} %param.6) | copy-start | bytes 3538948
  11.8 7.8 %collective-permute-start.5 = (bf16[576,128]{1,0:T(8,128)(2,1)S(1)}, bf16[576,128]{1,0:T(8,128)(2,1)S(1)}, u32[]{:S(2)}, u32[]{:S(2)}) collective-permute-start(bf16[576,128]{1,0:T(8,128)(2,1)S(1)} %pad_maximum_fusion.refs_0_), channel_id=1, source_target_pairs={{0,4},{1,5},{2,6},{3,7},{4,0},{5,1},{6,2},{7,3},{8,12},{9,13},{10,... | collective-permute-start | bytes 442376 | tf_op jit(solution)/shard_map/ppermute | solution.py:229
  13.4 7.9 %collective-permute-start.4 = (bf16[576,128]{1,0:T(8,128)(2,1)S(1)}, bf16[576,128]{1,0:T(8,128)(2,1)S(1)}, u32[]{:S(2)}, u32[]{:S(2)}) collective-permute-start(bf16[576,128]{1,0:T(8,128)(2,1)S(1)} %pad_maximum_fusion.refs_0_), channel_id=1, source_target_pairs={{0,2},{1,3},{2,0},{3,1},{4,6},{5,7},{6,4},{7,5},{8,10},{9,11},{10,... | collective-permute-start | bytes 442376 | tf_op jit(solution)/shard_map/ppermute | solution.py:229
  14.9 6.3 %collective-permute-start.3 = (bf16[576,128]{1,0:T(8,128)(2,1)S(1)}, bf16[576,128]{1,0:T(8,128)(2,1)S(1)}, u32[]{:S(2)}, u32[]{:S(2)}) collective-permute-start(bf16[576,128]{1,0:T(8,128)(2,1)S(1)} %pad_maximum_fusion.refs_0_), channel_id=1, source_target_pairs={{0,6},{1,7},{2,4},{3,5},{4,2},{5,3},{6,0},{7,1},{8,14},{9,15},{10,... | collective-permute-start | bytes 442376 | tf_op jit(solution)/shard_map/ppermute | solution.py:229
  17.3 1.4 %collective-permute-start.6 = (bf16[576,128]{1,0:T(8,128)(2,1)S(1)}, bf16[576,128]{1,0:T(8,128)(2,1)S(1)}, u32[]{:S(2)}, u32[]{:S(2)}) collective-permute-start(bf16[576,128]{1,0:T(8,128)(2,1)S(1)} %pad_maximum_fusion.refs_0_), channel_id=1, source_target_pairs={{0,1},{1,0},{2,3},{3,2},{4,5},{5,4},{6,7},{7,6},{8,9},{9,8},{10,11... | collective-permute-start | bytes 442376 | tf_op jit(solution)/shard_map/ppermute | solution.py:229
  21.2 1.8 %collective-permute-start.7 = (bf16[576,128]{1,0:T(8,128)(2,1)S(1)}, bf16[576,128]{1,0:T(8,128)(2,1)S(1)}, u32[]{:S(2)}, u32[]{:S(2)}) collective-permute-start(bf16[576,128]{1,0:T(8,128)(2,1)S(1)} %collective-permute-done.3.refs_0_.refs_1_), channel_id=1, source_target_pairs={{0,1},{1,0},{2,3},{3,2},{4,5},{5,4},{6,7},{7,6},{8,9},{9,8},{10,11... | collective-permute-start | bytes 442376 | tf_op jit(solution)/shard_map/ppermute | solution.py:229
  21.2 1.8 %collective-permute-start.8 = (bf16[576,128]{1,0:T(8,128)(2,1)S(1)}, bf16[576,128]{1,0:T(8,128)(2,1)S(1)}, u32[]{:S(2)}, u32[]{:S(2)}) collective-permute-start(bf16[576,128]{1,0:T(8,128)(2,1)S(1)} %collective-permute-done.4.refs_1_.refs_2_), channel_id=1, source_target_pairs={{0,1},{1,0},{2,3},{3,2},{4,5},{5,4},{6,7},{7,6},{8,9},{9,8},{10,11... | collective-permute-start | bytes 442376 | tf_op jit(solution)/shard_map/ppermute | solution.py:229
  21.7 1.4 %collective-permute-start.9 = (bf16[576,128]{1,0:T(8,128)(2,1)S(1)}, bf16[576,128]{1,0:T(8,128)(2,1)S(1)}, u32[]{:S(2)}, u32[]{:S(2)}) collective-permute-start(bf16[576,128]{1,0:T(8,128)(2,1)S(1)} %collective-permute-done.5.refs_2_.refs_3_), channel_id=1, source_target_pairs={{0,1},{1,0},{2,3},{3,2},{4,5},{5,4},{6,7},{7,6},{8,9},{9,8},{10,11... | collective-permute-start | bytes 442376 | tf_op jit(solution)/shard_map/ppermute | solution.py:229
  26.0 2.2 %collective-permute-start.10 = (bf16[1152,128]{1,0:T(8,128)(2,1)S(1)}, bf16[1152,128]{1,0:T(8,128)(2,1)S(1)}, u32[]{:S(2)}, u32[]{:S(2)}) collective-permute-start(bf16[1152,128]{1,0:T(8,128)(2,1)S(1)} %get-tuple-element.56), channel_id=1, source_target_pairs={{0,1},{1,0},{2,3},{3,2},{4,5},{5,4},{6,7},{7,6},{8,9},{9,8},{10,11... | collective-permute-start | bytes 884744 | tf_op jit(solution)/shard_map/ppermute | solution.py:229
  28.1 2.2 %collective-permute-start.12 = (bf16[1152,128]{1,0:T(8,128)(2,1)S(1)}, bf16[1152,128]{1,0:T(8,128)(2,1)S(1)}, u32[]{:S(2)}, u32[]{:S(2)}) collective-permute-start(bf16[1152,128]{1,0:T(8,128)(2,1)S(1)} %get-tuple-element.59), channel_id=1, source_target_pairs={{0,1},{1,0},{2,3},{3,2},{4,5},{5,4},{6,7},{7,6},{8,9},{9,8},{10,11... | collective-permute-start | bytes 884744 | tf_op jit(solution)/shard_map/ppermute | solution.py:229
  28.3 7.7 %collective-permute-start.11 = (bf16[576,128]{1,0:T(8,128)(2,1)S(1)}, bf16[576,128]{1,0:T(8,128)(2,1)S(1)}, u32[]{:S(2)}, u32[]{:S(2)}) collective-permute-start(bf16[576,128]{1,0:T(8,128)(2,1)S(1)} %slice.96), channel_id=1, source_target_pairs={{0,6},{1,7},{2,4},{3,5},{4,2},{5,3},{6,0},{7,1},{8,14},{9,15},{10,... | collective-permute-start | bytes 442376 | tf_op jit(solution)/shard_map/ppermute | solution.py:229
  30.4 8.3 %collective-permute-start.13 = (bf16[576,128]{1,0:T(8,128)(2,1)S(1)}, bf16[576,128]{1,0:T(8,128)(2,1)S(1)}, u32[]{:S(2)}, u32[]{:S(2)}) collective-permute-start(bf16[576,128]{1,0:T(8,128)(2,1)S(1)} %get-tuple-element.64), channel_id=1, source_target_pairs={{0,2},{1,3},{2,0},{3,1},{4,6},{5,7},{6,4},{7,5},{8,10},{9,11},{10,... | collective-permute-start | bytes 442376 | tf_op jit(solution)/shard_map/ppermute | solution.py:229
  31.3 7.4 %collective-permute-start.14 = (bf16[576,128]{1,0:T(8,128)(2,1)S(1)}, bf16[576,128]{1,0:T(8,128)(2,1)S(1)}, u32[]{:S(2)}, u32[]{:S(2)}) collective-permute-start(bf16[576,128]{1,0:T(8,128)(2,1)S(1)} %get-tuple-element.65), channel_id=1, source_target_pairs={{0,4},{1,5},{2,6},{3,7},{4,0},{5,1},{6,2},{7,3},{8,12},{9,13},{10,... | collective-permute-start | bytes 442376 | tf_op jit(solution)/shard_map/ppermute | solution.py:229
  38.8 6.2 %collective-permute-start.15 = (bf16[144,128]{1,0:T(8,128)(2,1)S(1)}, bf16[144,128]{1,0:T(8,128)(2,1)S(1)}, u32[]{:S(2)}, u32[]{:S(2)}) collective-permute-start(bf16[144,128]{1,0:T(8,128)(2,1)S(1)} %get-tuple-element.66), channel_id=1, source_target_pairs={{0,24},{1,25},{2,26},{3,27},{4,28},{5,29},{6,30},{7,31},{8,16},{9,... | collective-permute-start | bytes 110600 | tf_op jit(solution)/shard_map/ppermute | solution.py:229
  40.6 5.3 %collective-permute-start.17 = (bf16[144,128]{1,0:T(8,128)(2,1)S(1)}, bf16[144,128]{1,0:T(8,128)(2,1)S(1)}, u32[]{:S(2)}, u32[]{:S(2)}) collective-permute-start(bf16[144,128]{1,0:T(8,128)(2,1)S(1)} %get-tuple-element.67), channel_id=1, source_target_pairs={{0,16},{1,17},{2,18},{3,19},{4,20},{5,21},{6,22},{7,23},{8,24},{9,... | collective-permute-start | bytes 110600 | tf_op jit(solution)/shard_map/ppermute | solution.py:229
  41.0 4.9 %collective-permute-start.16 = (bf16[144,128]{1,0:T(8,128)(2,1)S(1)}, bf16[144,128]{1,0:T(8,128)(2,1)S(1)}, u32[]{:S(2)}, u32[]{:S(2)}) collective-permute-start(bf16[144,128]{1,0:T(8,128)(2,1)S(1)} %get-tuple-element.68), channel_id=1, source_target_pairs={{0,8},{1,9},{2,10},{3,11},{4,12},{5,13},{6,14},{7,15},{8,0},{9,1},... | collective-permute-start | bytes 110600 | tf_op jit(solution)/shard_map/ppermute | solution.py:229
  46.0 0.6 %copy-start.3 = (f32[32,576]{1,0:T(8,128)}, f32[32,576]{1,0:T(8,128)S(1)}, u32[]{:S(2)}) copy-start(f32[32,576]{1,0:T(8,128)S(1)} %maximum_dynamic-update-slice_fusion) | copy-start | bytes 221188

commit v6 on v5

--- a/solution.py
+++ b/solution.py
@@ -96,12 +96,12 @@
 GROUP = 4
 
 
-def group_terms(qt_ref, og_ref, keys, kpos_ref, qpos_ref, g):
+def group_terms(qt_ref, og_ref, keys, kpos, qpos_ref, g):
     tokens = qt_ref.shape[2]
     width = og_ref.shape[2]
     qt = side_by_side([qt_ref[h] for h in range(g, g + GROUP)])
     scores = dot(keys, qt, 1, 0)
-    allowed = side_by_side([kpos_ref[...]] * GROUP) <= side_by_side([qpos_ref[...]] * GROUP)
+    allowed = side_by_side([kpos] * GROUP) <= side_by_side([qpos_ref[...]] * GROUP)
     scores = jnp.where(allowed, scores * (QK_HEAD**-0.5 * LOG2_E), LARGE_NEGATIVE)
     out_grad = og_ref[g : g + GROUP].reshape(GROUP * tokens, width)
     return scores, dot(keys[:, :width], out_grad, 1, 1)
@@ -111,13 +111,14 @@
     out_ref[...] = packed(rows_ref[...])
 
 
-def partial_kernel(piece, qt_ref, og_ref, rd_ref, kpos_ref, qpos_ref, *refs):
+def partial_kernel(spans, piece, qt_ref, og_ref, rd_ref, kpos_ref, qpos_ref, *refs):
     *piece_refs, mass_ref, vg_ref, peak_ref, sum_ref = refs
     heads, _, tokens = qt_ref.shape
     keys = key_rows(piece_refs, piece, qt_ref.shape[1])
+    kpos = jnp.concatenate([kpos_ref[span, :] for span in spans])
     for g in range(0, heads, GROUP):
         cols = slice(g * tokens, (g + GROUP) * tokens)
-        scores, value_grads = group_terms(qt_ref, og_ref, keys, kpos_ref, qpos_ref, g)
+        scores, value_grads = group_terms(qt_ref, og_ref, keys, kpos, qpos_ref, g)
         row_dots = side_by_side([rd_ref[h] for h in range(g, g + GROUP)])
         vg_ref[:, cols] = (value_grads - row_dots) * QK_HEAD**-0.5
         peak = jnp.max(scores, axis=0, keepdims=True)
@@ -136,9 +137,10 @@
     own = mass0.shape[0] // 2
     scale = QK_HEAD**-0.5
     keys = key_rows(piece_refs, piece, qt_ref.shape[1])
+    kpos = kpos_ref[half + own :, :]
     for g in range(0, heads, GROUP):
         cols = slice(g * tokens, (g + GROUP) * tokens)
-        scores, grads = group_terms(qt_ref, og_ref, keys, kpos_ref, qpos_ref, g)
+        scores, grads = group_terms(qt_ref, og_ref, keys, kpos, qpos_ref, g)
         last = jnp.max(scores, axis=0, keepdims=True)
         peak = jnp.maximum(jnp.maximum(peak0[:, cols], peak1[:, cols]), last)
         mass = jnp.exp2(scores - peak)
@@ -275,10 +277,12 @@
     def in_lanes(pos):
         return jnp.broadcast_to(pos[:, None], (pos.shape[0], LANES))
 
-    def partial_terms(pos, pieces):
-        count = pos.shape[0]
+    key_pos = in_lanes(jnp.concatenate([near_pos, far_pos]))
+
+    def partial_terms(spans, pieces):
+        count = sum(span.stop - span.start for span in spans)
         return call(
-            kernel(partial_kernel),
+            kernel(functools.partial(partial_kernel, spans)),
             [
                 pltpu.VMEM((count, rows), f32),
                 pltpu.VMEM((count, rows), f32),
@@ -286,20 +290,13 @@
                 pltpu.VMEM((1, rows), f32),
             ],
             2 * count * rows * (kv_width + width),
-            [qt, og, row_dots, pos, query_pos, *pieces],
+            [qt, og, row_dots, key_pos, query_pos, *pieces],
         )
 
-    own_lanes, near_lanes, far_lanes = lax.optimization_barrier(
-        (
-            in_lanes(jnp.concatenate([near_pos[:owned], far_pos[:owned]])),
-            in_lanes(near_pos[owned:]),
-            in_lanes(far_pos[owned:]),
-        )
-    )
-    terms0 = partial_terms(own_lanes, [own, own_far])
+    terms0 = partial_terms([slice(0, owned), slice(half, half + owned)], [own, own_far])
     near, terms0[2] = lax.optimization_barrier((near, terms0[2]))
     far = [exchange(p, 1) for p in near]
-    terms1 = partial_terms(near_lanes, near)
+    terms1 = partial_terms([slice(owned, half)], near)
     weights, score_grads, far_a = call(
         kernel(probs_kernel),
         [
@@ -308,7 +305,7 @@
             jax.ShapeDtypeStruct((high(half // 2), columns), bf16),
         ],
         3 * pair_macs,
-        [qt, og, row_dots, far_lanes, query_pos, *far, *terms0, *terms1],
+        [qt, og, row_dots, key_pos, query_pos, *far, *terms0, *terms1],
     )
     arrived = exchange(far_a, 1)
     near_a, far_b = call(

time: 46.8 us -> 46.7 us (level)
  transfers between devices with their start and end apart: 18 -> 18, of which waited for: 8 -> 9; matrix products, arithmetic and copies ran while one was open for 8% -> 8% of each run, Pallas kernels for 15% -> 15%
where the time goes in v6:
time: 46.7 us; the launch traced here: 46.6 us
  starting transfers between devices  18.5 us (40%)
  waiting for transfers between devices  11.6 us (25%)
  Pallas kernels  9.93 us (21%)
  other arithmetic  3.09 us (7%)
  local copies, waits for them, and re-layouts  2.52 us (5%)
  between operations  0.92 us (2%)
    ppermute x18, starting transfers between devices, exchange(): lax.ppermute(value, ('ctx', 'head'), [(i, i ^ mask) for i in range(device...  18.5 us
    ppermute x18, waiting for transfers between devices, exchange(): lax.ppermute(value, ('ctx', 'head'), [(i, i ^ mask) for i in range(device...  11.6 us
    pallas_call x7, Pallas kernels, call(): pl.pallas_call(kernel, in_specs=[VMEM] * len(operands), out_specs=[VMEM]...  9.93 us
    unnamed x1, other arithmetic  1.89 us
    unnamed x15, local copies, waits for them, and re-layouts  1.66 us
  transfers between devices with their start and end apart: 18, of which 9 were waited for; matrix products, arithmetic and copies ran while one was open for 8% of the time, Pallas kernels for 15%

profile of v6, /device:TPU:0, one launch (start us, length us, event | category | flops | bytes accessed | tf_op | source)
XLA Modules:
  0.0 46.6 jit_solution(15387467434225759466)
XLA Ops:
  0.7 0.9 %copy-done = bf16[128,576]{0,1:T(8,128)(2,1)S(1)} copy-done((bf16[128,576]{0,1:T(8,128)(2,1)S(1)}, bf16[128,576]{0,1:T(8,128)(2,1)}, u32[]{:S(2)}) %copy-start) | copy-done | bytes 147480
  1.9 5.1 %collective-permute-start.2 = (bf16[144,128]{1,0:T(8,128)(2,1)S(1)}, bf16[144,128]{1,0:T(8,128)(2,1)S(1)}, u32[]{:S(2)}, u32[]{:S(2)}) collective-permute-start(bf16[144,128]{1,0:T(8,128)(2,1)S(1)} %shard_map.77), channel_id=1, source_target_pairs={{0,24},{1,25},{2,26},{3,27},{4,28},{5,29},{6,30},{7,31},{8,16},{9,... | collective-permute-start | bytes 110600 | tf_op jit(solution)/shard_map/ppermute | solution.py:231
  6.9 0.6 %collective-permute-start = (bf16[144,128]{1,0:T(8,128)(2,1)S(1)}, bf16[144,128]{1,0:T(8,128)(2,1)S(1)}, u32[]{:S(2)}, u32[]{:S(2)}) collective-permute-start(bf16[144,128]{1,0:T(8,128)(2,1)S(1)} %shard_map.77), channel_id=1, source_target_pairs={{0,8},{1,9},{2,10},{3,11},{4,12},{5,13},{6,14},{7,15},{8,0},{9,1},... | collective-permute-start | bytes 110600 | tf_op jit(solution)/shard_map/ppermute | solution.py:231
  7.6 0.7 %xor_multiply_fusion = s32[16]{0:T(128)S(1)} fusion(s32[16]{0:T(128)} %constant.91.clone, s32[]{:T(128)S(6)} %add.144), kind=kLoop, calls=%fused_computation.50 | loop fusion | flops 32 | bytes 132 | tf_op jit(solution)/shard_map/mul | solution.py:268
  8.9 2.9 %collective-permute-done.1 = bf16[144,128]{1,0:T(8,128)(2,1)S(1)} collective-permute-done((bf16[144,128]{1,0:T(8,128)(2,1)S(1)}, bf16[144,128]{1,0:T(8,128)(2,1)S(1)}, u32[]{:S(2)}, u32[]{:S(2)}) %collective-permute-start.1) | collective-permute-done | bytes 36896 | tf_op jit(solution)/shard_map/ppermute | solution.py:231
  11.8 1.6 %collective-permute-start.5 = (bf16[576,128]{1,0:T(8,128)(2,1)S(1)}, bf16[576,128]{1,0:T(8,128)(2,1)S(1)}, u32[]{:S(2)}, u32[]{:S(2)}) collective-permute-start(bf16[576,128]{1,0:T(8,128)(2,1)S(1)} %pad_maximum_fusion.refs_0_), channel_id=1, source_target_pairs={{0,4},{1,5},{2,6},{3,7},{4,0},{5,1},{6,2},{7,3},{8,12},{9,13},{10,... | collective-permute-start | bytes 442376 | tf_op jit(solution)/shard_map/ppermute | solution.py:231
  13.4 1.5 %collective-permute-start.4 = (bf16[576,128]{1,0:T(8,128)(2,1)S(1)}, bf16[576,128]{1,0:T(8,128)(2,1)S(1)}, u32[]{:S(2)}, u32[]{:S(2)}) collective-permute-start(bf16[576,128]{1,0:T(8,128)(2,1)S(1)} %pad_maximum_fusion.refs_0_), channel_id=1, source_target_pairs={{0,2},{1,3},{2,0},{3,1},{4,6},{5,7},{6,4},{7,5},{8,10},{9,11},{10,... | collective-permute-start | bytes 442376 | tf_op jit(solution)/shard_map/ppermute | solution.py:231
  15.4 1.9 %fusion = f32[8,128]{0,1:T(8,128)S(1)} fusion(bf16[128,8,512]{2,1,0:T(8,128)(2,1)} %param.9, bf16[128,8,512]{2,1,0:T(8,128)(2,1)} %param.8), kind=kLoop, calls=%fused_computation.1 | loop fusion | flops 2096128 | bytes 2101248
  17.9 0.8 %collective-permute-done.6.refs_1_.refs_4_ = bf16[576,128]{1,0:T(8,128)(2,1)S(1)} collective-permute-done((bf16[576,128]{1,0:T(8,128)(2,1)S(1)}, bf16[576,128]{1,0:T(8,128)(2,1)S(1)}, u32[]{:S(2)}, u32[]{:S(2)}) %collective-permute-start.6) | collective-permute-done | bytes 147488 | tf_op jit(solution)/shard_map/ppermute | solution.py:231
  18.9 0.9 %shard_map.78 = (f32[256,1024]{1,0:T(8,128)S(1)}, f32[256,1024]{1,0:T(8,128)S(1)}, f32[1,1024]{1,0:T(1,128)S(1)}, f32[1,1024]{1,0:T(1,128)S(1)}) custom-call(bf16[8,576,128]{2,1,0:T(8,128)(2,1)S(1)} %bitcast.17, bf16[8,128,512]{2,1,0:T(8,128)(2,1)S(1)} %bitcast.12, f32[8,1,128]{2,1,0:T(1,128)S(1)} %bitcast.22, s32[1024,128]{1,0:T(8,128)S(1)} %broadcast_in_dim.48.kpos_ref, ...), custom_call_target="tpu_custom_call" | custom-call | flops 570425344 | bytes 4194304 | tf_op jit(solution)/shard_map/pallas_call | solution.py:194
  19.8 1.4 %collective-permute-done.4.refs_1_.refs_2_ = bf16[576,128]{1,0:T(8,128)(2,1)S(1)} collective-permute-done((bf16[576,128]{1,0:T(8,128)(2,1)S(1)}, bf16[576,128]{1,0:T(8,128)(2,1)S(1)}, u32[]{:S(2)}, u32[]{:S(2)}) %collective-permute-start.4) | collective-permute-done | bytes 147488 | tf_op jit(solution)/shard_map/ppermute | solution.py:231
  21.8 1.2 %shard_map.79 = (f32[384,1024]{1,0:T(8,128)S(1)}, f32[384,1024]{1,0:T(8,128)S(1)}, f32[1,1024]{1,0:T(1,128)S(1)}, f32[1,1024]{1,0:T(1,128)S(1)}) custom-call(bf16[8,576,128]{2,1,0:T(8,128)(2,1)S(1)} %bitcast.18, bf16[8,128,512]{2,1,0:T(8,128)(2,1)S(1)} %bitcast.13, f32[8,1,128]{2,1,0:T(1,128)S(1)} %bitcast.23, s32[1024,128]{1,0:T(8,128)S(1)} %broadcast_in_dim.48.kpos_ref, ...), custom_call_target="tpu_custom_call" | custom-call | flops 855638016 | bytes 4194304 | tf_op jit(solution)/shard_map/pallas_call | solution.py:194
  23.1 2.9 %shard_map.80 = (bf16[1024,1024]{1,0:T(8,128)(2,1)S(1)}, bf16[1024,1024]{1,0:T(8,128)(2,1)S(1)}, bf16[1152,128]{1,0:T(8,128)(2,1)S(1)}) custom-call(bf16[8,576,128]{2,1,0:T(8,128)(2,1)S(1)} %bitcast.19, bf16[8,128,512]{2,1,0:T(8,128)(2,1)S(1)} %bitcast.14, f32[8,1,128]{2,1,0:T(1,128)S(1)} %bitcast.24, s32[1024,128]{1,0:T(8,128)S(1)} %broadcast_in_dim.48.kpos_ref, ...), custom_call_target="tpu_custom_call" | custom-call | flops 1711276032 | bytes 4194304 | tf_op jit(solution)/shard_map/pallas_call | solution.py:194
  26.5 1.6 %shard_map.81 = (f32[1152,128]{1,0:T(8,128)S(1)}, bf16[1152,128]{1,0:T(8,128)(2,1)S(1)}) custom-call(bf16[8,576,128]{2,1,0:T(8,128)(2,1)S(1)} %bitcast.20, bf16[8,128,512]{2,1,0:T(8,128)(2,1)S(1)} %bitcast.15, bf16[1024,1024]{1,0:T(8,128)(2,1)S(1)} %get-tuple-element.47.p_ref, bf16[1024,1024]{1,0:T(8,128)(2,1)S(1)} %get-tuple-element.48.ds_ref), custom_call_target="tpu_custom_call" | custom-call | flops 1140850688 | bytes 4194304 | tf_op jit(solution)/shard_map/pallas_call | solution.py:194
  28.3 1.2 %collective-permute-start.11 = (bf16[576,128]{1,0:T(8,128)(2,1)S(1)}, bf16[576,128]{1,0:T(8,128)(2,1)S(1)}, u32[]{:S(2)}, u32[]{:S(2)}) collective-permute-start(bf16[576,128]{1,0:T(8,128)(2,1)S(1)} %slice.80), channel_id=1, source_target_pairs={{0,6},{1,7},{2,4},{3,5},{4,2},{5,3},{6,0},{7,1},{8,14},{9,15},{10,... | collective-permute-start | bytes 442376 | tf_op jit(solution)/shard_map/ppermute | solution.py:231
  29.5 0.9 %shard_map.82 = f32[1152,128]{1,0:T(8,128)S(1)} custom-call(bf16[8,576,128]{2,1,0:T(8,128)(2,1)S(1)} %bitcast.21, bf16[8,128,512]{2,1,0:T(8,128)(2,1)S(1)} %bitcast.16, bf16[1024,1024]{1,0:T(8,128)(2,1)S(1)} %get-tuple-element.47.p_ref, bf16[1024,1024]{1,0:T(8,128)(2,1)S(1)} %get-tuple-element.48.ds_ref, f32[1,1024]{1,0:T(1,128)S(1)} %get-tuple-element.52.refs_5_.after_ref), custom_call_target="tpu_custom_call" | custom-call | flops 570425344 | bytes 4194304 | tf_op jit(solution)/shard_map/pallas_call | solution.py:194
  30.5 0.8 %collective-permute-start.13 = (bf16[576,128]{1,0:T(8,128)(2,1)S(1)}, bf16[576,128]{1,0:T(8,128)(2,1)S(1)}, u32[]{:S(2)}, u32[]{:S(2)}) collective-permute-start(bf16[576,128]{1,0:T(8,128)(2,1)S(1)} %get-tuple-element.58), channel_id=1, source_target_pairs={{0,2},{1,3},{2,0},{3,1},{4,6},{5,7},{6,4},{7,5},{8,10},{9,11},{10,... | collective-permute-start | bytes 442376 | tf_op jit(solution)/shard_map/ppermute | solution.py:231
  31.3 1.6 %collective-permute-start.14 = (bf16[576,128]{1,0:T(8,128)(2,1)S(1)}, bf16[576,128]{1,0:T(8,128)(2,1)S(1)}, u32[]{:S(2)}, u32[]{:S(2)}) collective-permute-start(bf16[576,128]{1,0:T(8,128)(2,1)S(1)} %get-tuple-element.59), channel_id=1, source_target_pairs={{0,4},{1,5},{2,6},{3,7},{4,0},{5,1},{6,2},{7,3},{8,12},{9,13},{10,... | collective-permute-start | bytes 442376 | tf_op jit(solution)/shard_map/ppermute | solution.py:231
  32.9 2.4 %shard_map.83 = bf16[8,576,128]{2,1,0:T(8,128)(2,1)} custom-call(bf16[1024,1024]{1,0:T(8,128)(2,1)S(1)} %get-tuple-element.48.ds_ref, bf16[576,128]{1,0:T(8,128)(2,1)S(1)} %pad_maximum_fusion.refs_0_, bf16[576,128]{1,0:T(8,128)(2,1)S(1)} %collective-permute-done.3.refs_0_.refs_1_, bf16[576,128]{1,0:T(8,128)(2,1)S(1)} %collective-permute-done.4.refs_1_.refs_2_, ...), custom_call_target="tpu_custom_call" | custom-call | flops 1207959552 | bytes 4194304 | tf_op jit(solution)/shard_map/pallas_call | solution.py:194
  35.9 2.7 %collective-permute-done.13 = bf16[576,128]{1,0:T(8,128)(2,1)S(1)} collective-permute-done((bf16[576,128]{1,0:T(8,128)(2,1)S(1)}, bf16[576,128]{1,0:T(8,128)(2,1)S(1)}, u32[]{:S(2)}, u32[]{:S(2)}) %collective-permute-start.13) | collective-permute-done | bytes 147488 | tf_op jit(solution)/shard_map/ppermute | solution.py:231
  38.7 1.8 %collective-permute-start.15 = (bf16[144,128]{1,0:T(8,128)(2,1)S(1)}, bf16[144,128]{1,0:T(8,128)(2,1)S(1)}, u32[]{:S(2)}, u32[]{:S(2)}) collective-permute-start(bf16[144,128]{1,0:T(8,128)(2,1)S(1)} %get-tuple-element.60), channel_id=1, source_target_pairs={{0,24},{1,25},{2,26},{3,27},{4,28},{5,29},{6,30},{7,31},{8,16},{9,... | collective-permute-start | bytes 110600 | tf_op jit(solution)/shard_map/ppermute | solution.py:231
  40.9 2.3 %collective-permute-start.16 = (bf16[144,128]{1,0:T(8,128)(2,1)S(1)}, bf16[144,128]{1,0:T(8,128)(2,1)S(1)}, u32[]{:S(2)}, u32[]{:S(2)}) collective-permute-start(bf16[144,128]{1,0:T(8,128)(2,1)S(1)} %get-tuple-element.62), channel_id=1, source_target_pairs={{0,8},{1,9},{2,10},{3,11},{4,12},{5,13},{6,14},{7,15},{8,0},{9,1},... | collective-permute-start | bytes 110600 | tf_op jit(solution)/shard_map/ppermute | solution.py:231
  43.2 1.8 %collective-permute-done.15 = bf16[144,128]{1,0:T(8,128)(2,1)S(1)} collective-permute-done((bf16[144,128]{1,0:T(8,128)(2,1)S(1)}, bf16[144,128]{1,0:T(8,128)(2,1)S(1)}, u32[]{:S(2)}, u32[]{:S(2)}) %collective-permute-start.15) | collective-permute-done | bytes 36896 | tf_op jit(solution)/shard_map/ppermute | solution.py:231
  45.0 0.8 %collective-permute-done.17 = bf16[144,128]{1,0:T(8,128)(2,1)S(1)} collective-permute-done((bf16[144,128]{1,0:T(8,128)(2,1)S(1)}, bf16[144,128]{1,0:T(8,128)(2,1)S(1)}, u32[]{:S(2)}, u32[]{:S(2)}) %collective-permute-start.17) | collective-permute-done | bytes 36896 | tf_op jit(solution)/shard_map/ppermute | solution.py:231
  (60 shorter events, 5.4 us)
Async XLA Ops:
  0.6 0.9 %copy-start = (bf16[128,576]{0,1:T(8,128)(2,1)S(1)}, bf16[128,576]{0,1:T(8,128)(2,1)}, u32[]{:S(2)}) copy-start(bf16[128,576]{0,1:T(8,128)(2,1)} %param.7) | copy-start | bytes 442372
  0.6 16.7 %copy-start.4 = (s32[16]{0:T(128)S(1)}, s32[16]{0:T(128)}, u32[]{:S(2)}) copy-start(s32[16]{0:T(128)} %param.10) | copy-start | bytes 196
  0.7 16.9 %copy-start.2 = (bf16[128,8,512]{2,1,0:T(8,128)(2,1)S(1)}, bf16[128,8,512]{2,1,0:T(8,128)(2,1)}, u32[]{:S(2)}) copy-start(bf16[128,8,512]{2,1,0:T(8,128)(2,1)} %param.8) | copy-start | bytes 3145732
  1.9 7.0 %collective-permute-start.2 = (bf16[144,128]{1,0:T(8,128)(2,1)S(1)}, bf16[144,128]{1,0:T(8,128)(2,1)S(1)}, u32[]{:S(2)}, u32[]{:S(2)}) collective-permute-start(bf16[144,128]{1,0:T(8,128)(2,1)S(1)} %shard_map.77), channel_id=1, source_target_pairs={{0,24},{1,25},{2,26},{3,27},{4,28},{5,29},{6,30},{7,31},{8,16},{9,... | collective-permute-start | bytes 110600 | tf_op jit(solution)/shard_map/ppermute | solution.py:231
  6.9 4.9 %collective-permute-start.1 = (bf16[144,128]{1,0:T(8,128)(2,1)S(1)}, bf16[144,128]{1,0:T(8,128)(2,1)S(1)}, u32[]{:S(2)}, u32[]{:S(2)}) collective-permute-start(bf16[144,128]{1,0:T(8,128)(2,1)S(1)} %shard_map.77), channel_id=1, source_target_pairs={{0,16},{1,17},{2,18},{3,19},{4,20},{5,21},{6,22},{7,23},{8,24},{9,... | collective-permute-start | bytes 110600 | tf_op jit(solution)/shard_map/ppermute | solution.py:231
  6.9 4.9 %collective-permute-start = (bf16[144,128]{1,0:T(8,128)(2,1)S(1)}, bf16[144,128]{1,0:T(8,128)(2,1)S(1)}, u32[]{:S(2)}, u32[]{:S(2)}) collective-permute-start(bf16[144,128]{1,0:T(8,128)(2,1)S(1)} %shard_map.77), channel_id=1, source_target_pairs={{0,8},{1,9},{2,10},{3,11},{4,12},{5,13},{6,14},{7,15},{8,0},{9,1},... | collective-permute-start | bytes 110600 | tf_op jit(solution)/shard_map/ppermute | solution.py:231
  11.8 7.1 %copy-start.1 = (bf16[128,8,576]{0,2,1:T(8,128)(2,1)S(1)}, bf16[128,8,576]{0,2,1:T(8,128)(2,1)}, u32[]{:S(2)}) copy-start(bf16[128,8,576]{0,2,1:T(8,128)(2,1)} %param.6) | copy-start | bytes 3538948
  11.8 8.0 %collective-permute-start.5 = (bf16[576,128]{1,0:T(8,128)(2,1)S(1)}, bf16[576,128]{1,0:T(8,128)(2,1)S(1)}, u32[]{:S(2)}, u32[]{:S(2)}) collective-permute-start(bf16[576,128]{1,0:T(8,128)(2,1)S(1)} %pad_maximum_fusion.refs_0_), channel_id=1, source_target_pairs={{0,4},{1,5},{2,6},{3,7},{4,0},{5,1},{6,2},{7,3},{8,12},{9,13},{10,... | collective-permute-start | bytes 442376 | tf_op jit(solution)/shard_map/ppermute | solution.py:231
  13.4 7.9 %collective-permute-start.4 = (bf16[576,128]{1,0:T(8,128)(2,1)S(1)}, bf16[576,128]{1,0:T(8,128)(2,1)S(1)}, u32[]{:S(2)}, u32[]{:S(2)}) collective-permute-start(bf16[576,128]{1,0:T(8,128)(2,1)S(1)} %pad_maximum_fusion.refs_0_), channel_id=1, source_target_pairs={{0,2},{1,3},{2,0},{3,1},{4,6},{5,7},{6,4},{7,5},{8,10},{9,11},{10,... | collective-permute-start | bytes 442376 | tf_op jit(solution)/shard_map/ppermute | solution.py:231
  14.9 6.3 %collective-permute-start.3 = (bf16[576,128]{1,0:T(8,128)(2,1)S(1)}, bf16[576,128]{1,0:T(8,128)(2,1)S(1)}, u32[]{:S(2)}, u32[]{:S(2)}) collective-permute-start(bf16[576,128]{1,0:T(8,128)(2,1)S(1)} %pad_maximum_fusion.refs_0_), channel_id=1, source_target_pairs={{0,6},{1,7},{2,4},{3,5},{4,2},{5,3},{6,0},{7,1},{8,14},{9,15},{10,... | collective-permute-start | bytes 442376 | tf_op jit(solution)/shard_map/ppermute | solution.py:231
  17.3 1.4 %collective-permute-start.6 = (bf16[576,128]{1,0:T(8,128)(2,1)S(1)}, bf16[576,128]{1,0:T(8,128)(2,1)S(1)}, u32[]{:S(2)}, u32[]{:S(2)}) collective-permute-start(bf16[576,128]{1,0:T(8,128)(2,1)S(1)} %pad_maximum_fusion.refs_0_), channel_id=1, source_target_pairs={{0,1},{1,0},{2,3},{3,2},{4,5},{5,4},{6,7},{7,6},{8,9},{9,8},{10,11... | collective-permute-start | bytes 442376 | tf_op jit(solution)/shard_map/ppermute | solution.py:231
  21.2 1.8 %collective-permute-start.7 = (bf16[576,128]{1,0:T(8,128)(2,1)S(1)}, bf16[576,128]{1,0:T(8,128)(2,1)S(1)}, u32[]{:S(2)}, u32[]{:S(2)}) collective-permute-start(bf16[576,128]{1,0:T(8,128)(2,1)S(1)} %collective-permute-done.3.refs_0_.refs_1_), channel_id=1, source_target_pairs={{0,1},{1,0},{2,3},{3,2},{4,5},{5,4},{6,7},{7,6},{8,9},{9,8},{10,11... | collective-permute-start | bytes 442376 | tf_op jit(solution)/shard_map/ppermute | solution.py:231
  21.2 1.8 %collective-permute-start.8 = (bf16[576,128]{1,0:T(8,128)(2,1)S(1)}, bf16[576,128]{1,0:T(8,128)(2,1)S(1)}, u32[]{:S(2)}, u32[]{:S(2)}) collective-permute-start(bf16[576,128]{1,0:T(8,128)(2,1)S(1)} %collective-permute-done.4.refs_1_.refs_2_), channel_id=1, source_target_pairs={{0,1},{1,0},{2,3},{3,2},{4,5},{5,4},{6,7},{7,6},{8,9},{9,8},{10,11... | collective-permute-start | bytes 442376 | tf_op jit(solution)/shard_map/ppermute | solution.py:231
  21.7 1.4 %collective-permute-start.9 = (bf16[576,128]{1,0:T(8,128)(2,1)S(1)}, bf16[576,128]{1,0:T(8,128)(2,1)S(1)}, u32[]{:S(2)}, u32[]{:S(2)}) collective-permute-start(bf16[576,128]{1,0:T(8,128)(2,1)S(1)} %collective-permute-done.5.refs_2_.refs_3_), channel_id=1, source_target_pairs={{0,1},{1,0},{2,3},{3,2},{4,5},{5,4},{6,7},{7,6},{8,9},{9,8},{10,11... | collective-permute-start | bytes 442376 | tf_op jit(solution)/shard_map/ppermute | solution.py:231
  26.0 2.2 %collective-permute-start.10 = (bf16[1152,128]{1,0:T(8,128)(2,1)S(1)}, bf16[1152,128]{1,0:T(8,128)(2,1)S(1)}, u32[]{:S(2)}, u32[]{:S(2)}) collective-permute-start(bf16[1152,128]{1,0:T(8,128)(2,1)S(1)} %get-tuple-element.50), channel_id=1, source_target_pairs={{0,1},{1,0},{2,3},{3,2},{4,5},{5,4},{6,7},{7,6},{8,9},{9,8},{10,11... | collective-permute-start | bytes 884744 | tf_op jit(solution)/shard_map/ppermute | solution.py:231
  28.1 2.4 %collective-permute-start.12 = (bf16[1152,128]{1,0:T(8,128)(2,1)S(1)}, bf16[1152,128]{1,0:T(8,128)(2,1)S(1)}, u32[]{:S(2)}, u32[]{:S(2)}) collective-permute-start(bf16[1152,128]{1,0:T(8,128)(2,1)S(1)} %get-tuple-element.53), channel_id=1, source_target_pairs={{0,1},{1,0},{2,3},{3,2},{4,5},{5,4},{6,7},{7,6},{8,9},{9,8},{10,11... | collective-permute-start | bytes 884744 | tf_op jit(solution)/shard_map/ppermute | solution.py:231
  28.3 7.6 %collective-permute-start.11 = (bf16[576,128]{1,0:T(8,128)(2,1)S(1)}, bf16[576,128]{1,0:T(8,128)(2,1)S(1)}, u32[]{:S(2)}, u32[]{:S(2)}) collective-permute-start(bf16[576,128]{1,0:T(8,128)(2,1)S(1)} %slice.80), channel_id=1, source_target_pairs={{0,6},{1,7},{2,4},{3,5},{4,2},{5,3},{6,0},{7,1},{8,14},{9,15},{10,... | collective-permute-start | bytes 442376 | tf_op jit(solution)/shard_map/ppermute | solution.py:231
  30.5 8.1 %collective-permute-start.13 = (bf16[576,128]{1,0:T(8,128)(2,1)S(1)}, bf16[576,128]{1,0:T(8,128)(2,1)S(1)}, u32[]{:S(2)}, u32[]{:S(2)}) collective-permute-start(bf16[576,128]{1,0:T(8,128)(2,1)S(1)} %get-tuple-element.58), channel_id=1, source_target_pairs={{0,2},{1,3},{2,0},{3,1},{4,6},{5,7},{6,4},{7,5},{8,10},{9,11},{10,... | collective-permute-start | bytes 442376 | tf_op jit(solution)/shard_map/ppermute | solution.py:231
  31.3 7.3 %collective-permute-start.14 = (bf16[576,128]{1,0:T(8,128)(2,1)S(1)}, bf16[576,128]{1,0:T(8,128)(2,1)S(1)}, u32[]{:S(2)}, u32[]{:S(2)}) collective-permute-start(bf16[576,128]{1,0:T(8,128)(2,1)S(1)} %get-tuple-element.59), channel_id=1, source_target_pairs={{0,4},{1,5},{2,6},{3,7},{4,0},{5,1},{6,2},{7,3},{8,12},{9,13},{10,... | collective-permute-start | bytes 442376 | tf_op jit(solution)/shard_map/ppermute | solution.py:231
  38.7 6.2 %collective-permute-start.15 = (bf16[144,128]{1,0:T(8,128)(2,1)S(1)}, bf16[144,128]{1,0:T(8,128)(2,1)S(1)}, u32[]{:S(2)}, u32[]{:S(2)}) collective-permute-start(bf16[144,128]{1,0:T(8,128)(2,1)S(1)} %get-tuple-element.60), channel_id=1, source_target_pairs={{0,24},{1,25},{2,26},{3,27},{4,28},{5,29},{6,30},{7,31},{8,16},{9,... | collective-permute-start | bytes 110600 | tf_op jit(solution)/shard_map/ppermute | solution.py:231
  40.5 5.3 %collective-permute-start.17 = (bf16[144,128]{1,0:T(8,128)(2,1)S(1)}, bf16[144,128]{1,0:T(8,128)(2,1)S(1)}, u32[]{:S(2)}, u32[]{:S(2)}) collective-permute-start(bf16[144,128]{1,0:T(8,128)(2,1)S(1)} %get-tuple-element.61), channel_id=1, source_target_pairs={{0,16},{1,17},{2,18},{3,19},{4,20},{5,21},{6,22},{7,23},{8,24},{9,... | collective-permute-start | bytes 110600 | tf_op jit(solution)/shard_map/ppermute | solution.py:231
  40.9 4.9 %collective-permute-start.16 = (bf16[144,128]{1,0:T(8,128)(2,1)S(1)}, bf16[144,128]{1,0:T(8,128)(2,1)S(1)}, u32[]{:S(2)}, u32[]{:S(2)}) collective-permute-start(bf16[144,128]{1,0:T(8,128)(2,1)S(1)} %get-tuple-element.62), channel_id=1, source_target_pairs={{0,8},{1,9},{2,10},{3,11},{4,12},{5,13},{6,14},{7,15},{8,0},{9,1},... | collective-permute-start | bytes 110600 | tf_op jit(solution)/shard_map/ppermute | solution.py:231
  45.9 0.6 %copy-start.3 = (f32[32,576]{1,0:T(8,128)}, f32[32,576]{1,0:T(8,128)S(1)}, u32[]{:S(2)}) copy-start(f32[32,576]{1,0:T(8,128)S(1)} %maximum_dynamic-update-slice_fusion) | copy-start | bytes 221188

commit v7 on v5

--- a/solution.py
+++ b/solution.py
@@ -258,7 +258,7 @@
     for masks in reversed(phases[2:]):
         own = jnp.concatenate([own] + [exchange(own, m) for m in masks])
     own, out_grad, outputs, span_map = lax.optimization_barrier((own, out_grad, outputs, span_map))
-    near = {m: exchange(own, m) for m in phases[1]}
+    near = {m: exchange(own, m) for m in (phases[1][1], phases[1][0], phases[1][2])}
     near = [near[m] for m in around]
     og = out_grad.transpose(1, 0, 2)
     row_dots = jnp.einsum("ihc,ihc->hi", out_grad, outputs, preferred_element_type=f32)

time: 46.8 us -> 46.8 us (level)
  no operation moved by 1% of the time
where the time goes in v7:
time: 46.8 us; the launch traced here: 46.6 us
  starting transfers between devices  18.5 us (40%)
  waiting for transfers between devices  11.4 us (24%)
  Pallas kernels  10 us (21%)
  other arithmetic  3.09 us (7%)
  local copies, waits for them, and re-layouts  2.65 us (6%)
  between operations  0.97 us (2%)
    ppermute x18, starting transfers between devices, exchange(): lax.ppermute(value, ('ctx', 'head'), [(i, i ^ mask) for i in range(device...  18.5 us
    ppermute x18, waiting for transfers between devices, exchange(): lax.ppermute(value, ('ctx', 'head'), [(i, i ^ mask) for i in range(device...  11.4 us
    pallas_call x7, Pallas kernels, call(): pl.pallas_call(kernel, in_specs=[VMEM] * len(operands), out_specs=[VMEM]...  10 us
    unnamed x1, other arithmetic  1.89 us
    unnamed x15, local copies, waits for them, and re-layouts  1.66 us
  transfers between devices with their start and end apart: 18, of which 8 were waited for; matrix products, arithmetic and copies ran while one was open for 8% of the time, Pallas kernels for 15%

profile of v7, /device:TPU:0, one launch (start us, length us, event | category | flops | bytes accessed | tf_op | source)
XLA Modules:
  0.0 46.6 jit_solution(9779466538483485229)
XLA Ops:
  0.7 0.9 %copy-done = bf16[128,576]{0,1:T(8,128)(2,1)S(1)} copy-done((bf16[128,576]{0,1:T(8,128)(2,1)S(1)}, bf16[128,576]{0,1:T(8,128)(2,1)}, u32[]{:S(2)}) %copy-start) | copy-done | bytes 147480
  1.9 5.1 %collective-permute-start.2 = (bf16[144,128]{1,0:T(8,128)(2,1)S(1)}, bf16[144,128]{1,0:T(8,128)(2,1)S(1)}, u32[]{:S(2)}, u32[]{:S(2)}) collective-permute-start(bf16[144,128]{1,0:T(8,128)(2,1)S(1)} %shard_map.77), channel_id=1, source_target_pairs={{0,24},{1,25},{2,26},{3,27},{4,28},{5,29},{6,30},{7,31},{8,16},{9,... | collective-permute-start | bytes 110600 | tf_op jit(solution)/shard_map/ppermute | solution.py:229
  6.9 0.6 %collective-permute-start = (bf16[144,128]{1,0:T(8,128)(2,1)S(1)}, bf16[144,128]{1,0:T(8,128)(2,1)S(1)}, u32[]{:S(2)}, u32[]{:S(2)}) collective-permute-start(bf16[144,128]{1,0:T(8,128)(2,1)S(1)} %shard_map.77), channel_id=1, source_target_pairs={{0,8},{1,9},{2,10},{3,11},{4,12},{5,13},{6,14},{7,15},{8,0},{9,1},... | collective-permute-start | bytes 110600 | tf_op jit(solution)/shard_map/ppermute | solution.py:229
  7.6 0.7 %xor_multiply_fusion = s32[16]{0:T(128)S(1)} fusion(s32[16]{0:T(128)} %constant.91.clone, s32[]{:T(128)S(6)} %add.144), kind=kLoop, calls=%fused_computation.50 | loop fusion | flops 32 | bytes 132 | tf_op jit(solution)/shard_map/mul | solution.py:266
  8.9 2.9 %collective-permute-done.1 = bf16[144,128]{1,0:T(8,128)(2,1)S(1)} collective-permute-done((bf16[144,128]{1,0:T(8,128)(2,1)S(1)}, bf16[144,128]{1,0:T(8,128)(2,1)S(1)}, u32[]{:S(2)}, u32[]{:S(2)}) %collective-permute-start.1) | collective-permute-done | bytes 36896 | tf_op jit(solution)/shard_map/ppermute | solution.py:229
  11.8 1.6 %collective-permute-start.5 = (bf16[576,128]{1,0:T(8,128)(2,1)S(1)}, bf16[576,128]{1,0:T(8,128)(2,1)S(1)}, u32[]{:S(2)}, u32[]{:S(2)}) collective-permute-start(bf16[576,128]{1,0:T(8,128)(2,1)S(1)} %pad_maximum_fusion.refs_0_), channel_id=1, source_target_pairs={{0,4},{1,5},{2,6},{3,7},{4,0},{5,1},{6,2},{7,3},{8,12},{9,13},{10,... | collective-permute-start | bytes 442376 | tf_op jit(solution)/shard_map/ppermute | solution.py:229
  13.4 1.5 %collective-permute-start.4 = (bf16[576,128]{1,0:T(8,128)(2,1)S(1)}, bf16[576,128]{1,0:T(8,128)(2,1)S(1)}, u32[]{:S(2)}, u32[]{:S(2)}) collective-permute-start(bf16[576,128]{1,0:T(8,128)(2,1)S(1)} %pad_maximum_fusion.refs_0_), channel_id=1, source_target_pairs={{0,2},{1,3},{2,0},{3,1},{4,6},{5,7},{6,4},{7,5},{8,10},{9,11},{10,... | collective-permute-start | bytes 442376 | tf_op jit(solution)/shard_map/ppermute | solution.py:229
  15.4 1.9 %fusion = f32[8,128]{0,1:T(8,128)S(1)} fusion(bf16[128,8,512]{2,1,0:T(8,128)(2,1)} %param.9, bf16[128,8,512]{2,1,0:T(8,128)(2,1)} %param.8), kind=kLoop, calls=%fused_computation.1 | loop fusion | flops 2096128 | bytes 2101248
  18.7 0.9 %shard_map.78 = (f32[256,1024]{1,0:T(8,128)S(1)}, f32[256,1024]{1,0:T(8,128)S(1)}, f32[1,1024]{1,0:T(1,128)S(1)}, f32[1,1024]{1,0:T(1,128)S(1)}) custom-call(bf16[8,576,128]{2,1,0:T(8,128)(2,1)S(1)} %bitcast.17, bf16[8,128,512]{2,1,0:T(8,128)(2,1)S(1)} %bitcast.12, f32[8,1,128]{2,1,0:T(1,128)S(1)} %bitcast.22, s32[256,128]{1,0:T(8,128)S(1)} %broadcast_in_dim.36.kpos_ref, ...), custom_call_target="tpu_custom_call" | custom-call | flops 570425344 | bytes 4194304 | tf_op jit(solution)/shard_map/pallas_call | solution.py:192
  19.6 1.6 %collective-permute-done.4.refs_1_.refs_2_ = bf16[576,128]{1,0:T(8,128)(2,1)S(1)} collective-permute-done((bf16[576,128]{1,0:T(8,128)(2,1)S(1)}, bf16[576,128]{1,0:T(8,128)(2,1)S(1)}, u32[]{:S(2)}, u32[]{:S(2)}) %collective-permute-start.4) | collective-permute-done | bytes 147488 | tf_op jit(solution)/shard_map/ppermute | solution.py:229
  21.8 1.3 %shard_map.79 = (f32[384,1024]{1,0:T(8,128)S(1)}, f32[384,1024]{1,0:T(8,128)S(1)}, f32[1,1024]{1,0:T(1,128)S(1)}, f32[1,1024]{1,0:T(1,128)S(1)}) custom-call(bf16[8,576,128]{2,1,0:T(8,128)(2,1)S(1)} %bitcast.18, bf16[8,128,512]{2,1,0:T(8,128)(2,1)S(1)} %bitcast.13, f32[8,1,128]{2,1,0:T(1,128)S(1)} %bitcast.23, s32[384,128]{1,0:T(8,128)S(1)} %broadcast_in_dim.37.kpos_ref, ...), custom_call_target="tpu_custom_call" | custom-call | flops 855638016 | bytes 4194304 | tf_op jit(solution)/shard_map/pallas_call | solution.py:192
  23.1 2.9 %shard_map.80 = (bf16[1024,1024]{1,0:T(8,128)(2,1)S(1)}, bf16[1024,1024]{1,0:T(8,128)(2,1)S(1)}, bf16[1152,128]{1,0:T(8,128)(2,1)S(1)}) custom-call(bf16[8,576,128]{2,1,0:T(8,128)(2,1)S(1)} %bitcast.19, bf16[8,128,512]{2,1,0:T(8,128)(2,1)S(1)} %bitcast.14, f32[8,1,128]{2,1,0:T(1,128)S(1)} %bitcast.24, s32[384,128]{1,0:T(8,128)S(1)} %broadcast_in_dim.38.kpos_ref, ...), custom_call_target="tpu_custom_call" | custom-call | flops 1711276032 | bytes 4194304 | tf_op jit(solution)/shard_map/pallas_call | solution.py:192
  26.6 1.6 %shard_map.81 = (f32[1152,128]{1,0:T(8,128)S(1)}, bf16[1152,128]{1,0:T(8,128)(2,1)S(1)}) custom-call(bf16[8,576,128]{2,1,0:T(8,128)(2,1)S(1)} %bitcast.20, bf16[8,128,512]{2,1,0:T(8,128)(2,1)S(1)} %bitcast.15, bf16[1024,1024]{1,0:T(8,128)(2,1)S(1)} %get-tuple-element.53.p_ref, bf16[1024,1024]{1,0:T(8,128)(2,1)S(1)} %get-tuple-element.54.ds_ref), custom_call_target="tpu_custom_call" | custom-call | flops 1140850688 | bytes 4194304 | tf_op jit(solution)/shard_map/pallas_call | solution.py:192
  28.3 1.1 %collective-permute-start.11 = (bf16[576,128]{1,0:T(8,128)(2,1)S(1)}, bf16[576,128]{1,0:T(8,128)(2,1)S(1)}, u32[]{:S(2)}, u32[]{:S(2)}) collective-permute-start(bf16[576,128]{1,0:T(8,128)(2,1)S(1)} %slice.96), channel_id=1, source_target_pairs={{0,6},{1,7},{2,4},{3,5},{4,2},{5,3},{6,0},{7,1},{8,14},{9,15},{10,... | collective-permute-start | bytes 442376 | tf_op jit(solution)/shard_map/ppermute | solution.py:229
  29.4 0.9 %shard_map.82 = f32[1152,128]{1,0:T(8,128)S(1)} custom-call(bf16[8,576,128]{2,1,0:T(8,128)(2,1)S(1)} %bitcast.21, bf16[8,128,512]{2,1,0:T(8,128)(2,1)S(1)} %bitcast.16, bf16[1024,1024]{1,0:T(8,128)(2,1)S(1)} %get-tuple-element.53.p_ref, bf16[1024,1024]{1,0:T(8,128)(2,1)S(1)} %get-tuple-element.54.ds_ref, f32[1,1024]{1,0:T(1,128)S(1)} %get-tuple-element.58.refs_5_.after_ref), custom_call_target="tpu_custom_call" | custom-call | flops 570425344 | bytes 4194304 | tf_op jit(solution)/shard_map/pallas_call | solution.py:192
  30.4 0.9 %collective-permute-start.13 = (bf16[576,128]{1,0:T(8,128)(2,1)S(1)}, bf16[576,128]{1,0:T(8,128)(2,1)S(1)}, u32[]{:S(2)}, u32[]{:S(2)}) collective-permute-start(bf16[576,128]{1,0:T(8,128)(2,1)S(1)} %get-tuple-element.64), channel_id=1, source_target_pairs={{0,2},{1,3},{2,0},{3,1},{4,6},{5,7},{6,4},{7,5},{8,10},{9,11},{10,... | collective-permute-start | bytes 442376 | tf_op jit(solution)/shard_map/ppermute | solution.py:229
  31.3 1.6 %collective-permute-start.14 = (bf16[576,128]{1,0:T(8,128)(2,1)S(1)}, bf16[576,128]{1,0:T(8,128)(2,1)S(1)}, u32[]{:S(2)}, u32[]{:S(2)}) collective-permute-start(bf16[576,128]{1,0:T(8,128)(2,1)S(1)} %get-tuple-element.65), channel_id=1, source_target_pairs={{0,4},{1,5},{2,6},{3,7},{4,0},{5,1},{6,2},{7,3},{8,12},{9,13},{10,... | collective-permute-start | bytes 442376 | tf_op jit(solution)/shard_map/ppermute | solution.py:229
  32.9 2.4 %shard_map.83 = bf16[8,576,128]{2,1,0:T(8,128)(2,1)} custom-call(bf16[1024,1024]{1,0:T(8,128)(2,1)S(1)} %get-tuple-element.54.ds_ref, bf16[576,128]{1,0:T(8,128)(2,1)S(1)} %pad_maximum_fusion.refs_0_, bf16[576,128]{1,0:T(8,128)(2,1)S(1)} %collective-permute-done.3.refs_0_.refs_1_, bf16[576,128]{1,0:T(8,128)(2,1)S(1)} %collective-permute-done.4.refs_1_.refs_2_, ...), custom_call_target="tpu_custom_call" | custom-call | flops 1207959552 | bytes 4194304 | tf_op jit(solution)/shard_map/pallas_call | solution.py:192
  36.0 2.7 %collective-permute-done.13 = bf16[576,128]{1,0:T(8,128)(2,1)S(1)} collective-permute-done((bf16[576,128]{1,0:T(8,128)(2,1)S(1)}, bf16[576,128]{1,0:T(8,128)(2,1)S(1)}, u32[]{:S(2)}, u32[]{:S(2)}) %collective-permute-start.13) | collective-permute-done | bytes 147488 | tf_op jit(solution)/shard_map/ppermute | solution.py:229
  38.8 1.8 %collective-permute-start.15 = (bf16[144,128]{1,0:T(8,128)(2,1)S(1)}, bf16[144,128]{1,0:T(8,128)(2,1)S(1)}, u32[]{:S(2)}, u32[]{:S(2)}) collective-permute-start(bf16[144,128]{1,0:T(8,128)(2,1)S(1)} %get-tuple-element.66), channel_id=1, source_target_pairs={{0,24},{1,25},{2,26},{3,27},{4,28},{5,29},{6,30},{7,31},{8,16},{9,... | collective-permute-start | bytes 110600 | tf_op jit(solution)/shard_map/ppermute | solution.py:229
  41.0 2.3 %collective-permute-start.16 = (bf16[144,128]{1,0:T(8,128)(2,1)S(1)}, bf16[144,128]{1,0:T(8,128)(2,1)S(1)}, u32[]{:S(2)}, u32[]{:S(2)}) collective-permute-start(bf16[144,128]{1,0:T(8,128)(2,1)S(1)} %get-tuple-element.68), channel_id=1, source_target_pairs={{0,8},{1,9},{2,10},{3,11},{4,12},{5,13},{6,14},{7,15},{8,0},{9,1},... | collective-permute-start | bytes 110600 | tf_op jit(solution)/shard_map/ppermute | solution.py:229
  43.2 1.8 %collective-permute-done.15 = bf16[144,128]{1,0:T(8,128)(2,1)S(1)} collective-permute-done((bf16[144,128]{1,0:T(8,128)(2,1)S(1)}, bf16[144,128]{1,0:T(8,128)(2,1)S(1)}, u32[]{:S(2)}, u32[]{:S(2)}) %collective-permute-start.15) | collective-permute-done | bytes 36896 | tf_op jit(solution)/shard_map/ppermute | solution.py:229
  45.0 0.8 %collective-permute-done.17 = bf16[144,128]{1,0:T(8,128)(2,1)S(1)} collective-permute-done((bf16[144,128]{1,0:T(8,128)(2,1)S(1)}, bf16[144,128]{1,0:T(8,128)(2,1)S(1)}, u32[]{:S(2)}, u32[]{:S(2)}) %collective-permute-start.17) | collective-permute-done | bytes 36896 | tf_op jit(solution)/shard_map/ppermute | solution.py:229
  46.0 0.6 %copy-done.3 = f32[32,576]{1,0:T(8,128)} copy-done((f32[32,576]{1,0:T(8,128)}, f32[32,576]{1,0:T(8,128)S(1)}, u32[]{:S(2)}) %copy-start.3) | copy-done | bytes 73752
  (66 shorter events, 5.3 us)
Async XLA Ops:
  0.6 0.9 %copy-start = (bf16[128,576]{0,1:T(8,128)(2,1)S(1)}, bf16[128,576]{0,1:T(8,128)(2,1)}, u32[]{:S(2)}) copy-start(bf16[128,576]{0,1:T(8,128)(2,1)} %param.7) | copy-start | bytes 442372
  0.6 16.7 %copy-start.4 = (s32[16]{0:T(128)S(1)}, s32[16]{0:T(128)}, u32[]{:S(2)}) copy-start(s32[16]{0:T(128)} %param.10) | copy-start | bytes 196
  0.7 17.0 %copy-start.2 = (bf16[128,8,512]{2,1,0:T(8,128)(2,1)S(1)}, bf16[128,8,512]{2,1,0:T(8,128)(2,1)}, u32[]{:S(2)}) copy-start(bf16[128,8,512]{2,1,0:T(8,128)(2,1)} %param.8) | copy-start | bytes 3145732
  1.9 7.0 %collective-permute-start.2 = (bf16[144,128]{1,0:T(8,128)(2,1)S(1)}, bf16[144,128]{1,0:T(8,128)(2,1)S(1)}, u32[]{:S(2)}, u32[]{:S(2)}) collective-permute-start(bf16[144,128]{1,0:T(8,128)(2,1)S(1)} %shard_map.77), channel_id=1, source_target_pairs={{0,24},{1,25},{2,26},{3,27},{4,28},{5,29},{6,30},{7,31},{8,16},{9,... | collective-permute-start | bytes 110600 | tf_op jit(solution)/shard_map/ppermute | solution.py:229
  6.9 4.9 %collective-permute-start.1 = (bf16[144,128]{1,0:T(8,128)(2,1)S(1)}, bf16[144,128]{1,0:T(8,128)(2,1)S(1)}, u32[]{:S(2)}, u32[]{:S(2)}) collective-permute-start(bf16[144,128]{1,0:T(8,128)(2,1)S(1)} %shard_map.77), channel_id=1, source_target_pairs={{0,16},{1,17},{2,18},{3,19},{4,20},{5,21},{6,22},{7,23},{8,24},{9,... | collective-permute-start | bytes 110600 | tf_op jit(solution)/shard_map/ppermute | solution.py:229
  6.9 4.9 %collective-permute-start = (bf16[144,128]{1,0:T(8,128)(2,1)S(1)}, bf16[144,128]{1,0:T(8,128)(2,1)S(1)}, u32[]{:S(2)}, u32[]{:S(2)}) collective-permute-start(bf16[144,128]{1,0:T(8,128)(2,1)S(1)} %shard_map.77), channel_id=1, source_target_pairs={{0,8},{1,9},{2,10},{3,11},{4,12},{5,13},{6,14},{7,15},{8,0},{9,1},... | collective-permute-start | bytes 110600 | tf_op jit(solution)/shard_map/ppermute | solution.py:229
  11.8 6.9 %copy-start.1 = (bf16[128,8,576]{0,2,1:T(8,128)(2,1)S(1)}, bf16[128,8,576]{0,2,1:T(8,128)(2,1)}, u32[]{:S(2)}) copy-start(bf16[128,8,576]{0,2,1:T(8,128)(2,1)} %param.6) | copy-start | bytes 3538948
  11.8 7.8 %collective-permute-start.5 = (bf16[576,128]{1,0:T(8,128)(2,1)S(1)}, bf16[576,128]{1,0:T(8,128)(2,1)S(1)}, u32[]{:S(2)}, u32[]{:S(2)}) collective-permute-start(bf16[576,128]{1,0:T(8,128)(2,1)S(1)} %pad_maximum_fusion.refs_0_), channel_id=1, source_target_pairs={{0,4},{1,5},{2,6},{3,7},{4,0},{5,1},{6,2},{7,3},{8,12},{9,13},{10,... | collective-permute-start | bytes 442376 | tf_op jit(solution)/shard_map/ppermute | solution.py:229
  13.4 7.9 %collective-permute-start.4 = (bf16[576,128]{1,0:T(8,128)(2,1)S(1)}, bf16[576,128]{1,0:T(8,128)(2,1)S(1)}, u32[]{:S(2)}, u32[]{:S(2)}) collective-permute-start(bf16[576,128]{1,0:T(8,128)(2,1)S(1)} %pad_maximum_fusion.refs_0_), channel_id=1, source_target_pairs={{0,2},{1,3},{2,0},{3,1},{4,6},{5,7},{6,4},{7,5},{8,10},{9,11},{10,... | collective-permute-start | bytes 442376 | tf_op jit(solution)/shard_map/ppermute | solution.py:229
  14.9 6.3 %collective-permute-start.3 = (bf16[576,128]{1,0:T(8,128)(2,1)S(1)}, bf16[576,128]{1,0:T(8,128)(2,1)S(1)}, u32[]{:S(2)}, u32[]{:S(2)}) collective-permute-start(bf16[576,128]{1,0:T(8,128)(2,1)S(1)} %pad_maximum_fusion.refs_0_), channel_id=1, source_target_pairs={{0,6},{1,7},{2,4},{3,5},{4,2},{5,3},{6,0},{7,1},{8,14},{9,15},{10,... | collective-permute-start | bytes 442376 | tf_op jit(solution)/shard_map/ppermute | solution.py:229
  17.3 1.4 %collective-permute-start.6 = (bf16[576,128]{1,0:T(8,128)(2,1)S(1)}, bf16[576,128]{1,0:T(8,128)(2,1)S(1)}, u32[]{:S(2)}, u32[]{:S(2)}) collective-permute-start(bf16[576,128]{1,0:T(8,128)(2,1)S(1)} %pad_maximum_fusion.refs_0_), channel_id=1, source_target_pairs={{0,1},{1,0},{2,3},{3,2},{4,5},{5,4},{6,7},{7,6},{8,9},{9,8},{10,11... | collective-permute-start | bytes 442376 | tf_op jit(solution)/shard_map/ppermute | solution.py:229
  21.2 1.8 %collective-permute-start.7 = (bf16[576,128]{1,0:T(8,128)(2,1)S(1)}, bf16[576,128]{1,0:T(8,128)(2,1)S(1)}, u32[]{:S(2)}, u32[]{:S(2)}) collective-permute-start(bf16[576,128]{1,0:T(8,128)(2,1)S(1)} %collective-permute-done.3.refs_0_.refs_1_), channel_id=1, source_target_pairs={{0,1},{1,0},{2,3},{3,2},{4,5},{5,4},{6,7},{7,6},{8,9},{9,8},{10,11... | collective-permute-start | bytes 442376 | tf_op jit(solution)/shard_map/ppermute | solution.py:229
  21.2 1.8 %collective-permute-start.8 = (bf16[576,128]{1,0:T(8,128)(2,1)S(1)}, bf16[576,128]{1,0:T(8,128)(2,1)S(1)}, u32[]{:S(2)}, u32[]{:S(2)}) collective-permute-start(bf16[576,128]{1,0:T(8,128)(2,1)S(1)} %collective-permute-done.4.refs_1_.refs_2_), channel_id=1, source_target_pairs={{0,1},{1,0},{2,3},{3,2},{4,5},{5,4},{6,7},{7,6},{8,9},{9,8},{10,11... | collective-permute-start | bytes 442376 | tf_op jit(solution)/shard_map/ppermute | solution.py:229
  21.7 1.4 %collective-permute-start.9 = (bf16[576,128]{1,0:T(8,128)(2,1)S(1)}, bf16[576,128]{1,0:T(8,128)(2,1)S(1)}, u32[]{:S(2)}, u32[]{:S(2)}) collective-permute-start(bf16[576,128]{1,0:T(8,128)(2,1)S(1)} %collective-permute-done.5.refs_2_.refs_3_), channel_id=1, source_target_pairs={{0,1},{1,0},{2,3},{3,2},{4,5},{5,4},{6,7},{7,6},{8,9},{9,8},{10,11... | collective-permute-start | bytes 442376 | tf_op jit(solution)/shard_map/ppermute | solution.py:229
  26.0 2.2 %collective-permute-start.10 = (bf16[1152,128]{1,0:T(8,128)(2,1)S(1)}, bf16[1152,128]{1,0:T(8,128)(2,1)S(1)}, u32[]{:S(2)}, u32[]{:S(2)}) collective-permute-start(bf16[1152,128]{1,0:T(8,128)(2,1)S(1)} %get-tuple-element.56), channel_id=1, source_target_pairs={{0,1},{1,0},{2,3},{3,2},{4,5},{5,4},{6,7},{7,6},{8,9},{9,8},{10,11... | collective-permute-start | bytes 884744 | tf_op jit(solution)/shard_map/ppermute | solution.py:229
  28.1 2.2 %collective-permute-start.12 = (bf16[1152,128]{1,0:T(8,128)(2,1)S(1)}, bf16[1152,128]{1,0:T(8,128)(2,1)S(1)}, u32[]{:S(2)}, u32[]{:S(2)}) collective-permute-start(bf16[1152,128]{1,0:T(8,128)(2,1)S(1)} %get-tuple-element.59), channel_id=1, source_target_pairs={{0,1},{1,0},{2,3},{3,2},{4,5},{5,4},{6,7},{7,6},{8,9},{9,8},{10,11... | collective-permute-start | bytes 884744 | tf_op jit(solution)/shard_map/ppermute | solution.py:229
  28.3 7.7 %collective-permute-start.11 = (bf16[576,128]{1,0:T(8,128)(2,1)S(1)}, bf16[576,128]{1,0:T(8,128)(2,1)S(1)}, u32[]{:S(2)}, u32[]{:S(2)}) collective-permute-start(bf16[576,128]{1,0:T(8,128)(2,1)S(1)} %slice.96), channel_id=1, source_target_pairs={{0,6},{1,7},{2,4},{3,5},{4,2},{5,3},{6,0},{7,1},{8,14},{9,15},{10,... | collective-permute-start | bytes 442376 | tf_op jit(solution)/shard_map/ppermute | solution.py:229
  30.4 8.3 %collective-permute-start.13 = (bf16[576,128]{1,0:T(8,128)(2,1)S(1)}, bf16[576,128]{1,0:T(8,128)(2,1)S(1)}, u32[]{:S(2)}, u32[]{:S(2)}) collective-permute-start(bf16[576,128]{1,0:T(8,128)(2,1)S(1)} %get-tuple-element.64), channel_id=1, source_target_pairs={{0,2},{1,3},{2,0},{3,1},{4,6},{5,7},{6,4},{7,5},{8,10},{9,11},{10,... | collective-permute-start | bytes 442376 | tf_op jit(solution)/shard_map/ppermute | solution.py:229
  31.3 7.4 %collective-permute-start.14 = (bf16[576,128]{1,0:T(8,128)(2,1)S(1)}, bf16[576,128]{1,0:T(8,128)(2,1)S(1)}, u32[]{:S(2)}, u32[]{:S(2)}) collective-permute-start(bf16[576,128]{1,0:T(8,128)(2,1)S(1)} %get-tuple-element.65), channel_id=1, source_target_pairs={{0,4},{1,5},{2,6},{3,7},{4,0},{5,1},{6,2},{7,3},{8,12},{9,13},{10,... | collective-permute-start | bytes 442376 | tf_op jit(solution)/shard_map/ppermute | solution.py:229
  38.8 6.2 %collective-permute-start.15 = (bf16[144,128]{1,0:T(8,128)(2,1)S(1)}, bf16[144,128]{1,0:T(8,128)(2,1)S(1)}, u32[]{:S(2)}, u32[]{:S(2)}) collective-permute-start(bf16[144,128]{1,0:T(8,128)(2,1)S(1)} %get-tuple-element.66), channel_id=1, source_target_pairs={{0,24},{1,25},{2,26},{3,27},{4,28},{5,29},{6,30},{7,31},{8,16},{9,... | collective-permute-start | bytes 110600 | tf_op jit(solution)/shard_map/ppermute | solution.py:229
  40.6 5.3 %collective-permute-start.17 = (bf16[144,128]{1,0:T(8,128)(2,1)S(1)}, bf16[144,128]{1,0:T(8,128)(2,1)S(1)}, u32[]{:S(2)}, u32[]{:S(2)}) collective-permute-start(bf16[144,128]{1,0:T(8,128)(2,1)S(1)} %get-tuple-element.67), channel_id=1, source_target_pairs={{0,16},{1,17},{2,18},{3,19},{4,20},{5,21},{6,22},{7,23},{8,24},{9,... | collective-permute-start | bytes 110600 | tf_op jit(solution)/shard_map/ppermute | solution.py:229
  41.0 4.9 %collective-permute-start.16 = (bf16[144,128]{1,0:T(8,128)(2,1)S(1)}, bf16[144,128]{1,0:T(8,128)(2,1)S(1)}, u32[]{:S(2)}, u32[]{:S(2)}) collective-permute-start(bf16[144,128]{1,0:T(8,128)(2,1)S(1)} %get-tuple-element.68), channel_id=1, source_target_pairs={{0,8},{1,9},{2,10},{3,11},{4,12},{5,13},{6,14},{7,15},{8,0},{9,1},... | collective-permute-start | bytes 110600 | tf_op jit(solution)/shard_map/ppermute | solution.py:229
  46.0 0.6 %copy-start.3 = (f32[32,576]{1,0:T(8,128)}, f32[32,576]{1,0:T(8,128)S(1)}, u32[]{:S(2)}) copy-start(f32[32,576]{1,0:T(8,128)S(1)} %maximum_dynamic-update-slice_fusion) | copy-start | bytes 221188
